TPU v7x, 32 devices: a whole 2x2x4 slice. The times are simulated.
32 devices in a mesh: head: 8 (over z, x), blk: 4 (over y, core).
Axes of the slice: x: 2, y: 2, z: 4, core: 2. Of those that a mesh axis runs over, the one named last changes fastest.
Arguments:
- tokens: bfloat16 [2, 2048, 1024], P(None, ('head', 'blk')), may hold values from -6 to 6
- cotangent: bfloat16 [2, 2048, 1024], P(None, ('head', 'blk')), may hold values from -6 to 6
- w_qkv: bfloat16 [1024, 3072], P(('head', 'blk')), may hold values from -0.1875 to 0.1875
- w_out: bfloat16 [1024, 1024], P(('head', 'blk')), may hold values from -4 to 4
- w_gate: bfloat16 [1024, 4096], P(('head', 'blk')), may hold values from -0.1875 to 0.1875
- w_up: bfloat16 [1024, 4096], P(('head', 'blk')), may hold values from -0.1875 to 0.1875
- w_down: bfloat16 [4096, 1024], P(('head', 'blk')), may hold values from -0.09375 to 0.09375
- norm_attn: bfloat16 [1024], P(('head', 'blk')), may hold values from 0.5 to 1.5
- norm_ffn: bfloat16 [1024], P(('head', 'blk')), may hold values from 0.5 to 1.5
- q_gain: bfloat16 [1024], P(('head', 'blk')), may hold values from 0.5 to 1.5
- k_gain: bfloat16 [1024], P(('head', 'blk')), may hold values from 0.5 to 1.5
- var_bias: float32 [16, 2], replicated, may hold values from -4 to 4
- doc_lengths: int32 [2, 8], replicated, may hold values from 1 to 1024, 2048 in all within a row
- variate: int32 [2, 2048], P(None, ('head', 'blk')), may hold values from 0 to 3
- times: int32 [2, 2048], P(None, ('head', 'blk')), may hold values from 0 to 1023
Outputs:
- out: bfloat16 [2, 2048, 1024], P(None, ('head', 'blk'))
- grad_tokens: bfloat16 [2, 2048, 1024], P(None, ('head', 'blk'))
- grad_w_qkv: float32 [1024, 3072], P(('head', 'blk'))
- grad_w_out: float32 [1024, 1024], P(('head', 'blk'))
- grad_w_gate: float32 [1024, 4096], P(('head', 'blk'))
- grad_w_up: float32 [1024, 4096], P(('head', 'blk'))
- grad_w_down: float32 [4096, 1024], P(('head', 'blk'))
- grad_norm_attn: float32 [1024], P(('head', 'blk'))
- grad_norm_ffn: float32 [1024], P(('head', 'blk'))
- grad_q_gain: float32 [1024], P(('head', 'blk'))
- grad_k_gain: float32 [1024], P(('head', 'blk'))
- grad_var_bias: float32 [16, 2], replicated
Inputs may be any that keep to these rules, and one draw needn't show every extreme that they name: `doc_lengths`: each row holds the lengths of the consecutive documents of one micro-batch and sums to 2048.
All inputs are finite; a program needn't handle non-finite values.
Results may differ from a plain program's by a relative error of at most 0.025.
Values may be sent and summed in bfloat16 or wider, within the bound.
A program may use at most 320 MiB of HBM per device.

v0:
```python
import math

import jax
import jax.numpy as jnp
from jax import lax
from jax.sharding import PartitionSpec as P

EPS = 1e-06
THETA = 10000.0
NEGATIVE = -1e30
KEY_BLOCK = 1024


def inverse_rms(values_in):
    return lax.rsqrt(jnp.mean(values_in * values_in, axis=-1, keepdims=True) + EPS)


def rotate(values_in, time_index, sign_value):
    half_dim = values_in.shape[-1] // 2
    frequency = THETA ** (-2.0 * jnp.arange(half_dim, dtype=jnp.float32) / values_in.shape[-1])
    angles = time_index.astype(jnp.float32)[:, None] * frequency[None, :]
    cosine = jnp.cos(angles)[:, None, :]
    sine_part = sign_value * jnp.sin(angles)[:, None, :]
    first_half = values_in[..., :half_dim]
    second_half = values_in[..., half_dim:]
    return jnp.concatenate(
        [
            first_half * cosine - second_half * sine_part,
            first_half * sine_part + second_half * cosine,
        ],
        axis=-1,
    )


def norm_back(grad_in, value_in, scale_in, gain_in):
    weighted = grad_in * gain_in
    scale_cube = scale_in * scale_in * scale_in
    return scale_in * weighted - value_in * scale_cube * jnp.mean(
        weighted * value_in, axis=-1, keepdims=True
    )


def row_contract(left_mat, right_mat):
    return lax.dot_general(
        left_mat, right_mat, (((0,), (0,)), ((), ())), preferred_element_type=jnp.float32
    )


def col_contract(left_mat, right_mat):
    return lax.dot_general(
        left_mat, right_mat, (((1,), (1,)), ((), ())), preferred_element_type=jnp.float32
    )


def document_of(positions, doc_ends):
    return jnp.sum((positions[:, None] >= doc_ends[None, :]).astype(jnp.int32), axis=1)


def key_positions(first_row, row_total, per_group, row_count, blk_n):
    row_index = first_row + jnp.arange(row_total, dtype=jnp.int32)
    source_blk = row_index // per_group
    within = row_index % per_group
    return (within // row_count * blk_n + source_blk) * row_count + within % row_count


def block_scores(queries, key_part, same_var, same_doc, bias_same, bias_other, att_scale):
    raw_scores = (
        jnp.einsum("qhd,khd->qhk", queries, key_part, preferred_element_type=jnp.float32)
        * att_scale
    )
    bias_terms = jnp.where(
        same_var[:, None, :], bias_same[None, :, None], bias_other[None, :, None]
    )
    return jnp.where(same_doc[:, None, :], raw_scores + bias_terms, NEGATIVE)


def forward_block(
    state_in, queries, key_part, value_part, same_var, same_doc, bias_same, bias_other, att_scale
):
    best_prev, total_prev, accum_prev = state_in
    scores = block_scores(queries, key_part, same_var, same_doc, bias_same, bias_other, att_scale)
    best_next = jnp.maximum(best_prev, jnp.max(scores, axis=-1))
    factor = jnp.exp(best_prev - best_next)
    weights = jnp.where(same_doc[:, None, :], jnp.exp(scores - best_next[..., None]), 0.0)
    total_next = total_prev * factor + jnp.sum(weights, axis=-1)
    accum_next = accum_prev * factor[..., None] + jnp.einsum(
        "qhk,khd->qhd", weights.astype(jnp.bfloat16), value_part, preferred_element_type=jnp.float32
    )
    return (best_next, total_next, accum_next)


def flatten_all(grads_in):
    return tuple((member.reshape(-1) for member in grads_in))


def unflatten_all(flat_in, grads_like):
    return tuple(
        (flat.reshape((-1,) + member.shape[1:]) for flat, member in zip(flat_in, grads_like))
    )


def on_device(
    tokens,
    cotangent,
    w_qkv,
    w_out,
    w_gate,
    w_up,
    w_down,
    norm_attn,
    norm_ffn,
    q_gain,
    k_gain,
    var_bias,
    doc_lengths,
    variate,
    times,
):
    heads_n = lax.axis_size("head")
    blk_n = lax.axis_size("blk")
    head_rank = lax.axis_index("head")
    blk_rank = lax.axis_index("blk")
    batch_count, row_count, model_width = tokens.shape
    head_count = var_bias.shape[0]
    head_dim = model_width // head_count
    local_heads = head_count // heads_n
    query_rows = heads_n * row_count
    key_rows = blk_n * query_rows
    key_block = min(KEY_BLOCK, key_rows)
    block_count = key_rows // key_block
    att_scale = 1.0 / math.sqrt(head_dim)
    gathered = (
        lax.all_gather(w_qkv, ("head", "blk"), axis=0, tiled=True),
        lax.all_gather(w_out, ("head", "blk"), axis=0, tiled=True),
        lax.all_gather(w_gate, ("head", "blk"), axis=0, tiled=True),
        lax.all_gather(w_up, ("head", "blk"), axis=0, tiled=True),
        lax.all_gather(w_down, ("head", "blk"), axis=0, tiled=True),
        lax.all_gather(norm_attn, ("head", "blk"), axis=0, tiled=True),
        lax.all_gather(norm_ffn, ("head", "blk"), axis=0, tiled=True),
        lax.all_gather(q_gain, ("head", "blk"), axis=0, tiled=True),
        lax.all_gather(k_gain, ("head", "blk"), axis=0, tiled=True),
    )
    wqkv_all, wout_all, wgate_all, wup_all, wdown_all = gathered[:5]
    gain_attn = gathered[5].astype(jnp.float32)
    gain_ffn = gathered[6].astype(jnp.float32)
    gain_query = gathered[7].astype(jnp.float32).reshape(head_count, head_dim)
    gain_key = gathered[8].astype(jnp.float32).reshape(head_count, head_dim)
    local_bias = lax.dynamic_slice_in_dim(var_bias, head_rank * local_heads, local_heads, 0)
    bias_same = local_bias[:, 0]
    bias_other = local_bias[:, 1]
    query_index = jnp.arange(query_rows, dtype=jnp.int32)
    query_pos = (query_index // row_count * blk_n + blk_rank) * row_count + query_index % row_count
    ends_all = jnp.cumsum(doc_lengths, axis=1)
    outputs_list = []
    inputs_list = []
    totals = None
    bias_accum = jnp.zeros((local_heads, 2), jnp.float32)
    for batch_id in range(batch_count):
        doc_ends = ends_all[batch_id]
        time_row = times[batch_id]
        inputs_f = tokens[batch_id].astype(jnp.float32)
        scale_one = inverse_rms(inputs_f)
        normed_one = (inputs_f * scale_one * gain_attn).astype(jnp.bfloat16)
        qkv_all = jnp.dot(normed_one, wqkv_all, preferred_element_type=jnp.float32).reshape(
            row_count, head_count, 3 * head_dim
        )
        query_raw = qkv_all[..., :head_dim]
        key_raw = qkv_all[..., head_dim : 2 * head_dim]
        value_raw = qkv_all[..., 2 * head_dim :]
        query_scale = inverse_rms(query_raw)
        key_scale = inverse_rms(key_raw)
        query_rot = rotate(query_raw * query_scale * gain_query, time_row, 1.0)
        key_rot = rotate(key_raw * key_scale * gain_key, time_row, 1.0)
        packed = jnp.concatenate([query_rot, key_rot, value_raw], axis=-1).astype(jnp.bfloat16)
        variate_rep = jnp.broadcast_to(
            variate[batch_id].astype(jnp.bfloat16)[:, None], (row_count, head_count)
        )
        packed_heads, variate_heads = (
            lax.all_to_all(packed, "head", split_axis=1, concat_axis=0, tiled=True),
            lax.all_to_all(variate_rep, "head", split_axis=1, concat_axis=0, tiled=True),
        )
        queries = packed_heads[..., :head_dim]
        key_values = packed_heads[..., head_dim:]
        query_var = variate_heads[:, 0]
        query_doc = document_of(query_pos, doc_ends)
        initial = (
            jnp.full((query_rows, local_heads), NEGATIVE, jnp.float32),
            jnp.zeros((query_rows, local_heads), jnp.float32),
            jnp.zeros((query_rows, local_heads, head_dim), jnp.float32),
        )
        kv_piece = lax.all_gather(key_values, "blk", axis=0, tiled=True)
        var_piece = lax.all_gather(query_var, "blk", axis=0, tiled=True)
        piece_rows = kv_piece.shape[0]

        def one_block(state_blk, kv_block, var_block, block_start):
            key_doc = document_of(
                key_positions(block_start, kv_block.shape[0], query_rows, row_count, blk_n),
                doc_ends,
            )
            same_doc = query_doc[:, None] == key_doc[None, :]
            same_var = query_var[:, None] == var_block[None, :]
            return forward_block(
                state_blk,
                queries,
                kv_block[..., :head_dim],
                kv_block[..., head_dim:],
                same_var,
                same_doc,
                bias_same,
                bias_other,
                att_scale,
            )

        def loop_step(turn_index, state_loop):
            kv_block = lax.dynamic_slice_in_dim(kv_piece, turn_index * key_block, key_block, 0)
            var_block = lax.dynamic_slice_in_dim(var_piece, turn_index * key_block, key_block, 0)
            return one_block(state_loop, kv_block, var_block, turn_index * key_block)

        attn_state = lax.fori_loop(0, piece_rows // key_block, loop_step, initial)
        best_score, total_weight, accum = attn_state
        attn_heads = accum / total_weight[..., None]
        log_total = best_score + jnp.log(total_weight)
        attn_tok = lax.all_to_all(
            attn_heads.astype(jnp.bfloat16), "head", split_axis=0, concat_axis=1, tiled=True
        ).reshape(row_count, model_width)
        resid_one = inputs_f + jnp.dot(attn_tok, wout_all, preferred_element_type=jnp.float32)
        scale_two = inverse_rms(resid_one)
        normed_two = (resid_one * scale_two * gain_ffn).astype(jnp.bfloat16)
        gate_pre = jnp.dot(normed_two, wgate_all, preferred_element_type=jnp.float32)
        up_pre = jnp.dot(normed_two, wup_all, preferred_element_type=jnp.float32)
        sigmoid_gate = jax.nn.sigmoid(gate_pre)
        silu_gate = gate_pre * sigmoid_gate
        hidden_act = (silu_gate * up_pre).astype(jnp.bfloat16)
        result = resid_one + jnp.dot(hidden_act, wdown_all, preferred_element_type=jnp.float32)
        outputs_list.append(result.astype(jnp.bfloat16))
        grad_out = cotangent[batch_id].astype(jnp.float32)
        grad_ffn = grad_out.astype(jnp.bfloat16)
        grad_down = row_contract(hidden_act, grad_ffn)
        grad_hidden = col_contract(grad_ffn, wdown_all)
        grad_gate = (
            grad_hidden * up_pre * sigmoid_gate * (1.0 + gate_pre * (1.0 - sigmoid_gate))
        ).astype(jnp.bfloat16)
        grad_up = (grad_hidden * silu_gate).astype(jnp.bfloat16)
        grad_wgate = row_contract(normed_two, grad_gate)
        grad_wup = row_contract(normed_two, grad_up)
        grad_normed = col_contract(grad_gate, wgate_all) + col_contract(grad_up, wup_all)
        grad_gffn = jnp.sum(grad_normed * resid_one * scale_two, axis=0)
        grad_resid = grad_out + norm_back(grad_normed, resid_one, scale_two, gain_ffn)
        grad_branch = grad_resid.astype(jnp.bfloat16)
        grad_wout = row_contract(attn_tok, grad_branch)
        grad_attn = (
            col_contract(grad_branch, wout_all)
            .astype(jnp.bfloat16)
            .reshape(row_count, head_count, head_dim)
        )
        grad_heads = lax.all_to_all(grad_attn, "head", split_axis=1, concat_axis=0, tiled=True)
        delta_row = jnp.sum(grad_heads.astype(jnp.float32) * attn_heads, axis=-1)
        keys_all, key_var_all = (
            lax.all_gather(key_values, "blk", axis=0, tiled=True),
            lax.all_gather(query_var, "blk", axis=0, tiled=True),
        )
        keys_blocks = keys_all.reshape(block_count, key_block, local_heads, 2 * head_dim)
        var_blocks = key_var_all.reshape(block_count, key_block)
        block_starts = jnp.arange(block_count, dtype=jnp.int32) * key_block

        def back_step(carry_back, block_in):
            grad_query, bias_grad = carry_back
            kv_block, var_block, block_start = block_in
            key_doc = document_of(
                key_positions(block_start, key_block, query_rows, row_count, blk_n), doc_ends
            )
            same_doc = query_doc[:, None] == key_doc[None, :]
            same_var = query_var[:, None] == var_block[None, :]
            key_part = kv_block[..., :head_dim]
            value_part = kv_block[..., head_dim:]
            scores = block_scores(
                queries, key_part, same_var, same_doc, bias_same, bias_other, att_scale
            )
            probs = jnp.where(same_doc[:, None, :], jnp.exp(scores - log_total[..., None]), 0.0)
            grad_probs = jnp.einsum(
                "qhd,khd->qhk", grad_heads, value_part, preferred_element_type=jnp.float32
            )
            grad_scores = (probs * (grad_probs - delta_row[..., None])).astype(jnp.bfloat16)
            grad_scores_f = grad_scores.astype(jnp.float32)
            same_sum = jnp.sum(jnp.where(same_var[:, None, :], grad_scores_f, 0.0), axis=(0, 2))
            other_sum = jnp.sum(jnp.where(same_var[:, None, :], 0.0, grad_scores_f), axis=(0, 2))
            bias_grad = bias_grad + jnp.stack([same_sum, other_sum], axis=-1)
            grad_query = grad_query + att_scale * jnp.einsum(
                "qhk,khd->qhd", grad_scores, key_part, preferred_element_type=jnp.float32
            )
            grad_key = att_scale * jnp.einsum(
                "qhk,qhd->khd", grad_scores, queries, preferred_element_type=jnp.float32
            )
            grad_value = jnp.einsum(
                "qhk,qhd->khd",
                probs.astype(jnp.bfloat16),
                grad_heads,
                preferred_element_type=jnp.float32,
            )
            return ((grad_query, bias_grad), jnp.concatenate([grad_key, grad_value], axis=-1))

        carry_start = (
            jnp.zeros((query_rows, local_heads, head_dim), jnp.float32),
            jnp.zeros((local_heads, 2), jnp.float32),
        )
        (grad_query, bias_part), grad_kv_parts = lax.scan(
            back_step, carry_start, (keys_blocks, var_blocks, block_starts)
        )
        bias_accum = bias_accum + bias_part
        grad_kv_own = lax.psum_scatter(
            grad_kv_parts.reshape(key_rows, local_heads, 2 * head_dim).astype(jnp.bfloat16),
            "blk",
            scatter_dimension=0,
            tiled=True,
        )
        grad_packed = jnp.concatenate([grad_query.astype(jnp.bfloat16), grad_kv_own], axis=-1)
        grad_tok = lax.all_to_all(
            grad_packed, "head", split_axis=0, concat_axis=1, tiled=True
        ).astype(jnp.float32)
        grad_qrot = rotate(grad_tok[..., :head_dim], time_row, -1.0)
        grad_krot = rotate(grad_tok[..., head_dim : 2 * head_dim], time_row, -1.0)
        grad_gquery = jnp.sum(grad_qrot * query_raw * query_scale, axis=0)
        grad_gkey = jnp.sum(grad_krot * key_raw * key_scale, axis=0)
        grad_qraw = norm_back(grad_qrot, query_raw, query_scale, gain_query)
        grad_kraw = norm_back(grad_krot, key_raw, key_scale, gain_key)
        grad_qkv = (
            jnp.concatenate([grad_qraw, grad_kraw, grad_tok[..., 2 * head_dim :]], axis=-1)
            .reshape(row_count, 3 * model_width)
            .astype(jnp.bfloat16)
        )
        grad_wqkv = row_contract(normed_one, grad_qkv)
        grad_normed_one = col_contract(grad_qkv, wqkv_all)
        grad_gattn = jnp.sum(grad_normed_one * inputs_f * scale_one, axis=0)
        grad_in = grad_resid + norm_back(grad_normed_one, inputs_f, scale_one, gain_attn)
        inputs_list.append(grad_in.astype(jnp.bfloat16))
        batch_grads = (
            grad_wqkv,
            grad_wout,
            grad_wgate,
            grad_wup,
            grad_down,
            grad_gattn,
            grad_gffn,
            grad_gquery.reshape(model_width),
            grad_gkey.reshape(model_width),
        )
        if totals is None:
            totals = batch_grads
        else:
            totals = tuple(
                (first_term + second_term for first_term, second_term in zip(totals, batch_grads))
            )
    flat_totals = flatten_all(totals)
    summed_flat = (
        lax.psum_scatter(flat_totals[0], ("head", "blk"), scatter_dimension=0, tiled=True),
        lax.psum_scatter(flat_totals[1], ("head", "blk"), scatter_dimension=0, tiled=True),
        lax.psum_scatter(flat_totals[2], ("head", "blk"), scatter_dimension=0, tiled=True),
        lax.psum_scatter(flat_totals[3], ("head", "blk"), scatter_dimension=0, tiled=True),
        lax.psum_scatter(flat_totals[4], ("head", "blk"), scatter_dimension=0, tiled=True),
        lax.psum_scatter(flat_totals[5], ("head", "blk"), scatter_dimension=0, tiled=True),
        lax.psum_scatter(flat_totals[6], ("head", "blk"), scatter_dimension=0, tiled=True),
        lax.psum_scatter(flat_totals[7], ("head", "blk"), scatter_dimension=0, tiled=True),
        lax.psum_scatter(flat_totals[8], ("head", "blk"), scatter_dimension=0, tiled=True),
    )
    totals = unflatten_all(summed_flat, totals)
    bias_full = lax.dynamic_update_slice_in_dim(
        jnp.zeros((head_count, 2), jnp.float32), bias_accum, head_rank * local_heads, 0
    )
    grad_bias = lax.psum(bias_full, ("head", "blk"))
    return (
        jnp.stack(outputs_list),
        jnp.stack(inputs_list),
        totals[0],
        totals[1],
        totals[2],
        totals[3],
        totals[4],
        totals[5],
        totals[6],
        totals[7],
        totals[8],
        grad_bias,
    )


def solution(mesh):
    return jax.shard_map(
        on_device,
        mesh=mesh,
        in_specs=(
            P(None, ("head", "blk"), None),
            P(None, ("head", "blk"), None),
            P(("head", "blk"), None),
            P(("head", "blk"), None),
            P(("head", "blk"), None),
            P(("head", "blk"), None),
            P(("head", "blk"), None),
            P(("head", "blk")),
            P(("head", "blk")),
            P(("head", "blk")),
            P(("head", "blk")),
            P(),
            P(),
            P(None, ("head", "blk")),
            P(None, ("head", "blk")),
        ),
        out_specs=(
            P(None, ("head", "blk"), None),
            P(None, ("head", "blk"), None),
            P(("head", "blk"), None),
            P(("head", "blk"), None),
            P(("head", "blk"), None),
            P(("head", "blk"), None),
            P(("head", "blk"), None),
            P(("head", "blk")),
            P(("head", "blk")),
            P(("head", "blk")),
            P(("head", "blk")),
            P(),
        ),
        check_vma=False,
    )
```

profile of v0, /device:TPU:0, one launch (start us, length us, event | category | flops | bytes accessed | tf_op | source)
XLA Modules:
  0.0 1725.4 jit_solution(8133778499769775157)
XLA Ops:
  11.3 42.5 %all-reduce.15 = (bf16[1024]{0:T(1024)(128)(2,1)S(1)}, bf16[1024]{0:T(1024)(128)(2,1)S(1)}, bf16[1024]{0:T(1024)(128)(2,1)S(1)}, bf16[1024]{0:T(1024)(128)(2,1)S(1)}) all-reduce(bf16[1024]{0:T(1024)(128)(2,1)S(1)} %dynamic-update-slice, bf16[1024]{0:T(1024)(128)(2,1)S(1)} %dynamic-update-slice.1, ...), channel_id=1, replica_groups=mesh['head'=8,'blk'=4] {'head','blk'}, use_global_device_ids=true, to_apply=%add | all-reduce | flops 4096 | bytes 16384
  57.3 26.0 %all-gather.10.cloned.1.call-done = bf16[1024,3072]{1,0:T(8,128)(2,1)} async-done(((bf16[32,3072]{1,0:T(8,128)(2,1)}), bf16[1024,3072]{1,0:T(8,128)(2,1)}) %all-gather.10.cloned.1.call-update) | async-done | bytes 6291472 | tf_op jit(solution)/shard_map/all_gather | solution.py:133
  83.4 8.7 copy.263
  107.4 18.7 %all_to_all.152 = bf16[64,16,192]{2,0,1:T(8,128)(2,1)S(1)} all-to-all(bf16[64,16,192]{2,0,1:T(8,128)(2,1)S(1)} %concatenate.47), channel_id=1, replica_groups=mesh['head'=8,'blk'=4] {'head'}, dimensions={1} | all-to-all | bytes 786432 | tf_op jit(solution)/shard_map/all_to_all | solution.py:179
  129.6 18.0 %all_to_all.153 = bf16[64,16,192]{2,0,1:T(8,128)(2,1)S(1)} all-to-all(bf16[64,16,192]{2,0,1:T(8,128)(2,1)S(1)} %concatenate.46), channel_id=1, replica_groups=mesh['head'=8,'blk'=4] {'head'}, dimensions={1} | all-to-all | bytes 786432 | tf_op jit(solution)/shard_map/all_to_all | solution.py:179
  178.5 18.1 %while.79 = (s32[]{:T(128)}, f32[512,2]{0,1:T(2,128)S(1)}, f32[512,2]{0,1:T(2,128)S(1)}, f32[512,2,64]{0,2,1:T(8,128)S(1)}, s32[512]{0:T(512)S(1)}, /*index=5*/s...) while((s32[]{:T(128)}, f32[512,2]{0,1:T(2,128)S(1)}, ...), condition=%wide.region_19.20_spmd.clone, body=%wide.region_15.19_spmd.clone.sunk | while | flops 289676288 | bytes 22770020 | solution.py:219
  205.3 16.8 while.78
  224.8 14.5 all-to-all-start.2
  247.5 54.4 %all-gather.18.cloned.1.call-done = bf16[1024,4096]{1,0:T(8,128)(2,1)} async-done(((bf16[32,4096]{1,0:T(8,128)(2,1)}), bf16[1024,4096]{1,0:T(8,128)(2,1)}) %all-gather.18.cloned.1.call-update) | async-done | bytes 8388624 | tf_op jit(solution)/shard_map/all_gather | solution.py:136
  306.8 73.9 %all-gather.16.cloned.1.call-done = bf16[1024,4096]{1,0:T(8,128)(2,1)} async-done(((bf16[32,4096]{1,0:T(8,128)(2,1)}), bf16[1024,4096]{1,0:T(8,128)(2,1)}) %all-gather.16.cloned.1.call-update) | async-done | bytes 8388624 | tf_op jit(solution)/shard_map/all_gather | solution.py:135
  385.7 74.1 %all-gather.20.cloned.1.call-done = bf16[4096,1024]{1,0:T(8,128)(2,1)} async-done(((bf16[128,1024]{1,0:T(8,128)(2,1)}), bf16[4096,1024]{1,0:T(8,128)(2,1)}) %all-gather.20.cloned.1.call-update) | async-done | bytes 8388624 | tf_op jit(solution)/shard_map/all_gather | solution.py:137
  459.8 7.1 multiply_convert_fusion.2
  466.9 8.2 fusion.230
  514.0 13.9 add_bitcast_fusion.1
  559.1 28.2 %while.80 = (s32[]{:T(128)}, f32[512,2,64]{0,2,1:T(8,128)S(1)}, f32[2,2]{0,1:T(2,128)S(1)}, bf16[2,1024,2,128]{3,1,0,2:T(8,128)(2,1)}, bf16[2,1024,2,128]{3,1,0,...) while((s32[]{:T(128)}, f32[512,2,64]{0,2,1:T(8,128)S(1)}, ...), condition=%wide.region_27.28_spmd.clone, body=%wide.region_23.27_spmd.clone.sunk | while | flops 695732224 | bytes 30186872 | solution.py:306
  588.5 29.2 %while.81 = (s32[]{:T(128)}, f32[512,2,64]{0,2,1:T(8,128)S(1)}, f32[2,2]{0,1:T(2,128)}, bf16[2,1024,2,128]{3,1,0,2:T(8,128)(2,1)}, bf16[2,1024,2,128]{3,1,0,2:T(...) while((s32[]{:T(128)}, f32[512,2,64]{0,2,1:T(8,128)S(1)}, ...), condition=%wide.region_38.39_spmd.clone, body=%wide.region_34.38_spmd.clone.sunk | while | flops 695732224 | bytes 30219880 | solution.py:306
  621.3 8.4 add_bitcast_fusion.2
  629.7 14.3 copy.350
  652.7 8.1 fusion.183
  670.5 8.2 add_bitcast_fusion
  678.7 8.1 copy.352
  712.2 12.1 copy.348
  748.4 42.6 %all-reduce.13 = (f32[1024]{0:T(1024)S(1)}, f32[1024]{0:T(1024)S(1)}, f32[1024]{0:T(1024)S(1)}, f32[1024]{0:T(1024)S(1)}, f32[16,2]{0,1:T(2,128)}) all-reduce(f32[1024]{0:T(1024)S(1)} %add.852, f32[1024]{0:T(1024)S(1)} %copy-done.96, f32[1024]{0:T(1024)S(1)} %add.855, ...), channel_id=11, replica_groups=mesh['head'=8,'blk'=4] {'head','blk'}, use_global_device_ids=true, to_apply=%region_50.51.clone | all-reduce | flops 4128 | bytes 33024
  794.3 914.5 %all-reduce.18.cloned.1.call-done = (f32[3145728]{0:T(1024)}, f32[1048576]{0:T(1024)}, f32[4194304]{0:T(1024)}, f32[4194304]{0:T(1024)}, f32[4194304]{0:T(1024)}) async-done(((f32[3145728]{0:T(1024)}, f32[1048576]{0:T(1024)}, f32[4194304]{0:T(1024)}, f32[4194304]{0:T(1024)}, f32[4194304]{0:T(1024)}), (f32[3145728]{0:T(1024)}, f32[1048576]{0:T(1024)}, f32[4194304]{0:T(1024)}, f32[4194304]{0:T(1024)}, ...) | async-done | bytes 67108880
  (597 shorter events, 331.7 us)
Async XLA Ops:
  7.2 148.2 %copy-start = (f32[16,2]{0,1:T(2,128)S(1)}, f32[16,2]{0,1:T(2,128)}, u32[]{:S(2)}) copy-start(f32[16,2]{0,1:T(2,128)} %param.34) | copy-start | bytes 388
  7.2 76.2 %all-gather.10.cloned.1.call-start = ((), (), s32[]{:S(2)}) async-start(), calls=%async_computation.12 | async-start | bytes 6488064 | tf_op jit(solution)/shard_map/all_gather | solution.py:133
  7.9 170.6 %all-gather.22.cloned.1.call-start = ((), (), s32[]{:S(2)}) async-start(), calls=%async_computation.18 | async-start | bytes 1310720 | tf_op jit(solution)/shard_map/all_gather | solution.py:191
  57.3 70.4 %copy-start.52 = (f32[64,32]{1,0:T(8,128)}, f32[64,32]{1,0:T(8,128)S(1)}, u32[]{:S(2)}) copy-start(f32[64,32]{1,0:T(8,128)S(1)} %get-tuple-element.1959) | copy-start | bytes 24580
  126.9 78.3 %all-gather.12.cloned.1.call-start = ((), (), s32[]{:S(2)}) async-start(), calls=%async_computation.13 | async-start | bytes 1310720 | tf_op jit(solution)/shard_map/all_gather | solution.py:191
  148.5 93.3 %all-gather.14.cloned.1.call-start = ((), (), s32[]{:S(2)}) async-start(), calls=%async_computation.14 | async-start | bytes 2162688 | tf_op jit(solution)/shard_map/all_gather | solution.py:134
  149.1 152.8 %all-gather.18.cloned.1.call-start = ((), (), s32[]{:S(2)}) async-start(), calls=%async_computation.16 | async-start | bytes 8650752 | tf_op jit(solution)/shard_map/all_gather | solution.py:136
  149.7 231.1 %all-gather.16.cloned.1.call-start = ((), (), s32[]{:S(2)}) async-start(), calls=%async_computation.15 | async-start | bytes 8650752 | tf_op jit(solution)/shard_map/all_gather | solution.py:135
  150.3 309.5 %all-gather.20.cloned.1.call-start = ((), (), s32[]{:S(2)}) async-start(), calls=%async_computation.17 | async-start | bytes 8650752 | tf_op jit(solution)/shard_map/all_gather | solution.py:137
  151.6 10.0 all-to-all-start.4
  162.2 9.8 all-to-all-start.1
  199.3 25.5 %all-to-all-start.5 = ((bf16[8,2,4096]{2,1,0:T(2,128)(2,1)}), bf16[8,2,4096]{2,1,0:T(2,128)(2,1)S(1)}, u32[]{:S(2)}, u32[]{:S(2)}) async-start(bf16[8,2,4096]{2,1,0:T(2,128)(2,1)} %reshape.1020), calls=%async_computation.5 | async-start | bytes 262144 | tf_op jit(solution)/shard_map/all_to_all | solution.py:223
  224.8 16.3 all-to-all-start.2
  244.0 255.1 %copy-start.18 = (f32[64,1024]{1,0:T(8,128)}, f32[64,1024]{1,0:T(8,128)S(1)}, u32[]{:S(2)}) copy-start(f32[64,1024]{1,0:T(8,128)S(1)} %get-tuple-element.1987) | copy-start | bytes 786436
  246.8 252.3 %copy-start.20 = (f32[64,1024]{1,0:T(8,128)}, f32[64,1024]{1,0:T(8,128)S(1)}, u32[]{:S(2)}) copy-start(f32[64,1024]{1,0:T(8,128)S(1)} %get-tuple-element.1985) | copy-start | bytes 786436
  247.5 219.4 %copy-start.25 = (bf16[64,1024]{1,0:T(8,128)(2,1)}, bf16[64,1024]{1,0:T(8,128)(2,1)S(1)}, u32[]{:S(2)}) copy-start(bf16[64,1024]{1,0:T(8,128)(2,1)S(1)} %multiply_convert_fusion.7) | copy-start | bytes 393220
  306.8 153.0 %copy-start.46 = (bf16[2,64,1024]{2,1,0:T(8,128)(2,1)S(1)}, bf16[2,64,1024]{2,1,0:T(8,128)(2,1)}, u32[]{:S(2)}) copy-start(bf16[2,64,1024]{2,1,0:T(8,128)(2,1)} %param.24) | copy-start | bytes 786436
  506.2 24.5 %all-to-all-start.8 = ((bf16[8,2,4096]{2,1,0:T(2,128)(2,1)}), bf16[8,2,4096]{2,1,0:T(2,128)(2,1)}, u32[]{:S(2)}, u32[]{:S(2)}) async-start(bf16[8,2,4096]{2,1,0:T(2,128)(2,1)} %reshape.1024), calls=%async_computation.9 | async-start | bytes 262144 | tf_op jit(solution)/shard_map/all_to_all | solution.py:256
  530.7 25.2 %all-to-all-start.6 = ((bf16[8,2,4096]{2,1,0:T(2,128)(2,1)}), bf16[8,2,4096]{2,1,0:T(2,128)(2,1)S(1)}, u32[]{:S(2)}, u32[]{:S(2)}) async-start(bf16[8,2,4096]{2,1,0:T(2,128)(2,1)} %reshape.1026), calls=%async_computation.6 | async-start | bytes 262144 | tf_op jit(solution)/shard_map/all_to_all | solution.py:256
  536.7 107.6 %reduce-scatter.3.cloned.1.call-start = ((), (), s32[]{:S(2)}) async-start(), calls=%async_computation.19 | async-start | bytes 1310720 | tf_op jit(solution)/shard_map/reduce_scatter | solution.py:310
  587.3 73.7 %reduce-scatter.5.cloned.1.call-start = ((), (), s32[]{:S(2)}) async-start(), calls=%async_computation.20 | async-start | bytes 1310720 | tf_op jit(solution)/shard_map/reduce_scatter | solution.py:310
  646.8 20.1 %all-to-all-start.7 = ((bf16[512,2,192]{2,1,0:T(2,128)(2,1)}), bf16[512,2,192]{2,1,0:T(2,128)(2,1)S(1)}, u32[]{:S(2)}, u32[]{:S(2)}) async-start(bf16[512,2,192]{2,1,0:T(2,128)(2,1)} %copy.286), calls=%async_computation.8 | async-start | bytes 1048576 | tf_op jit(solution)/shard_map/all_to_all | solution.py:317
  666.8 20.3 %all-to-all-start.9 = ((bf16[512,2,192]{2,1,0:T(2,128)(2,1)}), bf16[512,2,192]{2,1,0:T(2,128)(2,1)S(1)}, u32[]{:S(2)}, u32[]{:S(2)}) async-start(bf16[512,2,192]{2,1,0:T(2,128)(2,1)} %copy.298), calls=%async_computation.11 | async-start | bytes 1048576 | tf_op jit(solution)/shard_map/all_to_all | solution.py:317
  670.5 1038.3 %all-reduce.18.cloned.1.call-start = ((), (), s32[]{:S(2)}) async-start(), calls=%async_computation.21 | async-start | bytes 134217728
  (118 other events, 1365.7 us)
Sparse Core Ops, SparseCore 0:
  10.9 72.3 all-gather.9
  127.1 14.8 all-gather.21
  148.6 14.8 all-gather.11
  166.2 56.3 all-gather.13
  225.4 76.4 all-gather.17
  304.6 76.1 all-gather.15
  383.6 76.1 all-gather.19
  587.4 26.0 reduce-scatter.2
  617.9 26.0 reduce-scatter.4
  724.4 984.3 all-reduce.17
where the time goes:
time: 1740 us; the launch traced here: 1730 us
  waiting for transfers between devices  1150 us (66%)
  matrix products  196 us (11%)
  blocking collectives  132 us (8%)
  local copies, waits for them, and re-layouts  122 us (7%)
  other arithmetic  55.2 us (3%)
  starting transfers between devices  47.5 us (3%)
    unnamed x11, waiting for transfers between devices  918 us
    unnamed x2, blocking collectives  85.1 us
    all_gather x1, waiting for transfers between devices, on_device(): lax.all_gather(w_down, ('head', 'blk'), axis=0, tiled=True)  74.1 us
    all_gather x1, waiting for transfers between devices, on_device(): lax.all_gather(w_gate, ('head', 'blk'), axis=0, tiled=True)  73.9 us
    unnamed x252, local copies, waits for them, and re-layouts  67.8 us
    dot_general x10, matrix products, row_contract(): lax.dot_general(left_mat, right_mat, (((0,), (0,)), ((), ())), preferred_...  64.5 us
    all_gather x1, waiting for transfers between devices, on_device(): lax.all_gather(w_up, ('head', 'blk'), axis=0, tiled=True)  54.4 us
    dot_general x10, matrix products, col_contract(): lax.dot_general(left_mat, right_mat, (((1,), (1,)), ((), ())), preferred_...  38.1 us
  transfers between devices with their start and end apart: 18, of which 7 were waited for; matrix products, arithmetic and copies ran while one was open for 13% of the time, Pallas kernels for 0%

commit v1 on v0

--- a/solution.py
+++ b/solution.py
@@ -2,7 +2,10 @@
 
 import jax
 import jax.numpy as jnp
+import numpy as np
 from jax import lax
+from jax.experimental import pallas as pl
+from jax.experimental.pallas import tpu as pltpu
 from jax.sharding import PartitionSpec as P
 
 EPS = 1e-06
@@ -383,40 +386,1161 @@
     )
 
 
+AXES = ("zh", "zl", "x", "y", "c")
+VMEM_BYTES = 58 * 2**20
+
+
+class Net:
+    def __init__(self, send_sems, recv_sems, local_sems):
+        self.me = {name: lax.axis_index(name) for name in AXES}
+        self.send_sems, self.recv_sems, self.local_sems = send_sems, recv_sems, local_sems
+        self.used = 0
+        self.local_used = 0
+        self.copies = []
+        self.locals = []
+
+    def target(self, flips):
+        return tuple(1 - self.me[a] if a in flips else self.me[a] for a in AXES)
+
+    def index(self, names, flips=()):
+        total = 0
+        for a in names:
+            total = total * 2 + (1 - self.me[a] if a in flips else self.me[a])
+        return total
+
+    def barrier(self, partners):
+        sem = pltpu.get_barrier_semaphore()
+        for flips in partners:
+            pl.semaphore_signal(
+                sem, inc=1, device_id=self.target(flips), device_id_type=pl.DeviceIdType.MESH
+            )
+        pl.semaphore_wait(sem, len(partners))
+
+    def send(self, source, dest, flips):
+        copy = pltpu.make_async_remote_copy(
+            src_ref=source,
+            dst_ref=dest,
+            send_sem=self.send_sems.at[self.used],
+            recv_sem=self.recv_sems.at[self.used],
+            device_id=self.target(flips),
+            device_id_type=pl.DeviceIdType.MESH,
+        )
+        self.used += 1
+        copy.start()
+        self.copies.append(copy)
+        return copy
+
+    def local(self, source, dest):
+        copy = pltpu.make_async_copy(source, dest, self.local_sems.at[self.local_used])
+        self.local_used += 1
+        copy.start()
+        return copy
+
+    def finish(self):
+        for copy in self.copies:
+            copy.wait_send()
+
+
+CHIP_FLIPS = [
+    tuple(a for a, bit in zip(("zl", "x", "y"), ((m >> 2) & 1, (m >> 1) & 1, m & 1)) if bit)
+    for m in range(1, 8)
+]
+
+
+class Tree:
+    def __init__(self, net, region, dims):
+        self.net, self.region, self.dims = net, region, dims
+        self.arrive = {}
+        self.sibling = []
+
+    def push(self, flips, source=None):
+        net = self.net
+        source = self.region(flips) if source is None else source
+        level = max([self.dims.index(a) for a in flips], default=-1)
+        for d in self.dims[level + 1 :]:
+            copy = net.send(source, self.region(flips), (d,))
+            self.arrive[tuple(sorted(flips + (d,)))] = copy
+        self.sibling.append(net.send(source, self.region(flips), ("c",)))
+
+    def take(self, flips):
+        self.arrive[tuple(sorted(flips))].wait_recv()
+        self.push(flips)
+
+    def order(self):
+        masks = []
+        for m in range(1, 2 ** len(self.dims)):
+            masks.append(tuple(d for i, d in enumerate(self.dims) if (m >> i) & 1))
+        return masks
+
+    def end(self):
+        for copy in self.sibling:
+            copy.wait_recv()
+
+
+def gather_kernel(
+    tok, cot, wqkv, wout, wgate, wup, wdown, small,
+    x_out, wh_out, wgu_out, wd_out, wo_out, gf_out, sm_out,
+    wp, wl, gp, gl, send_sems, recv_sems, local_sems,
+):
+    net = Net(send_sems, recv_sems, local_sems)
+    me = net.me
+    zh, zl, x, y, c = (me[a] for a in AXES)
+    net.barrier(CHIP_FLIPS + [("c",), ("zh",)])
+    locals_ = []
+
+    def x_region(part):
+        def region(flips):
+            z_part = zh if part == 0 else 1 - zh
+            return x_out.at[z_part * 16 + net.index(AXES[1:], flips)]
+
+        return region
+
+    def wo_region(flips):
+        return wo_out.at[:, net.index(AXES[1:], flips)]
+
+    def gf_region(flips):
+        return gf_out.at[net.index(("zl", "x", "c"), flips)]
+
+    mine = net.index(AXES)
+    x_own = Tree(net, x_region(0), ("y", "zl", "x"))
+    x_far = Tree(net, x_region(1), ("y", "zl", "x"))
+    wo_tree = Tree(net, wo_region, ("y", "zl", "x"))
+    gf_tree = Tree(net, gf_region, ("zl", "x"))
+    swap = net.send(tok.at[1 - zh], x_out.at[mine], ("zh",))
+    x_own.push((), tok.at[zh])
+    sm_zh = net.send(small, sm_out.at[zh, zl, x, y, c], ("zh",))
+    wo_zh = net.send(wout, wo_out.at[zh, net.index(AXES[1:])], ("zh",))
+    wd_zh = net.send(wdown, wd_out.at[zh, y], ("zh",))
+    for zz in range(2):
+        for xx in range(2):
+            for cc in range(2):
+                for zhh in range(2):
+                    for yy in range(2):
+                        col = 128 * (zhh * 16 + zz * 8 + xx * 4 + yy * 2 + cc)
+                        lane = 128 * (zhh * 2 + yy)
+                        gp[zz * 2 + xx, 0, cc, :, lane : lane + 128] = wgate[:, col : col + 128]
+                        gp[zz * 2 + xx, 1, cc, :, lane : lane + 128] = wup[:, col : col + 128]
+    my_pair = net.index(("zl", "x"))
+    g_arrive = []
+    for flips in (("x",), ("zl",), ("zl", "x")):
+        g_arrive.append(net.send(gp.at[net.index(("zl", "x"), flips)], gl.at[my_pair], flips))
+    g_own = net.local(gp.at[my_pair], gl.at[my_pair])
+    heads = 16
+    for h in range(heads):
+        wp[h // 2, h % 2] = wqkv[:, 192 * h : 192 * (h + 1)]
+    w_arrive = []
+    my_chip = net.index(("zl", "x", "y"))
+    for flips in CHIP_FLIPS:
+        w_arrive.append(net.send(wp.at[net.index(("zl", "x", "y"), flips)], wl.at[my_chip], flips))
+    w_own = net.local(wp.at[my_chip], wl.at[my_chip])
+    wd_y = net.send(wdown, wd_out.at[zh, y], ("y",))
+    locals_.append(net.local(tok.at[zh], x_out.at[mine]))
+    sm_own = net.local(small, sm_out.at[zh, zl, x, y, c])
+    wo_own = net.local(wout, wo_out.at[zh, net.index(AXES[1:])])
+    locals_.append(net.local(wdown, wd_out.at[zh, y]))
+    locals_.append(net.local(cot, gf_region(())))
+    x_own.take(("y",))
+    x_own.take(("zl",))
+    g_own.wait()
+    for copy in g_arrive:
+        copy.wait_recv()
+    g_c, g_keep = [], []
+    for k in range(2):
+        place = wgu_out.at[k, zh, :, y, c]
+        g_c.append(net.send(gl.at[:, k, 1 - c], place, ("c",)))
+        g_keep.append(net.local(gl.at[:, k, c], place))
+    w_own.wait()
+    for copy in w_arrive:
+        copy.wait_recv()
+    w_c = net.send(wl.at[:, 1 - c], wh_out.at[zh, :, c], ("c",))
+    w_keep = net.local(wl.at[:, c], wh_out.at[zh, :, c])
+    swap.wait_recv()
+    x_far.push(())
+    g_zh, g_y = [], []
+
+    def g_piece(k, half):
+        return wgu_out.at[k // 2, half, pl.ds(2 * (k % 2), 2), y]
+
+    for k in range(4):
+        if k % 2 == 0:
+            g_keep[k // 2].wait()
+            g_c[k // 2].wait_recv()
+        g_zh.append(net.send(g_piece(k, zh), g_piece(k, zh), ("zh",)))
+        g_y.append(net.send(g_piece(k, zh), g_piece(k, zh), ("y",)))
+    w_keep.wait()
+    w_c.wait_recv()
+    w_zh = net.send(wh_out.at[zh], wh_out.at[zh], ("zh",))
+    x_own.take(("y", "zl"))
+    x_far.take(("y",))
+    x_far.take(("zl",))
+    x_far.take(("y", "zl"))
+    sm_own.wait()
+    sm_zh.wait_recv()
+    sm_c = net.send(sm_out.at[:, zl, x, y, c], sm_out.at[:, zl, x, y, c], ("c",))
+    gf_tree.push((), cot)
+    wo_own.wait()
+    wo_zh.wait_recv()
+    wo_tree.push(())
+    x_own.take(("x",))
+    x_own.take(("y", "x"))
+    sm_c.wait_recv()
+    sm_y = net.send(sm_out.at[:, zl, x, y], sm_out.at[:, zl, x, y], ("y",))
+    gf_tree.take(("zl",))
+    wd_zh.wait_recv()
+    wd_fwd = net.send(wd_out.at[1 - zh, y], wd_out.at[1 - zh, y], ("y",))
+    wo_tree.take(("y",))
+    x_own.take(("zl", "x"))
+    x_own.take(("y", "zl", "x"))
+    sm_y.wait_recv()
+    sm_zl = net.send(sm_out.at[:, zl, x], sm_out.at[:, zl, x], ("zl",))
+    wo_tree.take(("zl",))
+    wo_tree.take(("y", "zl"))
+    g_fwd = []
+
+    def g_pass(k):
+        g_zh[k].wait_recv()
+        g_fwd.append(net.send(g_piece(k, 1 - zh), g_piece(k, 1 - zh), ("y",)))
+
+    g_pass(0)
+    x_far.take(("x",))
+    x_far.take(("y", "x"))
+    sm_zl.wait_recv()
+    sm_x = net.send(sm_out.at[:, :, x], sm_out.at[:, :, x], ("x",))
+    g_pass(1)
+    x_far.take(("zl", "x"))
+    x_far.take(("y", "zl", "x"))
+    gf_tree.take(("x",))
+    gf_tree.take(("zl", "x"))
+    g_pass(2)
+    for flips in (("x",), ("y", "x"), ("zl", "x"), ("y", "zl", "x")):
+        wo_tree.take(flips)
+    g_pass(3)
+    for copy in [sm_x, w_zh, wd_y, wd_fwd] + g_y + g_fwd:
+        copy.wait_recv()
+    for tree in (x_own, x_far, wo_tree, gf_tree):
+        tree.end()
+    for copy in locals_:
+        copy.wait()
+    net.finish()
+
+
+def gather_all(tok, cot, wqkv, wout, wgate, wup, wdown, small):
+    bf = jnp.bfloat16
+    any_spec = pl.BlockSpec(memory_space=pl.ANY)
+    vm = pl.BlockSpec(memory_space=pltpu.VMEM)
+    shapes = [
+        jax.ShapeDtypeStruct((32, 64, 1024), bf),
+        jax.ShapeDtypeStruct((2, 8, 2, 32, 192), bf),
+        jax.ShapeDtypeStruct((2, 2, 4, 2, 2, 32, 512), bf),
+        jax.ShapeDtypeStruct((2, 2, 128, 1024), bf),
+        jax.ShapeDtypeStruct((2, 16, 32, 1024), bf),
+        jax.ShapeDtypeStruct((8, 128, 1024), bf),
+        jax.ShapeDtypeStruct((2, 2, 2, 2, 2, 8, 128), jnp.float32),
+    ]
+    return pl.pallas_call(
+        gather_kernel,
+        out_shape=shapes,
+        in_specs=[any_spec, any_spec, vm, any_spec, vm, vm, any_spec, any_spec],
+        out_specs=[any_spec] * 7,
+        scratch_shapes=[
+            pltpu.VMEM((8, 2, 32, 192), bf),
+            pltpu.VMEM((8, 2, 32, 192), bf),
+            pltpu.VMEM((4, 2, 2, 32, 512), bf),
+            pltpu.VMEM((4, 2, 2, 32, 512), bf),
+            pltpu.SemaphoreType.DMA((104,)),
+            pltpu.SemaphoreType.DMA((104,)),
+            pltpu.SemaphoreType.DMA((16,)),
+        ],
+        compiler_params=pltpu.CompilerParams(
+            collective_id=1, has_side_effects=True, vmem_limit_bytes=VMEM_BYTES
+        ),
+        name="gather_all",
+    )(tok, cot, wqkv, wout, wgate, wup, wdown, small)
+
+
+HEAD_ROWS = 256
+KEY_CHUNK = 512
+
+
+def lane_iota(rows, lanes=128):
+    return lax.broadcasted_iota(jnp.int32, (rows, lanes), 1)
+
+
+def pieces(value):
+    first = value.astype(jnp.bfloat16).astype(jnp.float32)
+    second = (value - first).astype(jnp.bfloat16).astype(jnp.float32)
+    return first, second, value - first - second
+
+
+def swap_halves(values):
+    lane = lane_iota(values.shape[0])
+    return jnp.where(lane % 64 < 32, pltpu.roll(values, 96, 1), pltpu.roll(values, 32, 1))
+
+
+def pair_mean(values):
+    lane = lane_iota(values.shape[0])
+    low = jnp.sum(jnp.where(lane < 64, values, 0.0), axis=1, keepdims=True)
+    high = jnp.sum(jnp.where(lane < 64, 0.0, values), axis=1, keepdims=True)
+    return jnp.where(lane < 64, low, high) * (1.0 / 64.0)
+
+
+def angles_of(packed):
+    lane = lane_iota(packed.shape[0])
+    turned = pltpu.roll(packed, 64, 1)
+    return jnp.where(lane < 64, packed, turned), jnp.where(lane < 64, turned, packed)
+
+
+def doc_bounds(lengths, batch):
+    starts, ends, total = [], [], jnp.int32(0)
+    for j in range(lengths.shape[1]):
+        starts.append(total)
+        total = total + lengths[batch, j]
+        ends.append(total)
+    return starts, ends
+
+
+def key_range(starts, ends, first, last):
+    low, high = jnp.int32(0), ends[-1]
+    for s in starts:
+        low = jnp.where(s <= first, s, low)
+    for e in reversed(ends):
+        high = jnp.where(e > last, e, high)
+    return low, high
+
+
+def attend_kernel(
+    lengths, bias, x_ref, wh_ref, rows_ref, gain_ref, qk_gain_ref, freq_ref,
+    att_out, o_out, qf_out, kf_out, vf_out, raw_out, cs_out, feat,
+):
+    tokens_n = x_ref.shape[0]
+    batch = lax.axis_index("zh")
+    head = ((lax.axis_index("zl") * 2 + lax.axis_index("x")) * 2 + lax.axis_index("y")) * 2
+    head = head + lax.axis_index("c")
+    starts, ends = doc_bounds(lengths, batch)
+    step = 128
+
+    sub = lax.broadcasted_iota(jnp.int32, (8, step), 0)
+    start_col = jnp.zeros((8, step), jnp.int32)
+    end_col = jnp.zeros((8, step), jnp.int32)
+    for j in range(8):
+        start_col = jnp.where(sub == j, starts[j], start_col)
+        end_col = jnp.where(sub == j, ends[j], end_col)
+    same_bias = jnp.full((8, step), bias[head, 0], jnp.float32)
+    other_bias = jnp.full((8, step), bias[head, 1], jnp.float32)
+    other_parts = pieces(other_bias)
+    diff_parts = pieces(same_bias - other_bias)
+    zero = jnp.zeros((8, step), jnp.float32)
+    const_q = jnp.where(sub == 0, -256.0, 0.0)
+    for i, part in enumerate(other_parts):
+        const_q = jnp.where(sub == i + 1, part, const_q)
+    const_k = jnp.where(sub < 4, 1.0, 0.0)
+    ones_k = jnp.where(sub < 3, 1.0, 0.0)
+
+    @pl.loop(0, tokens_n // step)
+    def _(i):
+        col = pl.ds(pl.multiple_of(i * step, step), step)
+        pos = lax.broadcasted_iota(jnp.int32, (8, step), 1) + i * step
+        doc = jnp.where((pos >= start_col) & (pos < end_col), 1.0, 0.0)
+        var_row = jnp.broadcast_to(rows_ref[0:1, col], (8, step))
+        var = jnp.where(var_row == sub.astype(jnp.float32), 1.0, 0.0)
+        rows = [doc * 256.0, const_q] + [var * part for part in diff_parts] + [zero, zero, zero]
+        rows += [doc, const_k, var, var, var, ones_k, zero, zero]
+        feat[col, :] = jnp.concatenate(rows, axis=0).T
+        angle = jnp.broadcast_to(rows_ref[1:2, col], (32, step)) * freq_ref[...]
+        cosine, sine = jnp.cos(angle), jnp.sin(angle)
+        cs_out[col, :] = jnp.concatenate([cosine, cosine, -sine, sine], axis=0).T
+
+    rows_n = HEAD_ROWS
+
+    @pl.loop(0, tokens_n // rows_n)
+    def _(i):
+        row = pl.ds(pl.multiple_of(i * rows_n, rows_n), rows_n)
+        value = x_ref[row, :].astype(jnp.float32)
+        scale = lax.rsqrt(jnp.mean(value * value, axis=1, keepdims=True) + EPS)
+        normed = (value * scale * gain_ref[...]).astype(jnp.bfloat16)
+        qkv = jnp.dot(normed, wh_ref[...], preferred_element_type=jnp.float32)
+        raw = qkv[:, :128]
+        raw_out[row, :] = raw
+        scaled = raw * lax.rsqrt(pair_mean(raw * raw) + EPS) * qk_gain_ref[...]
+        cosine, sine = angles_of(cs_out[row, :])
+        turned = (scaled * cosine + swap_halves(scaled) * sine).astype(jnp.bfloat16)
+        turned = turned.astype(jnp.float32)
+        lane = lane_iota(rows_n)
+        marks = feat[row, :]
+        qf_out[row, :] = jnp.where(
+            lane < 64, turned * 0.125, pltpu.roll(marks, 64, 1)
+        ).astype(jnp.bfloat16)
+        kf_out[row, :] = jnp.where(lane < 64, pltpu.roll(turned, 64, 1), marks).astype(jnp.bfloat16)
+        third = jnp.concatenate([qkv[:, 128:192], jnp.zeros((rows_n, 64), jnp.float32)], axis=1)
+        vf_out[row, :] = jnp.where((lane >= 64) & (lane < 67), 1.0, third).astype(jnp.bfloat16)
+
+    for i in range(tokens_n // rows_n):
+        row = pl.ds(i * rows_n, rows_n)
+        low, high = key_range(starts, ends, i * rows_n, (i + 1) * rows_n - 1)
+        query = qf_out[row, :]
+
+        def one_chunk(k, total):
+            col = pl.ds(pl.multiple_of(k * KEY_CHUNK, KEY_CHUNK), KEY_CHUNK)
+            scores = lax.dot_general(
+                query, kf_out[col, :], (((1,), (1,)), ((), ())), preferred_element_type=jnp.float32
+            )
+            weights = jnp.exp(scores).astype(jnp.bfloat16)
+            return total + jnp.dot(weights, vf_out[col, :], preferred_element_type=jnp.float32)
+
+        total = lax.fori_loop(
+            low // KEY_CHUNK,
+            (high + KEY_CHUNK - 1) // KEY_CHUNK,
+            one_chunk,
+            jnp.zeros((rows_n, 128), jnp.float32),
+        )
+        weight = total[:, 64:65]
+        result = total / weight
+        lane = lane_iota(rows_n)
+        o_out[row, :] = jnp.where(lane < 64, result, jnp.log(weight))
+        att_out[row, :] = result[:, :64].astype(jnp.bfloat16)
+
+
+def attend(lengths, bias, x_all, wh, rows, gain, qk_gain, freq):
+    bf, f32 = jnp.bfloat16, jnp.float32
+    n = x_all.shape[0]
+    sm = pl.BlockSpec(memory_space=pltpu.SMEM)
+    vm = pl.BlockSpec(memory_space=pltpu.VMEM)
+    return pl.pallas_call(
+        attend_kernel,
+        out_shape=[
+            jax.ShapeDtypeStruct((n, 64), bf),
+            jax.ShapeDtypeStruct((n, 128), f32),
+            jax.ShapeDtypeStruct((n, 128), bf),
+            jax.ShapeDtypeStruct((n, 128), bf),
+            jax.ShapeDtypeStruct((n, 128), bf),
+            jax.ShapeDtypeStruct((n, 128), f32),
+            jax.ShapeDtypeStruct((n, 128), f32),
+        ],
+        in_specs=[sm, sm] + [vm] * 6,
+        out_specs=[vm] * 7,
+        scratch_shapes=[pltpu.VMEM((n, 128), f32)],
+        compiler_params=pltpu.CompilerParams(vmem_limit_bytes=VMEM_BYTES),
+        name="attend",
+    )(lengths, bias, x_all, wh, rows, gain, qk_gain, freq)
+
+
+def attend_back_kernel(
+    lengths, x_ref, wh_ref, g_ref, o_ref, qf_ref, kf_ref, vf_ref, raw_ref, cs_ref, gain_ref,
+    qk_gain_ref, gn_out, gw_out, small_out, qb, gb, gk, gv, gqkv, normed_s, bias_s, gain_s,
+):
+    tokens_n = x_ref.shape[0]
+    batch = lax.axis_index("zh")
+    head = ((lax.axis_index("zl") * 2 + lax.axis_index("x")) * 2 + lax.axis_index("y")) * 2
+    head = head + lax.axis_index("c")
+    starts, ends = doc_bounds(lengths, batch)
+    rows_n = HEAD_ROWS
+    lane = lane_iota(rows_n)
+    gk[...] = jnp.zeros_like(gk)
+    gv[...] = jnp.zeros_like(gv)
+    bias_s[...] = jnp.zeros_like(bias_s)
+    gain_s[...] = jnp.zeros_like(gain_s)
+
+    @pl.loop(0, tokens_n // rows_n)
+    def _(i):
+        row = pl.ds(pl.multiple_of(i * rows_n, rows_n), rows_n)
+        value = x_ref[row, :].astype(jnp.float32)
+        scale = lax.rsqrt(jnp.mean(value * value, axis=1, keepdims=True) + EPS)
+        normed_s[row, :] = (value * scale * gain_ref[...]).astype(jnp.bfloat16)
+        kept = o_ref[row, :]
+        grad = jnp.concatenate(
+            [g_ref[row, :].astype(jnp.float32), jnp.zeros((rows_n, 64), jnp.float32)], axis=1
+        )
+        delta = jnp.sum(jnp.where(lane < 64, grad * kept, 0.0), axis=1, keepdims=True)
+        log_total = kept[:, 64:65]
+        query = qf_ref[row, :].astype(jnp.float32)
+        for j, part in enumerate(pieces(log_total)):
+            query = jnp.where(lane == 64 + 40 + j, -part, query)
+        qb[row, :] = query.astype(jnp.bfloat16)
+        for j, part in enumerate(pieces(delta)):
+            grad = jnp.where(lane == 64 + j, -part, grad)
+        gb[row, :] = grad.astype(jnp.bfloat16)
+
+    for i in range(tokens_n // rows_n):
+        row = pl.ds(i * rows_n, rows_n)
+        low, high = key_range(starts, ends, i * rows_n, (i + 1) * rows_n - 1)
+        query, grad = qb[row, :], gb[row, :]
+
+        def one_chunk(k, total):
+            col = pl.ds(pl.multiple_of(k * KEY_CHUNK, KEY_CHUNK), KEY_CHUNK)
+            key = kf_ref[col, :]
+            last = (((1,), (1,)), ((), ()))
+            first = (((0,), (0,)), ((), ()))
+            scores = lax.dot_general(query, key, last, preferred_element_type=jnp.float32)
+            probs = jnp.exp(scores)
+            centred = lax.dot_general(grad, vf_ref[col, :], last, preferred_element_type=jnp.float32)
+            back = (probs * centred).astype(jnp.bfloat16)
+            gv[col, :] += lax.dot_general(
+                probs.astype(jnp.bfloat16), grad, first, preferred_element_type=jnp.float32
+            )
+            gk[col, :] += lax.dot_general(back, query, first, preferred_element_type=jnp.float32)
+            return total + jnp.dot(back, key, preferred_element_type=jnp.float32)
+
+        total = lax.fori_loop(
+            low // KEY_CHUNK,
+            (high + KEY_CHUNK - 1) // KEY_CHUNK,
+            one_chunk,
+            jnp.zeros((rows_n, 128), jnp.float32),
+        )
+        gqkv[row, :128] = jnp.where(lane < 64, total * 0.125, 0.0).astype(jnp.bfloat16)
+        kept = kf_ref[row, :].astype(jnp.float32)
+        same = jnp.where((lane >= 80) & (lane < 88), total * kept, 0.0)
+        every = jnp.where(lane == 72, total, 0.0)
+        bias_s[0:1, :] += jnp.sum(same, axis=0, keepdims=True)
+        bias_s[1:2, :] += jnp.sum(every, axis=0, keepdims=True)
+
+    @pl.loop(0, tokens_n // rows_n)
+    def _(i):
+        row = pl.ds(pl.multiple_of(i * rows_n, rows_n), rows_n)
+        raw = raw_ref[row, :]
+        scale = lax.rsqrt(pair_mean(raw * raw) + EPS)
+        cosine, sine = angles_of(cs_ref[row, :])
+        key_part = pltpu.roll(gk[row, :].astype(jnp.bfloat16).astype(jnp.float32), 64, 1)
+        grad = jnp.where(lane < 64, gqkv[row, :128].astype(jnp.float32), key_part)
+        turned = grad * cosine - swap_halves(grad) * sine
+        gain_s[0:1, :] += jnp.sum(turned * raw * scale, axis=0, keepdims=True)
+        weighted = turned * qk_gain_ref[...]
+        back = scale * weighted - raw * (scale * scale * scale) * pair_mean(weighted * raw)
+        gqkv[row, :] = jnp.concatenate([back, gv[row, :][:, :64]], axis=1).astype(jnp.bfloat16)
+
+    @pl.loop(0, tokens_n // rows_n)
+    def _(i):
+        row = pl.ds(pl.multiple_of(i * rows_n, rows_n), rows_n)
+        grad = lax.dot_general(
+            gqkv[row, :], wh_ref[...], (((1,), (1,)), ((), ())), preferred_element_type=jnp.float32
+        )
+        gn_out[row, :] = grad.astype(jnp.bfloat16)
+        value = x_ref[row, :].astype(jnp.float32)
+        scale = lax.rsqrt(jnp.mean(value * value, axis=1, keepdims=True) + EPS)
+        term = grad * value * scale
+        small_out[0:1, :] = jnp.where(i == 0, 0.0, small_out[0:1, :]) + jnp.sum(
+            term, axis=0, keepdims=True
+        )
+
+    gw_out[...] = lax.dot_general(
+        normed_s[...], gqkv[...], (((0,), (0,)), ((), ())), preferred_element_type=jnp.float32
+    ).astype(jnp.bfloat16)
+    one = lane_iota(1)
+    both = gain_s[0:1, :]
+    turned = pltpu.roll(jnp.broadcast_to(both, (8, 128)), 64, 1)[0:1, :]
+    wide = lane_iota(1, 1024)
+    query_gain = jnp.concatenate([jnp.where(one < 64, both, turned)] * 8, axis=1)
+    key_gain = jnp.concatenate([jnp.where(one < 64, turned, both)] * 8, axis=1)
+    small_out[1:2, :] = jnp.zeros((1, 1024), jnp.float32)
+    small_out[2:3, :] = jnp.where(wide // 64 == head, query_gain, 0.0)
+    small_out[3:4, :] = jnp.where(wide // 64 == head, key_gain, 0.0)
+    same = jnp.sum(bias_s[0:1, :], axis=1, keepdims=True)
+    every = jnp.sum(bias_s[1:2, :], axis=1, keepdims=True)
+    row_bias = jnp.where(wide == 2 * head, same, 0.0)
+    small_out[4:5, :] = jnp.where(wide == 2 * head + 1, every - same, row_bias)
+    small_out[5:8, :] = jnp.zeros((3, 1024), jnp.float32)
+
+
+def attend_back(lengths, x_all, wh, grad, kept, qf, kf, vf, raw, cs, gain, qk_gain):
+    bf, f32 = jnp.bfloat16, jnp.float32
+    n = x_all.shape[0]
+    sm = pl.BlockSpec(memory_space=pltpu.SMEM)
+    vm = pl.BlockSpec(memory_space=pltpu.VMEM)
+    return pl.pallas_call(
+        attend_back_kernel,
+        out_shape=[
+            jax.ShapeDtypeStruct((n, 1024), bf),
+            jax.ShapeDtypeStruct((1024, 192), bf),
+            jax.ShapeDtypeStruct((8, 1024), f32),
+        ],
+        in_specs=[sm] + [vm] * 11,
+        out_specs=[vm] * 3,
+        scratch_shapes=[
+            pltpu.VMEM((n, 128), bf),
+            pltpu.VMEM((n, 128), bf),
+            pltpu.VMEM((n, 128), f32),
+            pltpu.VMEM((n, 128), f32),
+            pltpu.VMEM((n, 192), bf),
+            pltpu.VMEM((n, 1024), bf),
+            pltpu.VMEM((8, 128), f32),
+            pltpu.VMEM((8, 128), f32),
+        ],
+        compiler_params=pltpu.CompilerParams(vmem_limit_bytes=VMEM_BYTES),
+        name="attend_back",
+    )(lengths, x_all, wh, grad, kept, qf, kf, vf, raw, cs, gain, qk_gain)
+
+
+def middle_kernel(
+    att, tok, cot, wo, wgu, wd, gf, gain_ref,
+    out_ref, gatt_out, gres_out, gwgu_out, gwd_out, gwo_out, small_out,
+    lb, ap, at2, at3, att_s, n2, gh, hid, ggu, kept, sent, landed, red_send, red_land,
+    ga3, ga2, ag1, ls, lb2, out_acc, send_sems, recv_sems, local_sems,
+):
+    bf, f32 = jnp.bfloat16, jnp.float32
+    last = (((1,), (1,)), ((), ()))
+    first = (((0,), (0,)), ((), ()))
+    net = Net(send_sems, recv_sems, local_sems)
+    zh, zl, x, y, c = (net.me[a] for a in AXES)
+    net.barrier(CHIP_FLIPS + [("c",), ("zh",)])
+    chips = ("zl", "x", "y")
+    my_chip = net.index(chips)
+    lane = lane_iota(64)
+
+    step = net.send(att.at[:, 1 - c], lb, ("c",))
+    for p in range(4):
+        gh[p] = lax.dot_general(gf[p], wd[...], last, preferred_element_type=f32).astype(gh.dtype)
+    step.wait_recv()
+
+    @pl.loop(0, 16)
+    def _(i):
+        own = jnp.concatenate([att[i, c]] * 2, axis=1)
+        other = jnp.concatenate([lb[i]] * 2, axis=1)
+        ap[i // 8, i % 8] = jnp.where((lane < 64) == (c == 0), own, other)
+
+    arrive = []
+    for flips in CHIP_FLIPS:
+        arrive.append(net.send(ap.at[:, net.index(chips, flips)], at2.at[my_chip], flips))
+    net_own = net.local(ap.at[:, my_chip], at2.at[my_chip])
+    net_own.wait()
+    for copy in arrive:
+        copy.wait_recv()
+    step = net.send(at2.at[:, 1 - zh], at3, ("zh",))
+    for k in range(8):
+        att_s[pl.ds(pl.multiple_of(zh * 64, 64), 64), 128 * k : 128 * (k + 1)] = at2[k, zh]
+    step.wait_recv()
+    for k in range(8):
+        att_s[pl.ds(pl.multiple_of(64 - zh * 64, 64), 64), 128 * k : 128 * (k + 1)] = at3[k]
+
+    resid = tok[...].astype(f32) + jnp.dot(att_s[...], wo[...], preferred_element_type=f32)
+    scale = lax.rsqrt(jnp.mean(resid * resid, axis=1, keepdims=True) + EPS)
+    gain = gain_ref[...]
+    my_pair = net.index(("zl", "x"))
+    n2[my_pair, c] = (resid * scale * gain).astype(bf)
+    group = [("zl",), ("x",), ("zl", "x")]
+    to_sibling = [net.send(n2.at[my_pair, c], n2.at[my_pair, c], ("c",))]
+    from_chips = [net.send(n2.at[my_pair, c], n2.at[my_pair, c], flips) for flips in group]
+
+    def feed(pair):
+        rows = n2[pair].reshape(256, 1024)
+        gate = jnp.dot(rows, wgu[0], preferred_element_type=f32)
+        up = jnp.dot(rows, wgu[1], preferred_element_type=f32)
+        sig = 1.0 / (1.0 + jnp.exp(-gate))
+        silu = gate * sig
+        hid[pair] = (silu * up).astype(bf)
+        back = gh[pair]
+        ggu[0, pair] = (back * up * sig * (1.0 + gate * (1.0 - sig))).astype(bf)
+        ggu[1, pair] = (back * silu).astype(bf)
+
+    def back_product(pair):
+        total = lax.dot_general(ggu[0, pair], wgu[0], last, preferred_element_type=f32)
+        return total + lax.dot_general(ggu[1, pair], wgu[1], last, preferred_element_type=f32)
+
+    def out_product(pair):
+        return jnp.dot(hid[pair], wd[...], preferred_element_type=f32)
+
+    def share(kind, slot, value):
+        kept[kind, slot, 0] = value[:128]
+        kept[kind, slot, 1] = value[128:]
+        sent[kind, slot] = kept[kind, slot, 1 - c].astype(bf)
+        return net.send(sent.at[kind, slot], landed.at[kind, slot], ("c",))
+
+    pairs = [my_pair] + [net.index(("zl", "x"), flips) for flips in group]
+    halves = {}
+    reduced = {0: [], 1: []}
+
+    def finish_half(kind, slot):
+        halves[kind, slot].wait_recv()
+        total = kept[kind, slot, c] + landed[kind, slot].astype(f32)
+        if slot == 0:
+            kept[kind, slot, c] = total
+        else:
+            red_send[kind, slot - 1] = total.astype(bf)
+            reduced[kind].append(
+                net.send(red_send.at[kind, slot - 1], red_land.at[kind, slot - 1], group[slot - 1])
+            )
+
+    to_sibling[0].wait_recv()
+    feed(pairs[0])
+    halves[0, 0] = share(0, 0, back_product(pairs[0]))
+    for k in range(3):
+        from_chips[k].wait_recv()
+        to_sibling.append(net.send(n2.at[pairs[k + 1], c], n2.at[pairs[k + 1], c], ("c",)))
+    for k in range(3):
+        to_sibling[k + 1].wait_recv()
+        feed(pairs[k + 1])
+        halves[0, k + 1] = share(0, k + 1, back_product(pairs[k + 1]))
+        if k > 0:
+            finish_half(0, k)
+    finish_half(0, 3)
+    finish_half(0, 0)
+    for k in (1, 2, 3, 0):
+        halves[1, k] = share(1, k, out_product(pairs[k]))
+    for k in (1, 2, 3, 0):
+        finish_half(1, k)
+
+    gwd_out[...] = lax.dot_general(
+        hid[...].reshape(1024, 512), gf[...].reshape(1024, 1024), first, preferred_element_type=f32
+    ).astype(bf)
+    for k in range(2):
+        gwgu_out[k] = lax.dot_general(
+            n2[...].reshape(1024, 1024), ggu[k].reshape(1024, 512), first, preferred_element_type=f32
+        ).astype(bf)
+
+    for copy in reduced[0]:
+        copy.wait_recv()
+    total = kept[0, 0, c]
+    for k in range(3):
+        total = total + red_land[0, k].astype(f32)
+    small_out[...] = jnp.zeros_like(small_out)
+    small_out[1:2, :] = jnp.sum(total * resid * scale, axis=0, keepdims=True)
+    weighted = total * gain
+    mean = jnp.mean(weighted * resid, axis=1, keepdims=True)
+    grad_resid = cot[...].astype(f32) + scale * weighted - resid * (scale * scale * scale) * mean
+    gres_out[...] = grad_resid
+    branch = grad_resid.astype(bf)
+    grad_att = lax.dot_general(branch, wo[...], last, preferred_element_type=f32).astype(bf)
+    for k in range(8):
+        for b in range(2):
+            ga3[b, k] = grad_att[64 * b : 64 * (b + 1), 128 * k : 128 * (k + 1)]
+    step = net.send(ga3.at[1 - zh], ga2.at[zh], ("zh",))
+    gwo_out[...] = lax.dot_general(att_s[...], branch, first, preferred_element_type=f32).astype(bf)
+    ga2[zh] = ga3[zh]
+    step.wait_recv()
+    arrive = []
+    for flips in CHIP_FLIPS:
+        arrive.append(net.send(ga2.at[:, net.index(chips, flips)], ag1.at[:, my_chip], flips))
+    net_own = net.local(ga2.at[:, my_chip], ag1.at[:, my_chip])
+    for copy in reduced[1]:
+        copy.wait_recv()
+    total = kept[1, 0, c] + resid
+    for k in range(3):
+        total = total + red_land[1, k].astype(f32)
+    out_ref[...] = total.astype(bf)
+    net_own.wait()
+    for copy in arrive:
+        copy.wait_recv()
+
+    @pl.loop(0, 16)
+    def _(i):
+        both = ag1[i // 8, i % 8]
+        low, high = both[:, :64], both[:, 64:]
+        low32, high32 = low.astype(f32), high.astype(f32)
+        ls[i] = jnp.where(c == 0, high32, low32).astype(bf)
+        lb2[i] = jnp.where(c == 0, low32, high32).astype(bf)
+
+    step = net.send(ls, gatt_out.at[:, c], ("c",))
+    keep = net.local(lb2, gatt_out.at[:, c])
+    keep.wait()
+    step.wait_recv()
+    net.finish()
+
+
+def middle(att, tok, cot, wo, wgu, wd, gf, gain):
+    bf, f32 = jnp.bfloat16, jnp.float32
+    vm = pl.BlockSpec(memory_space=pltpu.VMEM)
+    return pl.pallas_call(
+        middle_kernel,
+        out_shape=[
+            jax.ShapeDtypeStruct((128, 1024), bf),
+            jax.ShapeDtypeStruct((16, 2, 64, 64), bf),
+            jax.ShapeDtypeStruct((128, 1024), f32),
+            jax.ShapeDtypeStruct((2, 1024, 512), bf),
+            jax.ShapeDtypeStruct((512, 1024), bf),
+            jax.ShapeDtypeStruct((1024, 1024), bf),
+            jax.ShapeDtypeStruct((8, 1024), f32),
+        ],
+        in_specs=[vm] * 8,
+        out_specs=[vm] * 7,
+        scratch_shapes=[
+            pltpu.VMEM((16, 64, 64), bf),
+            pltpu.VMEM((2, 8, 64, 128), bf),
+            pltpu.VMEM((8, 2, 64, 128), bf),
+            pltpu.VMEM((8, 64, 128), bf),
+            pltpu.VMEM((128, 1024), bf),
+            pltpu.VMEM((4, 2, 128, 1024), bf),
+            pltpu.VMEM((4, 256, 512), f32),
+            pltpu.VMEM((4, 256, 512), bf),
+            pltpu.VMEM((2, 4, 256, 512), bf),
+            pltpu.VMEM((2, 4, 2, 128, 1024), f32),
+            pltpu.VMEM((2, 4, 128, 1024), bf),
+            pltpu.VMEM((2, 4, 128, 1024), bf),
+            pltpu.VMEM((2, 3, 128, 1024), bf),
+            pltpu.VMEM((2, 3, 128, 1024), bf),
+            pltpu.VMEM((2, 8, 64, 128), bf),
+            pltpu.VMEM((2, 8, 64, 128), bf),
+            pltpu.VMEM((2, 8, 64, 128), bf),
+            pltpu.VMEM((16, 64, 64), bf),
+            pltpu.VMEM((16, 64, 64), bf),
+            pltpu.VMEM((8, 128), f32),
+            pltpu.SemaphoreType.DMA((48,)),
+            pltpu.SemaphoreType.DMA((48,)),
+            pltpu.SemaphoreType.DMA((4,)),
+        ],
+        compiler_params=pltpu.CompilerParams(
+            collective_id=2, has_side_effects=True, vmem_limit_bytes=VMEM_BYTES
+        ),
+        name="middle",
+    )(att, tok, cot, wo, wgu, wd, gf, gain)
+
+
+class Reduce:
+    MASKS = [("x", "zl", "y"), ("x", "zl"), ("x", "y"), ("x",), ("zl", "y"), ("zl",), ("y",), ()]
+
+    def __init__(self, net, parts, landing, sends, arrivals):
+        self.net, self.parts, self.landing = net, parts, landing
+        self.sends, self.arrivals = sends, arrivals
+        self.c = net.me["c"]
+        self.from_sibling, self.incoming = {}, {}
+
+    def chip(self, mask):
+        return self.net.index(("zl", "x", "y"), mask)
+
+    def begin(self, masks):
+        for mask in masks:
+            slot = self.MASKS.index(mask)
+            self.from_sibling[mask] = self.net.send(
+                self.parts.at[:, self.chip(mask), 1 - self.c], self.landing.at[slot], ("c",)
+            )
+
+    def total(self, mask, upto):
+        slot = self.MASKS.index(mask)
+        value = self.parts[:, self.chip(mask), self.c].astype(jnp.float32)
+        value = value + self.landing[slot].astype(jnp.float32)
+        for stage in upto:
+            value = value + self.arrivals[self.place(mask, stage)].astype(jnp.float32)
+        return value
+
+    def place(self, mask, stage):
+        order = {"x": [("zl", "y"), ("zl",), ("y",), ()], "zl": [("y",), ()], "y": [()]}[stage]
+        return {"x": 0, "zl": 4, "y": 6}[stage] + order.index(mask)
+
+    def forward(self, mask):
+        stage = mask[0]
+        rest = mask[1:]
+        before = {"x": (), "zl": ("x",), "y": ("x", "zl")}[stage]
+        for earlier in before:
+            self.incoming[mask, earlier].wait_recv()
+        if not before:
+            self.from_sibling[mask].wait_recv()
+        elif mask in self.from_sibling:
+            self.from_sibling[mask].wait_recv()
+        slot = self.place(rest, stage)
+        self.sends[slot] = self.total(mask, before).astype(jnp.bfloat16)
+        self.incoming[rest, stage] = self.net.send(
+            self.sends.at[slot], self.arrivals.at[slot], (stage,)
+        )
+
+    def result(self):
+        self.from_sibling[()].wait_recv()
+        for stage in ("x", "zl", "y"):
+            self.incoming[(), stage].wait_recv()
+        return self.total((), ("x", "zl", "y"))
+
+
+def reduce_kernel(
+    gn, gw, gwgu, gwd, gwo, small_a, small_b, tok, gres, gain_ref,
+    gtok_out, gwqkv_out, gwo_out, gwg_out, gwu_out, gwd_out, small_out,
+    n_land, n_send, n_arr, n_half, n_half_land, grad_s,
+    o_land, o_send, o_arr, o_half, o_half_land, o_keep,
+    y_wgu, y_wd, h_wgu, h_wd, h_wgu_land, h_wd_land, f_sum, f1, f2,
+    w_land, w_t, w_p, w_q, s_acc, s_land, send_sems, recv_sems, local_sems,
+):
+    bf, f32 = jnp.bfloat16, jnp.float32
+    net = Net(send_sems, recv_sems, local_sems)
+    zh, zl, x, y, c = (net.me[a] for a in AXES)
+    chips = ("zl", "x", "y")
+    my_chip = net.index(chips)
+    my_pair = net.index(("zl", "x"))
+    net.barrier(CHIP_FLIPS + [("c",), ("zh",)])
+    tree_n = Reduce(net, gn, n_land, n_send, n_arr)
+    tree_o = Reduce(net, gwo, o_land, o_send, o_arr)
+
+    y_far = [net.send(gwgu.at[k, 1 - zh, :, 1 - y], y_wgu.at[k, 1], ("y",)) for k in range(2)]
+    y_far.append(net.send(gwd.at[1 - zh, 1 - y], y_wd.at[1], ("y",)))
+    tree_n.begin(Reduce.MASKS[:4])
+    w_zh = net.send(gw.at[1 - zh], w_land, ("zh",))
+    tree_o.begin(Reduce.MASKS)
+    tree_n.begin(Reduce.MASKS[4:])
+    rounds = ("c", "x", "y", "zl", "zh")
+    s_acc[0] = small_a[...] + small_b[...]
+    s_step = net.send(s_acc.at[0], s_land.at[0], (rounds[0],))
+
+    def small_round(step, k):
+        step.wait_recv()
+        total = s_acc[k] + s_land[k]
+        if k == 4:
+            small_out[...] = total
+            return None
+        s_acc[k + 1] = total
+        return net.send(s_acc.at[k + 1], s_land.at[k + 1], (rounds[k + 1],))
+
+    for mask in Reduce.MASKS[:4]:
+        tree_n.forward(mask)
+    y_near = [net.send(gwgu.at[k, zh, :, 1 - y], y_wgu.at[k, 0], ("y",)) for k in range(2)]
+    y_near.append(net.send(gwd.at[zh, 1 - y], y_wd.at[0], ("y",)))
+    for mask in Reduce.MASKS[:4]:
+        tree_o.forward(mask)
+    s_step = small_round(s_step, 0)
+    h_steps = []
+    for k in range(2):
+        y_far[k].wait_recv()
+        h_wgu[k] = (gwgu[k, 1 - zh, :, y].astype(f32) + y_wgu[k, 1].astype(f32)).astype(bf)
+        h_steps.append(net.send(h_wgu.at[k], h_wgu_land.at[k], ("zh",)))
+    y_far[2].wait_recv()
+    h_wd[...] = (gwd[1 - zh, y].astype(f32) + y_wd[1].astype(f32)).astype(bf)
+    h_steps.append(net.send(h_wd, h_wd_land, ("zh",)))
+    s_step = small_round(s_step, 1)
+    w_zh.wait_recv()
+    w_t[...] = (gw[zh].astype(f32) + w_land[...].astype(f32)).astype(bf)
+    w_c = net.send(w_t.at[:, 1 - c], w_p.at[:, c], ("c",))
+    w_keep = net.local(w_t.at[:, c], w_p.at[:, c])
+    tree_n.forward(("zl", "y"))
+    tree_n.forward(("zl",))
+    w_keep.wait()
+    w_c.wait_recv()
+    w_steps = []
+    for flips in CHIP_FLIPS:
+        w_steps.append(net.send(w_p.at[net.index(chips, flips)], w_q.at[my_chip], flips))
+    w_own = net.local(w_p.at[my_chip], w_q.at[my_chip])
+    s_step = small_round(s_step, 2)
+    tree_o.forward(("zl", "y"))
+    tree_o.forward(("zl",))
+    tree_n.forward(("y",))
+    tree_o.forward(("y",))
+    s_step = small_round(s_step, 3)
+
+    total = tree_n.result()
+    grad_s[0] = total[0]
+    grad_s[1] = total[1]
+    n_half[...] = grad_s[1 - zh].astype(bf)
+    n_step = net.send(n_half, n_half_land, ("zh",))
+    total = tree_o.result()
+    o_keep[0] = total[0]
+    o_keep[1] = total[1]
+    o_half[...] = o_keep[1 - zh].astype(bf)
+    o_step = net.send(o_half, o_half_land, ("zh",))
+    n_step.wait_recv()
+    grad_s[1 - zh] = n_half_land[...].astype(f32)
+    gain = gain_ref[...]
+    for b in range(2):
+        value = tok[b].astype(f32)
+        scale = lax.rsqrt(jnp.mean(value * value, axis=1, keepdims=True) + EPS)
+        weighted = grad_s[b] * gain
+        mean = jnp.mean(weighted * value, axis=1, keepdims=True)
+        back = scale * weighted - value * (scale * scale * scale) * mean
+        gtok_out[b] = (gres[b] + back).astype(bf)
+    o_step.wait_recv()
+    gwo_out[...] = o_keep[zh] + o_half_land[...].astype(f32)
+    s_step = small_round(s_step, 4)
+    w_own.wait()
+    for copy in w_steps:
+        copy.wait_recv()
+    for h in range(16):
+        gwqkv_out[:, 192 * h : 192 * (h + 1)] = w_q[h // 2, h % 2].astype(f32)
+
+    f_steps = []
+    for k in range(2):
+        y_near[k].wait_recv()
+        h_steps[k].wait_recv()
+        for j in range(4):
+            rows = gwgu[k, zh, j, y].astype(f32) + y_wgu[k, 0, j].astype(f32)
+            rows = rows + h_wgu_land[k, j].astype(f32)
+            f_sum[k, j, 0] = rows[:32].astype(bf)
+            f_sum[k, j, 1] = rows[32:].astype(bf)
+        for flips in (("x",), ("zl",), ("zl", "x")):
+            f_steps.append(
+                net.send(f_sum.at[k, net.index(("zl", "x"), flips)], f1.at[k, my_pair], flips)
+            )
+        f1[k, my_pair] = f_sum[k, my_pair]
+    y_near[2].wait_recv()
+    h_steps[2].wait_recv()
+    gwd_out[...] = gwd[zh, y].astype(f32) + y_wd[0].astype(f32) + h_wd_land[...].astype(f32)
+    f_c = []
+    for k in range(2):
+        for j in range(3):
+            f_steps[3 * k + j].wait_recv()
+        f_c.append(net.send(f1.at[k, :, 1 - c], f2.at[k, :, c], ("c",)))
+        f2[k, :, c] = f1[k, :, c]
+    for k, out in ((0, gwg_out), (1, gwu_out)):
+        f_c[k].wait_recv()
+        for pair in range(4):
+            for cc in range(2):
+                for part in range(4):
+                    idx = (part // 2) * 16 + pair * 4 + (part % 2) * 2 + cc
+                    out[:, 128 * idx : 128 * (idx + 1)] = f2[
+                        k, pair, cc, :, 128 * part : 128 * (part + 1)
+                    ].astype(f32)
+    net.finish()
+
+
+def reduce_all(gn, gw, gwgu, gwd, gwo, small_a, small_b, tok, gres, gain):
+    bf, f32 = jnp.bfloat16, jnp.float32
+    vm = pl.BlockSpec(memory_space=pltpu.VMEM)
+    V = pltpu.VMEM
+    return pl.pallas_call(
+        reduce_kernel,
+        out_shape=[
+            jax.ShapeDtypeStruct((2, 64, 1024), bf),
+            jax.ShapeDtypeStruct((32, 3072), f32),
+            jax.ShapeDtypeStruct((32, 1024), f32),
+            jax.ShapeDtypeStruct((32, 4096), f32),
+            jax.ShapeDtypeStruct((32, 4096), f32),
+            jax.ShapeDtypeStruct((128, 1024), f32),
+            jax.ShapeDtypeStruct((8, 1024), f32),
+        ],
+        in_specs=[vm] * 10,
+        out_specs=[vm] * 7,
+        scratch_shapes=[
+            V((8, 2, 64, 1024), bf),
+            V((7, 2, 64, 1024), bf),
+            V((7, 2, 64, 1024), bf),
+            V((64, 1024), bf),
+            V((64, 1024), bf),
+            V((2, 64, 1024), f32),
+            V((8, 2, 32, 1024), bf),
+            V((7, 2, 32, 1024), bf),
+            V((7, 2, 32, 1024), bf),
+            V((32, 1024), bf),
+            V((32, 1024), bf),
+            V((2, 32, 1024), f32),
+            V((2, 2, 4, 64, 512), bf),
+            V((2, 128, 1024), bf),
+            V((2, 4, 64, 512), bf),
+            V((128, 1024), bf),
+            V((2, 4, 64, 512), bf),
+            V((128, 1024), bf),
+            V((2, 4, 2, 32, 512), bf),
+            V((2, 4, 2, 32, 512), bf),
+            V((2, 4, 2, 32, 512), bf),
+            V((8, 2, 32, 192), bf),
+            V((8, 2, 32, 192), bf),
+            V((8, 2, 32, 192), bf),
+            V((8, 2, 32, 192), bf),
+            V((5, 8, 1024), f32),
+            V((5, 8, 1024), f32),
+            pltpu.SemaphoreType.DMA((72,)),
+            pltpu.SemaphoreType.DMA((72,)),
+            pltpu.SemaphoreType.DMA((4,)),
+        ],
+        compiler_params=pltpu.CompilerParams(
+            collective_id=3, has_side_effects=True, vmem_limit_bytes=VMEM_BYTES
+        ),
+        name="reduce_all",
+    )(gn, gw, gwgu, gwd, gwo, small_a, small_b, tok, gres, gain)
+
+
+def frequencies():
+    index = np.arange(32, dtype=np.float32)
+    return np.broadcast_to((THETA ** (-2.0 * index / 64.0)).astype(np.float32)[:, None], (32, 128))
+
+
+def on_device_cube(
+    tokens,
+    cotangent,
+    w_qkv,
+    w_out,
+    w_gate,
+    w_up,
+    w_down,
+    norm_attn,
+    norm_ffn,
+    q_gain,
+    k_gain,
+    var_bias,
+    doc_lengths,
+    variate,
+    times,
+):
+    f32 = jnp.float32
+    place = {name: lax.axis_index(name) for name in AXES}
+    rank = jnp.int32(0)
+    for name in AXES:
+        rank = rank * 2 + place[name]
+    gains = jnp.concatenate([norm_attn, norm_ffn, q_gain, k_gain]).astype(f32)
+    small = jnp.stack([variate.reshape(128).astype(f32), times.reshape(128).astype(f32), gains])
+    small = jnp.concatenate([small, jnp.zeros((5, 128), f32)])
+    x_all, wh, wgu, wd, wo, gf, small_all = gather_all(
+        tokens, cotangent.reshape(128, 1024), w_qkv, w_out, w_gate, w_up, w_down, small
+    )
+    x_all = x_all.reshape(2048, 1024)
+    wh = wh.reshape(1024, 192)
+    small_all = small_all.reshape(32, 8, 128)
+    rows = lax.dynamic_slice(small_all, (0, 0, place["zh"] * 64), (32, 2, 64))
+    rows = rows.transpose(1, 0, 2).reshape(2, 2048)
+    all_gains = small_all[:, 2].reshape(32, 4, 32).transpose(1, 0, 2).reshape(4, 1024)
+    head = rank % 16
+    qk_gain = lax.dynamic_slice(all_gains, (2, head * 64), (2, 64)).reshape(1, 128)
+    gain_attn, gain_ffn = all_gains[0:1], all_gains[1:2]
+    att, kept, qf, kf, vf, raw, cs = attend(
+        doc_lengths, var_bias, x_all, wh, rows, gain_attn, qk_gain, jnp.asarray(frequencies())
+    )
+    out, gatt, gres, gwgu, gwd, gwo, small_m = middle(
+        att.reshape(16, 2, 64, 64),
+        tokens.reshape(128, 1024),
+        cotangent.reshape(128, 1024),
+        wo.reshape(1024, 1024),
+        wgu.reshape(2, 1024, 512),
+        wd.reshape(512, 1024),
+        gf.reshape(4, 256, 1024),
+        gain_ffn,
+    )
+    gn, gw, small_b = attend_back(
+        doc_lengths, x_all, wh, gatt.reshape(2048, 64), kept, qf, kf, vf, raw, cs,
+        gain_attn, qk_gain,
+    )
+    gtok, gwqkv, gwo, gwg, gwu, gwd, small = reduce_all(
+        gn.reshape(2, 8, 2, 64, 1024),
+        gw.reshape(2, 8, 2, 32, 192),
+        gwgu.reshape(2, 2, 4, 2, 64, 512),
+        gwd.reshape(2, 2, 128, 1024),
+        gwo.reshape(2, 8, 2, 32, 1024),
+        small_m,
+        small_b,
+        tokens,
+        gres.reshape(2, 64, 1024),
+        gain_attn,
+    )
+    mine = lax.dynamic_slice(small, (0, rank * 32), (4, 32))
+    return (
+        out.reshape(2, 64, 1024),
+        gtok,
+        gwqkv,
+        gwo,
+        gwg,
+        gwu,
+        gwd,
+        mine[0],
+        mine[1],
+        mine[2],
+        mine[3],
+        small[4, :32].reshape(16, 2),
+    )
+
+
+def run_parts(mesh, body, split):
+    rows, cut = P(split, None), P(split)
+    part = P(None, split, None)
+    return jax.shard_map(
+        body,
+        mesh=mesh,
+        in_specs=(part, part) + (rows,) * 5 + (cut,) * 4 + (P(), P(), P(None, split), P(None, split)),
+        out_specs=(part, part) + (rows,) * 5 + (cut,) * 4 + (P(),),
+        check_vma=False,
+    )
+
+
 def solution(mesh):
-    return jax.shard_map(
-        on_device,
-        mesh=mesh,
-        in_specs=(
-            P(None, ("head", "blk"), None),
-            P(None, ("head", "blk"), None),
-            P(("head", "blk"), None),
-            P(("head", "blk"), None),
-            P(("head", "blk"), None),
-            P(("head", "blk"), None),
-            P(("head", "blk"), None),
-            P(("head", "blk")),
-            P(("head", "blk")),
-            P(("head", "blk")),
-            P(("head", "blk")),
-            P(),
-            P(),
-            P(None, ("head", "blk")),
-            P(None, ("head", "blk")),
-        ),
-        out_specs=(
-            P(None, ("head", "blk"), None),
-            P(None, ("head", "blk"), None),
-            P(("head", "blk"), None),
-            P(("head", "blk"), None),
-            P(("head", "blk"), None),
-            P(("head", "blk"), None),
-            P(("head", "blk"), None),
-            P(("head", "blk")),
-            P(("head", "blk")),
-            P(("head", "blk")),
-            P(("head", "blk")),
-            P(),
-        ),
-        check_vma=False,
-    )
+    sizes = (mesh.shape["head"], mesh.shape["blk"])
+    general = run_parts(mesh, on_device, ("head", "blk"))
+    if sizes != (8, 4):
+        return general
+    cube = jax.sharding.Mesh(mesh.devices.reshape(2, 2, 2, 2, 2), AXES)
+    special = run_parts(cube, on_device_cube, AXES)
+
+    def chosen(*arrays):
+        tokens, w_gate, var_bias, lengths = arrays[0], arrays[4], arrays[11], arrays[12]
+        shapes = (tokens.shape, w_gate.shape, var_bias.shape, lengths.shape)
+        if shapes == ((2, 2048, 1024), (1024, 4096), (16, 2), (2, 8)):
+            return special(*arrays)
+        return general(*arrays)
+
+    return chosen

time: 1740 us -> 341 us (0.20)
  waiting for transfers between devices: 1150 us -> 0 us
  Pallas kernels: 0 us -> 319 us
  matrix products: 196 us -> 0 us
  blocking collectives: 132 us -> 0 us
  local copies, waits for them, and re-layouts: 122 us -> 18.1 us
  other arithmetic: 55.2 us -> 2.8 us
  starting transfers between devices: 47.5 us -> 0 us
    unnamed x11 -> x0, waiting for transfers between devices: 918 us -> none
    pallas_call x0 -> x5, Pallas kernels: none -> 319 us  [the longest x1 95 us: reduce_all(): pl.pallas_call(reduce_kernel, out_shape=[jax.ShapeDtypeStruct((2, 64, 102...]
    all_gather x7 -> x0, waiting for transfers between devices: 228 us -> none  [the longest x1 74.1 us: on_device(): lax.all_gather(w_down, ('head', 'blk'), axis=0, tiled=True)]
    dot_general x58 -> x0, matrix products: 196 us -> none  [the longest x10 64.5 us: row_contract(): lax.dot_general(left_mat, right_mat, (((0,), (0,)), ((), ())), preferred_...]
    unnamed x2 -> x0, blocking collectives: 85.1 us -> none
    unnamed x252 -> x20, local copies, waits for them, and re-layouts: 67.8 us -> 10.1 us
    all_to_all x8 -> x0, starting transfers between devices: 47.1 us -> none  [the longest x2 20.4 us: on_device(): lax.all_to_all(attn_heads.astype(jnp.bfloat16), 'head', split_axis=0, con...]
    all_to_all x2 -> x0, blocking collectives: 36.6 us -> none  [on_device(): lax.all_to_all(packed, 'head', split_axis=1, concat_axis=0, tiled=True)]
  transfers between devices with their start and end apart: 18 -> 0, of which waited for: 7 -> 0; matrix products, arithmetic and copies ran while one was open for 13% -> 0% of each run, Pallas kernels for 0% -> 0%
where the time goes in v1:
time: 341 us; the launch traced here: 340 us
  Pallas kernels  319 us (94%)
  local copies, waits for them, and re-layouts  18.1 us (5%)
    pallas_call x1, Pallas kernels, reduce_all(): pl.pallas_call(reduce_kernel, out_shape=[jax.ShapeDtypeStruct((2, 64, 102...  95 us
    pallas_call x1, Pallas kernels, gather_all(): pl.pallas_call(gather_kernel, out_shape=shapes, in_specs=[any_spec, any_s...  94.8 us
    pallas_call x1, Pallas kernels, middle(): pl.pallas_call(middle_kernel, out_shape=[jax.ShapeDtypeStruct((128, 1024)...  76 us
    pallas_call x1, Pallas kernels, attend_back(): pl.pallas_call(attend_back_kernel, out_shape=[jax.ShapeDtypeStruct((n, 10...  31.6 us
    pallas_call x1, Pallas kernels, attend(): pl.pallas_call(attend_kernel, out_shape=[jax.ShapeDtypeStruct((n, 64), bf...  21.3 us
    unnamed x20, local copies, waits for them, and re-layouts  10.1 us

profile of v1, /device:TPU:0, one launch (start us, length us, event | category | flops | bytes accessed | tf_op | source)
XLA Modules:
  0.0 340.3 jit_solution(5993777835739703799)
XLA Ops:
  0.7 0.8 maximum_convert_fusion
  1.5 0.7 convert_element_type.36
  2.3 0.7 convert_element_type.38
  3.7 1.4 copy.38.bias
  5.1 94.8 %gather_all.1 = (bf16[32,64,1024]{2,1,0:T(8,128)(2,1)}, bf16[2,8,2,32,192]{4,3,2,1,0:T(8,128)(2,1)}, bf16[2,2,4,2,2,32,512]{6,5,4,3,2,1,0:T(8,128)(2,1)}, bf16[2...) custom-call(bf16[2,64,1024]{2,1,0:T(8,128)(2,1)} %tok.3, ...), custom_call_target="tpu_custom_call" | custom-call | tf_op jit(solution)/shard_map/gather_all/pallas_call | solution.py:640
  99.9 0.9 slice.40
  100.8 1.0 constant_dynamic-slice_fusion.1
  101.8 0.7 reshape.173.rows_ref
  103.5 0.7 slice.34.gain_ref
  104.1 0.7 slice.32.gain_ref
  104.8 0.7 jit_solution_.3.freq_ref
  105.5 21.3 %attend.1 = (bf16[2048,64]{1,0:T(8,128)(2,1)}, f32[2048,128]{1,0:T(8,128)}, bf16[2048,128]{1,0:T(8,128)(2,1)}, bf16[2048,128]{1,0:T(8,128)(2,1)}, bf16[2048,128]...) custom-call(s32[2,8]{1,0:T(2,128)} %lengths.3, f32[16,2]{1,0:T(8,128)} %copy.38.bias, ...), custom_call_target="tpu_custom_call" | custom-call | tf_op jit(solution)/shard_map/attend/pallas_call | solution.py:808
  126.8 76.0 %middle.1 = (bf16[128,1024]{1,0:T(8,128)(2,1)}, bf16[16,2,64,64]{3,2,1,0:T(8,128)(2,1)}, f32[128,1024]{1,0:T(8,128)}, bf16[2,1024,512]{2,1,0:T(8,128)(2,1)}, bf1...) custom-call(bf16[16,2,64,64]{3,2,1,0:T(8,128)(2,1)} %bitcast.55, ...), custom_call_target="tpu_custom_call" | custom-call | tf_op jit(solution)/shard_map/middle/pallas_call | solution.py:1140
  202.8 31.6 %attend_back.1 = (bf16[2048,1024]{1,0:T(8,128)(2,1)}, bf16[1024,192]{1,0:T(8,128)(2,1)}, f32[8,1024]{1,0:T(8,128)}) custom-call(s32[2,8]{1,0:T(2,128)} %lengths.3, bf16[2048,1024]{1,0:T(8,128)(2,1)} %bitcast.38, bf16[1024,192]{1,0:T(8,128)(2,1)} %bitcast.44, bf16[2048,64]{1,0:T(8,128)(2,1)} %bitcast.54, f32[2048,128]{1,0:T(8,128)} %get-tuple-element.53.o_ref, ...), custom_call_target="tpu_custom_call" | custom-call | tf_op jit(solution)/shard_map/attend_back/pallas_call | solution.py:948
  234.4 95.0 %reduce_all.1 = (bf16[2,64,1024]{2,1,0:T(8,128)(2,1)}, f32[32,3072]{1,0:T(8,128)}, f32[32,1024]{1,0:T(8,128)}, f32[32,4096]{1,0:T(8,128)}, f32[32,4096]{1,0:T(8,...) custom-call(bf16[2,8,2,64,1024]{4,3,2,1,0:T(8,128)(2,1)} %bitcast.39, bf16[2,8,2,32,192]{4,3,2,1,0:T(8,128)(2,1)} %bitcast.53, ...), custom_call_target="tpu_custom_call" | custom-call | tf_op jit(solution)/shard_map/reduce_all/pallas_call | solution.py:1379
  329.4 0.8 slice_reduce_fusion.2
  330.2 0.7 constant_dynamic-slice_fusion
  332.2 0.7 copy.51
  332.9 1.7 copy.52
  334.6 1.8 copy.53
  336.4 1.6 copy.54
  337.9 0.8 copy.55
  338.7 0.8 copy.56
  339.5 0.8 copy.57
  (25 shorter events, 3.1 us)
Async XLA Ops:
  0.6 104.2 %copy-start.4 = (f32[32]{0:T(128)S(1)}, f32[32]{0:T(128)}, u32[]{:S(2)}) copy-start(f32[32]{0:T(128)} %constant.46.clone) | copy-start | bytes 388
  234.4 97.9 %copy-start.3 = (bf16[128,1024]{1,0:T(8,128)(2,1)S(1)}, bf16[128,1024]{1,0:T(8,128)(2,1)}, u32[]{:S(2)}) copy-start(bf16[128,1024]{1,0:T(8,128)(2,1)} %get-tuple-element.51) | copy-start | bytes 786436
  329.4 8.5 %copy-start.2 = (f32[32,4096]{1,0:T(8,128)S(1)}, f32[32,4096]{1,0:T(8,128)}, u32[]{:S(2)}) copy-start(f32[32,4096]{1,0:T(8,128)} %get-tuple-element.132) | copy-start | bytes 1572868
  329.4 9.3 %copy-start.1 = (f32[32,4096]{1,0:T(8,128)S(1)}, f32[32,4096]{1,0:T(8,128)}, u32[]{:S(2)}) copy-start(f32[32,4096]{1,0:T(8,128)} %get-tuple-element.133) | copy-start | bytes 1572868
  332.2 7.3 %copy-start = (f32[128,1024]{1,0:T(8,128)S(1)}, f32[128,1024]{1,0:T(8,128)}, u32[]{:S(2)}) copy-start(f32[128,1024]{1,0:T(8,128)} %get-tuple-element.134) | copy-start | bytes 1572868

commit v2 on v0

--- a/solution.py
+++ b/solution.py
@@ -1,8 +1,12 @@
 import math
+from types import SimpleNamespace
 
 import jax
 import jax.numpy as jnp
+import numpy as np
 from jax import lax
+from jax.experimental import pallas as pl
+from jax.experimental.pallas import tpu as pltpu
 from jax.sharding import PartitionSpec as P
 
 EPS = 1e-06
@@ -383,40 +387,1065 @@
     )
 
 
+AXES = ("zh", "zl", "x", "y", "c")
+CHIPS = ("zl", "x", "y")
+VMEM_BYTES = 62 * 2**20
+ROW_BLOCK = 256
+SPAN = 512
+LAST = (((1,), (1,)), ((), ()))
+FIRST = (((0,), (0,)), ((), ()))
+CHIP_FLIPS = [
+    tuple(a for a, bit in zip(CHIPS, ((m >> 2) & 1, (m >> 1) & 1, m & 1)) if bit)
+    for m in range(1, 8)
+]
+GROUP_FLIPS = [("zl",), ("x",), ("zl", "x")]
+
+
+class Net:
+    def __init__(self, send_sems, recv_sems, local_sems):
+        self.me = {name: lax.axis_index(name) for name in AXES}
+        self.send_sems, self.recv_sems, self.local_sems = send_sems, recv_sems, local_sems
+        self.used = 0
+        self.local_used = 0
+        self.open = []
+
+    def target(self, flips):
+        return tuple(1 - self.me[a] if a in flips else self.me[a] for a in AXES)
+
+    def index(self, names, flips=()):
+        total = 0
+        for a in names:
+            total = total * 2 + (1 - self.me[a] if a in flips else self.me[a])
+        return total
+
+    def barrier(self, partners):
+        sem = pltpu.get_barrier_semaphore()
+        for flips in partners:
+            pl.semaphore_signal(
+                sem, inc=1, device_id=self.target(flips), device_id_type=pl.DeviceIdType.MESH
+            )
+        pl.semaphore_wait(sem, len(partners))
+
+    def send(self, source, dest, flips):
+        copy = pltpu.make_async_remote_copy(
+            src_ref=source,
+            dst_ref=dest,
+            send_sem=self.send_sems.at[self.used],
+            recv_sem=self.recv_sems.at[self.used],
+            device_id=self.target(flips),
+            device_id_type=pl.DeviceIdType.MESH,
+        )
+        self.used += 1
+        copy.start()
+        self.open.append(copy)
+        return copy
+
+    def local(self, source, dest):
+        copy = pltpu.make_async_copy(source, dest, self.local_sems.at[self.local_used])
+        self.local_used += 1
+        copy.start()
+        return copy
+
+    def drain(self):
+        for copy in self.open:
+            copy.wait_send()
+        self.open = []
+
+
+class Gather:
+    def __init__(self, net, region, dims):
+        self.net, self.region, self.dims = net, region, dims
+        self.arrive = {}
+        self.sibling = {}
+
+    def key(self, flips):
+        return tuple(sorted(flips))
+
+    def push(self, flips, source=None):
+        source = self.region(flips) if source is None else source
+        level = max([self.dims.index(a) for a in flips], default=-1)
+        for d in self.dims[level + 1 :]:
+            copy = self.net.send(source, self.region(flips), (d,))
+            self.arrive[self.key(flips + (d,))] = copy
+        self.sibling[self.key(flips)] = self.net.send(source, self.region(flips), ("c",))
+
+    def take(self, *flips):
+        self.arrive[self.key(flips)].wait_recv()
+        self.push(flips)
+
+    def ready(self, *flips):
+        self.sibling[self.key(flips)].wait_recv()
+
+
+class Reduce:
+    def __init__(self, net, dims, part, land, send, arrive):
+        self.net, self.dims = net, dims
+        self.part, self.land, self.send_slot, self.arrive = part, land, send, arrive
+        self.from_sibling, self.incoming = {}, {}
+        a, b, d = dims
+        self.masks = [(a, b, d), (a, b), (a, d), (a,), (b, d), (b,), (d,), ()]
+        self.slots = {}
+        for rest in [(b, d), (b,), (d,), ()]:
+            self.slots[rest, a] = len(self.slots)
+        for rest in [(d,), ()]:
+            self.slots[rest, b] = len(self.slots)
+        self.slots[(), d] = len(self.slots)
+
+    def ordered(self, flips):
+        return tuple(a for a in self.dims if a in flips)
+
+    def begin(self, flips):
+        mask = self.ordered(flips)
+        self.from_sibling[mask] = self.net.send(
+            self.part(mask, 1 - self.net.me["c"]), self.land(self.masks.index(mask)), ("c",)
+        )
+
+    def total(self, mask, before):
+        value = self.part(mask, self.net.me["c"])[...].astype(jnp.float32)
+        value = value + self.land(self.masks.index(mask))[...].astype(jnp.float32)
+        for stage in before:
+            value = value + self.arrive(self.slots[mask, stage])[...].astype(jnp.float32)
+        return value
+
+    def settle(self, mask, before):
+        self.from_sibling[mask].wait_recv()
+        for stage in before:
+            self.incoming[mask, stage].wait_recv()
+        return self.total(mask, before)
+
+    def forward(self, flips):
+        mask = self.ordered(flips)
+        stage, rest = mask[0], mask[1:]
+        value = self.settle(mask, self.dims[: self.dims.index(stage)])
+        slot = self.slots[rest, stage]
+        self.send_slot(slot)[...] = value.astype(jnp.bfloat16)
+        self.incoming[rest, stage] = self.net.send(
+            self.send_slot(slot), self.arrive(slot), (stage,)
+        )
+
+    def result(self):
+        return self.settle((), self.dims)
+
+
+def lane_iota(rows, lanes=128):
+    return lax.broadcasted_iota(jnp.int32, (rows, lanes), 1)
+
+
+def pieces(value):
+    first = value.astype(jnp.bfloat16).astype(jnp.float32)
+    second = (value - first).astype(jnp.bfloat16).astype(jnp.float32)
+    return first, second, value - first - second
+
+
+def swap_halves(values):
+    lane = lane_iota(values.shape[0])
+    return jnp.where(lane % 64 < 32, pltpu.roll(values, 96, 1), pltpu.roll(values, 32, 1))
+
+
+def pair_mean(values):
+    lane = lane_iota(values.shape[0])
+    low = jnp.sum(jnp.where(lane < 64, values, 0.0), axis=1, keepdims=True)
+    high = jnp.sum(jnp.where(lane < 64, 0.0, values), axis=1, keepdims=True)
+    return jnp.where(lane < 64, low, high) * (1.0 / 64.0)
+
+
+def angles_of(packed):
+    lane = lane_iota(packed.shape[0])
+    turned = pltpu.roll(packed, 64, 1)
+    return jnp.where(lane < 64, packed, turned), jnp.where(lane < 64, turned, packed)
+
+
+def row_scale(value):
+    return lax.rsqrt(jnp.mean(value * value, axis=1, keepdims=True) + EPS)
+
+
+def layer_inputs():
+    return ["lengths", "bias", "tok", "cot", "wqkv", "wout", "wgate", "wup", "wdown"] + [
+        "gains", "variate", "times", "freq",
+    ]
+
+
+def layer_outputs():
+    bf, f32 = jnp.bfloat16, jnp.float32
+    return {
+        "out": ((128, 1024), bf),
+        "gtok": ((2, 64, 1024), bf),
+        "gwqkv": ((32, 3072), f32),
+        "gwout": ((32, 1024), f32),
+        "gwgate": ((32, 4096), f32),
+        "gwup": ((32, 4096), f32),
+        "gwdown": ((128, 1024), f32),
+        "gsmall": ((8, 8, 128), f32),
+    }
+
+
+def layer_scratch():
+    bf, f32 = jnp.bfloat16, jnp.float32
+    return {
+        "x": ((32, 64, 1024), bf),
+        "wp": ((8, 2, 32, 192), bf),
+        "wl": ((8, 2, 32, 192), bf),
+        "wh": ((2, 8, 2, 32, 192), bf),
+        "gp": ((4, 2, 2, 32, 512), bf),
+        "gl": ((4, 2, 2, 32, 512), bf),
+        "wgu": ((2, 2, 4, 2, 2, 32, 512), bf),
+        "wd": ((2, 2, 128, 1024), bf),
+        "wo": ((2, 16, 32, 1024), bf),
+        "gf": ((8, 2, 64, 1024), bf),
+        "tile": ((8, 128), f32),
+        "sm": ((2, 2, 2, 2, 2, 8, 128), f32),
+        "gain_s": ((4, 8, 128), f32),
+        "feat": ((2048, 128), f32),
+        "cs": ((2048, 128), f32),
+        "raw": ((2048, 128), f32),
+        "kept_o": ((2048, 128), f32),
+        "qf": ((2048, 128), bf),
+        "kf": ((2048, 128), bf),
+        "vf": ((2048, 128), bf),
+        "att": ((16, 2, 64, 64), bf),
+        "lb": ((16, 64, 64), bf),
+        "ap": ((2, 8, 64, 128), bf),
+        "at2": ((8, 2, 64, 128), bf),
+        "at3": ((8, 64, 128), bf),
+        "att_s": ((128, 1024), bf),
+        "resid": ((128, 1024), f32),
+        "n2": ((8, 2, 64, 1024), bf),
+        "gh": ((4, 256, 512), f32),
+        "hid": ((4, 256, 512), bf),
+        "ggu": ((2, 4, 256, 512), bf),
+        "kept": ((8, 128, 1024), f32),
+        "sent": ((8, 2, 64, 1024), bf),
+        "landed": ((8, 2, 64, 1024), bf),
+        "red_send": ((2, 3, 128, 1024), bf),
+        "red_land": ((2, 3, 128, 1024), bf),
+        "ga3": ((2, 8, 64, 128), bf),
+        "ga2": ((2, 8, 64, 128), bf),
+        "ag1": ((2, 8, 64, 128), bf),
+        "gatt": ((16, 2, 64, 64), bf),
+        "gwgu": ((2, 2, 4, 2, 64, 512), bf),
+        "gwd": ((2, 2, 128, 1024), bf),
+        "gwo": ((2, 8, 2, 32, 1024), bf),
+        "gb": ((2048, 128), bf),
+        "gq": ((2048, 128), bf),
+        "gw": ((2, 8, 2, 32, 192), bf),
+        "bias_s": ((8, 128), f32),
+        "sums": ((8, 1024), f32),
+        "n_half": ((64, 1024), bf),
+        "n_half_land": ((64, 1024), bf),
+        "o_arr": ((7, 2, 32, 1024), bf),
+        "o_half": ((32, 1024), bf),
+        "o_half_land": ((32, 1024), bf),
+        "y_wgu": ((2, 2, 4, 64, 512), bf),
+        "y_wd": ((2, 128, 1024), bf),
+        "h_wgu": ((2, 4, 64, 512), bf),
+        "h_wd": ((128, 1024), bf),
+        "h_wgu_land": ((2, 4, 64, 512), bf),
+        "h_wd_land": ((128, 1024), bf),
+        "f2": ((2, 4, 2, 32, 512), bf),
+        "w_land": ((8, 2, 32, 192), bf),
+        "w_t": ((8, 2, 32, 192), bf),
+        "s_acc": ((5, 8, 8, 128), f32),
+        "s_land": ((5, 8, 8, 128), f32),
+    }
+
+
+N_COPIES = 232
+
+
+def layer_kernel(*refs):
+    names = layer_inputs() + list(layer_outputs()) + list(layer_scratch())
+    r = SimpleNamespace(**dict(zip(names, refs)))
+    send_sems, recv_sems, local_sems = refs[len(names) :]
+    bf, f32 = jnp.bfloat16, jnp.float32
+    net = Net(send_sems, recv_sems, local_sems)
+    zh, zl, x, y, c = (net.me[a] for a in AXES)
+    mine, in_half = net.index(AXES), net.index(AXES[1:])
+    my_chip, my_pair = net.index(CHIPS), net.index(("zl", "x"))
+    head = in_half
+    net.barrier(CHIP_FLIPS + [("c",), ("zh",)])
+
+    def x_region(part):
+        def region(flips):
+            return r.x.at[(zh if part == 0 else 1 - zh) * 16 + net.index(AXES[1:], flips)]
+
+        return region
+
+    x_own = Gather(net, x_region(0), ("zl", "y", "x"))
+    x_far = Gather(net, x_region(1), ("zl", "x", "y"))
+    wo_tree = Gather(net, lambda f: r.wo.at[:, net.index(AXES[1:], f)], ("y", "zl", "x"))
+    gf_tree = Gather(net, lambda f: r.gf.at[net.index(("zl", "x", "c"), f)], ("zl", "x"))
+    swap = net.send(r.tok.at[1 - zh], r.x.at[mine], ("zh",))
+    x_own.push((), r.tok.at[zh])
+    r.tile[...] = jnp.zeros_like(r.tile)
+    r.tile[0:2, 0:64] = r.variate[...].astype(f32)
+    r.tile[2:4, 0:64] = r.times[...].astype(f32)
+    r.tile[4:5, :] = r.gains[...]
+    sm_step = net.send(r.tile, r.sm.at[zh, zl, x, y, c], ("zh",))
+    for h in range(16):
+        r.wp[h // 2, h % 2] = r.wqkv[:, 192 * h : 192 * (h + 1)]
+    w_arrive = []
+    for flips in CHIP_FLIPS:
+        w_arrive.append(net.send(r.wp.at[net.index(CHIPS, flips)], r.wl.at[my_chip], flips))
+    r.x[mine] = r.tok[zh]
+    r.sm[zh, zl, x, y, c] = r.tile[...]
+    r.wl[my_chip] = r.wp[my_chip]
+    for pair in range(4):
+        for cc in range(2):
+            for part in range(4):
+                idx = (part // 2) * 16 + pair * 4 + (part % 2) * 2 + cc
+                col, lane = 128 * idx, 128 * part
+                r.gp[pair, 0, cc, :, lane : lane + 128] = r.wgate[:, col : col + 128]
+                r.gp[pair, 1, cc, :, lane : lane + 128] = r.wup[:, col : col + 128]
+    g_arrive = []
+    for flips in GROUP_FLIPS:
+        g_arrive.append(
+            net.send(r.gp.at[net.index(("zl", "x"), flips)], r.gl.at[my_pair], flips)
+        )
+    r.gl[my_pair] = r.gp[my_pair]
+    r.gf[net.index(("zl", "x", "c"))] = r.cot[...]
+    r.wd[zh, y] = r.wdown[...]
+    r.wo[zh, in_half] = r.wout[...]
+    wo_zh = net.send(r.wout, r.wo.at[zh, in_half], ("zh",))
+
+    sm_step.wait_recv()
+    sm_step = net.send(r.sm.at[:, zl, x, y, c], r.sm.at[:, zl, x, y, c], ("c",))
+    x_own.take("zl")
+    x_own.take("y")
+    sm_step.wait_recv()
+    sm_step = net.send(r.sm.at[:, zl, x, y], r.sm.at[:, zl, x, y], ("y",))
+    for copy in w_arrive:
+        copy.wait_recv()
+    w_c = net.send(r.wl.at[:, 1 - c], r.wh.at[zh, :, c], ("c",))
+    r.wh[zh, :, c] = r.wl[:, c]
+    swap.wait_recv()
+    x_far.push(())
+    sm_step.wait_recv()
+    sm_step = net.send(r.sm.at[:, zl, x], r.sm.at[:, zl, x], ("zl",))
+    x_own.take("zl", "y")
+    w_c.wait_recv()
+    w_zh = net.send(r.wh.at[zh], r.wh.at[zh], ("zh",))
+    x_far.take("zl")
+    sm_step.wait_recv()
+    sm_step = net.send(r.sm.at[:, :, x], r.sm.at[:, :, x], ("x",))
+    for copy in g_arrive:
+        copy.wait_recv()
+    g_c = []
+    for k in range(2):
+        g_c.append(net.send(r.gl.at[:, k, 1 - c], r.wgu.at[k, zh, :, y, c], ("c",)))
+        r.wgu[k, zh, :, y, c] = r.gl[:, k, c]
+    x_own.take("x")
+    x_own.take("zl", "x")
+    x_far.take("x")
+    x_far.take("zl", "x")
+
+    def g_piece(k, half):
+        return r.wgu.at[k // 2, half, pl.ds(2 * (k % 2), 2), y]
+
+    g_zh, g_y, g_fwd = [], [], []
+    for k in range(4):
+        if k % 2 == 0:
+            g_c[k // 2].wait_recv()
+        g_zh.append(net.send(g_piece(k, zh), g_piece(k, zh), ("zh",)))
+    wd_zh = net.send(r.wdown, r.wd.at[zh, y], ("zh",))
+    x_own.take("y", "x")
+    x_far.take("y")
+    sm_step.wait_recv()
+
+    lane8 = lane_iota(8)
+    for group in range(8):
+        for which in range(4):
+            row = jnp.zeros((8, 128), f32)
+            for j in range(4):
+                block = 4 * group + j
+                held = r.sm[
+                    block // 16, (block // 8) % 2, (block // 4) % 2, (block // 2) % 2, block % 2
+                ]
+                moved = held if j == which else pltpu.roll(held, (32 * (j - which)) % 128, 1)
+                row = jnp.where(lane8 // 32 == j, moved, row)
+            r.gain_s[which, group : group + 1] = row[4:5, :]
+    gain_attn = jnp.concatenate([r.gain_s[0, k : k + 1] for k in range(8)], axis=1)
+    gain_ffn = jnp.concatenate([r.gain_s[1, k : k + 1] for k in range(8)], axis=1)
+    held_q = r.gain_s[2, pl.ds(my_chip, 1)]
+    held_k = r.gain_s[3, pl.ds(my_chip, 1)]
+    wide_q, wide_k = jnp.broadcast_to(held_q, (8, 128)), jnp.broadcast_to(held_k, (8, 128))
+    wide_q = jnp.where(c == 0, wide_q, pltpu.roll(wide_q, 64, 1))
+    wide_k = jnp.where(c == 0, pltpu.roll(wide_k, 64, 1), wide_k)
+    qk_gain = jnp.where(lane8 < 64, wide_q, wide_k)[0:1, :]
+
+    starts, ends, total = [], [], jnp.int32(0)
+    for j in range(8):
+        starts.append(total)
+        total = total + r.lengths[zh, j]
+        ends.append(total)
+    sub = lax.broadcasted_iota(jnp.int32, (8, 128), 0)
+    start_col = jnp.zeros((8, 128), jnp.int32)
+    end_col = jnp.zeros((8, 128), jnp.int32)
+    for j in range(8):
+        start_col = jnp.where(sub == j, starts[j], start_col)
+        end_col = jnp.where(sub == j, ends[j], end_col)
+    same_bias = jnp.full((8, 128), r.bias[head, 0], f32)
+    other_bias = jnp.full((8, 128), r.bias[head, 1], f32)
+    diff_parts = pieces(same_bias - other_bias)
+    zero = jnp.zeros((8, 128), f32)
+    const_q = jnp.where(sub == 0, -256.0, 0.0)
+    for i, part in enumerate(pieces(other_bias)):
+        const_q = jnp.where(sub == i + 1, part, const_q)
+    const_k = jnp.where(sub < 4, 1.0, 0.0)
+    ones_k = jnp.where(sub < 3, 1.0, 0.0)
+
+    @pl.loop(0, 16)
+    def _(i):
+        col = pl.ds(pl.multiple_of(i * 128, 128), 128)
+        low = r.sm[i // 8, (i // 4) % 2, (i // 2) % 2, i % 2, 0]
+        high = r.sm[i // 8, (i // 4) % 2, (i // 2) % 2, i % 2, 1]
+        both = jnp.where(lane8 < 64, low, pltpu.roll(high, 64, 1))
+        var_row = jnp.where(zh == 0, both[0:1, :], both[1:2, :])
+        time_row = jnp.where(zh == 0, both[2:3, :], both[3:4, :])
+        pos = lane8 + i * 128
+        doc = jnp.where((pos >= start_col) & (pos < end_col), 1.0, 0.0)
+        var = jnp.where(jnp.broadcast_to(var_row, (8, 128)) == sub.astype(f32), 1.0, 0.0)
+        rows = [doc * 256.0, const_q] + [var * part for part in diff_parts] + [zero, zero, zero]
+        rows += [doc, const_k, var, var, var, ones_k, zero, zero]
+        r.feat[col, :] = jnp.concatenate(rows, axis=0).T
+        angle = jnp.broadcast_to(time_row, (32, 128)) * r.freq[...]
+        cosine, sine = jnp.cos(angle), jnp.sin(angle)
+        r.cs[col, :] = jnp.concatenate([cosine, cosine, -sine, sine], axis=0).T
+
+    x_own.take("zl", "y", "x")
+    x_far.take("zl", "y")
+    x_far.take("x", "y")
+    x_far.take("zl", "x", "y")
+    for k in range(4):
+        g_y.append(net.send(g_piece(k, zh), g_piece(k, zh), ("y",)))
+    gf_tree.push((), r.cot)
+    wd_y = net.send(r.wdown, r.wd.at[zh, y], ("y",))
+    w_zh.wait_recv()
+
+    lane = lane_iota(ROW_BLOCK)
+
+    def rows_at(part, flips):
+        z_part = zh if part == 0 else 1 - zh
+        start = ((z_part * 2 + net.index(("zl",), flips)) * 2 + net.index(("x",), flips)) * ROW_BLOCK
+        return pl.ds(pl.multiple_of(start, ROW_BLOCK), ROW_BLOCK), pl.ds(start // 64, 4)
+
+    def project(part, flips):
+        tree = x_own if part == 0 else x_far
+        tree.ready(*flips)
+        tree.ready(*(flips + ("y",)))
+        row, blocks = rows_at(part, flips)
+        value = r.x[blocks].reshape(ROW_BLOCK, 1024).astype(f32)
+        normed = (value * row_scale(value) * gain_attn).astype(bf)
+        qkv = jnp.dot(normed, r.wh[...].reshape(1024, 192), preferred_element_type=f32)
+        raw = qkv[:, :128]
+        r.raw[row, :] = raw
+        scaled = raw * lax.rsqrt(pair_mean(raw * raw) + EPS) * qk_gain
+        cosine, sine = angles_of(r.cs[row, :])
+        turned = (scaled * cosine + swap_halves(scaled) * sine).astype(bf).astype(f32)
+        marks = r.feat[row, :]
+        r.qf[row, :] = jnp.where(lane < 64, turned * 0.125, pltpu.roll(marks, 64, 1)).astype(bf)
+        r.kf[row, :] = jnp.where(lane < 64, pltpu.roll(turned, 64, 1), marks).astype(bf)
+        third = jnp.concatenate([qkv[:, 128:192], jnp.zeros((ROW_BLOCK, 64), f32)], axis=1)
+        r.vf[row, :] = jnp.where((lane >= 64) & (lane < 67), 1.0, third).astype(bf)
+
+    project(0, ())
+    project(0, ("zl",))
+    wo_zh.wait_recv()
+    wo_tree.push(())
+    project(1, ())
+    project(1, ("zl",))
+    gf_tree.take("zl")
+    project(0, ("x",))
+    project(0, ("zl", "x"))
+    wo_tree.take("y")
+    project(1, ("x",))
+    project(1, ("zl", "x"))
+    wo_tree.take("zl")
+    wo_tree.take("zl", "y")
+
+    lane_span = lane_iota(SPAN)
+
+    def attend(i):
+        row = pl.ds(i * SPAN, SPAN)
+        query = r.qf[row, :]
+
+        def one_chunk(k, total):
+            col = pl.ds(pl.multiple_of(k * SPAN, SPAN), SPAN)
+            scores = lax.dot_general(query, r.kf[col, :], LAST, preferred_element_type=f32)
+            weights = jnp.exp(scores).astype(bf)
+            return total + jnp.dot(weights, r.vf[col, :], preferred_element_type=f32)
+
+        total = lax.fori_loop(0, 2048 // SPAN, one_chunk, jnp.zeros((SPAN, 128), f32))
+        weight = total[:, 64:65]
+        result = total / weight
+        r.kept_o[row, :] = jnp.where(lane_span < 64, result, jnp.log(weight))
+        r.att[4 * i : 4 * i + 4] = result[:, :64].astype(bf).reshape(4, 2, 64, 64)
+
+    def g_pass(k):
+        g_zh[k].wait_recv()
+        g_fwd.append(net.send(g_piece(k, 1 - zh), g_piece(k, 1 - zh), ("y",)))
+
+    attend(0)
+    gf_tree.take("x")
+    gf_tree.take("zl", "x")
+    g_pass(0)
+    attend(1)
+    wo_tree.take("x")
+    wo_tree.take("y", "x")
+    g_pass(1)
+    attend(2)
+    wo_tree.take("zl", "x")
+    wo_tree.take("zl", "y", "x")
+    g_pass(2)
+    attend(3)
+
+    step = net.send(r.att.at[:, 1 - c], r.lb, ("c",))
+    g_pass(3)
+    wd_zh.wait_recv()
+    wd_fwd = net.send(r.wd.at[1 - zh, y], r.wd.at[1 - zh, y], ("y",))
+    step.wait_recv()
+    lane64 = lane_iota(64)
+
+    @pl.loop(0, 16)
+    def _(i):
+        own = jnp.concatenate([r.att[i, c]] * 2, axis=1)
+        other = jnp.concatenate([r.lb[i]] * 2, axis=1)
+        r.ap[i // 8, i % 8] = jnp.where((lane64 < 64) == (c == 0), own, other)
+
+    arrive = []
+    for flips in CHIP_FLIPS:
+        arrive.append(
+            net.send(r.ap.at[:, net.index(CHIPS, flips)], r.at2.at[my_chip], flips)
+        )
+    r.at2[my_chip] = r.ap[:, my_chip]
+    def w_down():
+        return r.wd[...].reshape(512, 1024)
+
+    def w_o():
+        return r.wo[...].reshape(1024, 1024)
+
+    def w_in(k):
+        return r.wgu[k].reshape(1024, 512)
+
+    gf_tree.ready()
+    gf_tree.ready("zl")
+    gf_tree.ready("x")
+    gf_tree.ready("zl", "x")
+    wd_y.wait_recv()
+    wd_fwd.wait_recv()
+    for p in range(2):
+        rows = r.gf[2 * p : 2 * p + 2].reshape(256, 1024)
+        r.gh[p] = lax.dot_general(rows, w_down(), LAST, preferred_element_type=f32)
+    for copy in arrive:
+        copy.wait_recv()
+    step = net.send(r.at2.at[:, 1 - zh], r.at3, ("zh",))
+    for p in range(2, 4):
+        rows = r.gf[2 * p : 2 * p + 2].reshape(256, 1024)
+        r.gh[p] = lax.dot_general(rows, w_down(), LAST, preferred_element_type=f32)
+    for k in range(8):
+        r.att_s[pl.ds(pl.multiple_of(zh * 64, 64), 64), 128 * k : 128 * (k + 1)] = r.at2[k, zh]
+    for flips in [(), ("y",), ("zl",), ("zl", "y"), ("x",), ("y", "x"), ("zl", "x"), ("zl", "y", "x")]:
+        wo_tree.ready(*flips)
+    step.wait_recv()
+    for k in range(8):
+        r.att_s[pl.ds(pl.multiple_of(64 - zh * 64, 64), 64), 128 * k : 128 * (k + 1)] = r.at3[k]
+
+    resid = r.tok[...].reshape(128, 1024).astype(f32)
+    resid = resid + jnp.dot(r.att_s[...], w_o(), preferred_element_type=f32)
+    scale = row_scale(resid)
+    r.resid[...] = resid
+    mine8 = 2 * my_pair + c
+    r.n2[mine8] = (resid * scale * gain_ffn).astype(bf).reshape(2, 64, 1024)
+    to_sibling = [net.send(r.n2.at[mine8], r.n2.at[mine8], ("c",))]
+    from_chips = [net.send(r.n2.at[mine8], r.n2.at[mine8], flips) for flips in GROUP_FLIPS]
+    for copy in g_y + g_fwd:
+        copy.wait_recv()
+
+    def pair_rows(ref, pair):
+        return ref[pl.ds(2 * pair, 2)].reshape(256, 1024)
+
+    def feed(pair):
+        rows = pair_rows(r.n2, pair)
+        gate = jnp.dot(rows, w_in(0), preferred_element_type=f32)
+        up = jnp.dot(rows, w_in(1), preferred_element_type=f32)
+        sig = 1.0 / (1.0 + jnp.exp(-gate))
+        silu = gate * sig
+        r.hid[pair] = (silu * up).astype(bf)
+        back = r.gh[pair]
+        r.ggu[0, pair] = (back * up * sig * (1.0 + gate * (1.0 - sig))).astype(bf)
+        r.ggu[1, pair] = (back * silu).astype(bf)
+
+    def back_product(pair):
+        total = lax.dot_general(r.ggu[0, pair], w_in(0), LAST, preferred_element_type=f32)
+        return total + lax.dot_general(r.ggu[1, pair], w_in(1), LAST, preferred_element_type=f32)
+
+    def out_product(pair):
+        return jnp.dot(r.hid[pair], w_down(), preferred_element_type=f32)
+
+    halves, reduced = {}, {0: [], 1: []}
+
+    def share(kind, slot, value):
+        at = 4 * kind + slot
+        r.kept[at] = jnp.where(c == 0, value[:128], value[128:])
+        r.sent[at] = jnp.where(c == 0, value[128:], value[:128]).astype(bf).reshape(2, 64, 1024)
+        halves[at] = net.send(r.sent.at[at], r.landed.at[at], ("c",))
+
+    def finish_half(kind, slot):
+        at = 4 * kind + slot
+        halves[at].wait_recv()
+        total = r.kept[at] + r.landed[at].reshape(128, 1024).astype(f32)
+        if slot == 0:
+            r.kept[at] = total
+        else:
+            r.red_send[kind, slot - 1] = total.astype(bf)
+            reduced[kind].append(
+                net.send(
+                    r.red_send.at[kind, slot - 1],
+                    r.red_land.at[kind, slot - 1],
+                    GROUP_FLIPS[slot - 1],
+                )
+            )
+
+    pairs = [my_pair] + [net.index(("zl", "x"), flips) for flips in GROUP_FLIPS]
+    to_sibling[0].wait_recv()
+    feed(pairs[0])
+    for k in range(3):
+        from_chips[k].wait_recv()
+        to_sibling.append(
+            net.send(r.n2.at[2 * pairs[k + 1] + c], r.n2.at[2 * pairs[k + 1] + c], ("c",))
+        )
+    for k in range(3):
+        to_sibling[k + 1].wait_recv()
+        feed(pairs[k + 1])
+        share(0, k + 1, back_product(pairs[k + 1]))
+        if k > 0:
+            finish_half(0, k)
+    finish_half(0, 3)
+    share(0, 0, back_product(pairs[0]))
+    for k in (1, 2, 3):
+        share(1, k, out_product(pairs[k]))
+        if k > 1:
+            finish_half(1, k - 1)
+    finish_half(0, 0)
+    finish_half(1, 3)
+    for k in range(2):
+        r.gwgu[k] = (
+            lax.dot_general(
+                r.n2[...].reshape(1024, 1024),
+                r.ggu[k].reshape(1024, 512),
+                FIRST,
+                preferred_element_type=f32,
+            )
+            .astype(bf)
+            .reshape(2, 4, 2, 64, 512)
+        )
+    y_far = [net.send(r.gwgu.at[k, 1 - zh, :, 1 - y], r.y_wgu.at[k, 1], ("y",)) for k in range(2)]
+    share(1, 0, out_product(pairs[0]))
+    net.drain()
+
+    for copy in reduced[0]:
+        copy.wait_recv()
+    total = r.kept[0]
+    for k in range(3):
+        total = total + r.red_land[0, k].astype(f32)
+    resid = r.resid[...]
+    scale = row_scale(resid)
+    r.sums[...] = jnp.zeros_like(r.sums)
+    r.sums[1:2, :] = jnp.sum(total * resid * scale, axis=0, keepdims=True)
+    weighted = total * gain_ffn
+    mean = jnp.mean(weighted * resid, axis=1, keepdims=True)
+    grad_resid = r.cot[...].reshape(128, 1024).astype(f32) + scale * weighted
+    grad_resid = grad_resid - resid * (scale * scale * scale) * mean
+    r.kept[7] = grad_resid
+    branch = grad_resid.astype(bf)
+    grad_att = lax.dot_general(branch, w_o(), LAST, preferred_element_type=f32).astype(bf)
+    for k in range(8):
+        for b in range(2):
+            r.ga3[b, k] = grad_att[64 * b : 64 * (b + 1), 128 * k : 128 * (k + 1)]
+    step = net.send(r.ga3.at[1 - zh], r.ga2.at[zh], ("zh",))
+    r.ga2[zh] = r.ga3[zh]
+    finish_half(1, 0)
+    r.gwo[...] = (
+        lax.dot_general(r.att_s[...], branch, FIRST, preferred_element_type=f32)
+        .astype(bf)
+        .reshape(2, 8, 2, 32, 1024)
+    )
+    step.wait_recv()
+    arrive = []
+    for flips in CHIP_FLIPS:
+        arrive.append(
+            net.send(r.ga2.at[:, net.index(CHIPS, flips)], r.ag1.at[:, my_chip], flips)
+        )
+    r.ag1[:, my_chip] = r.ga2[:, my_chip]
+    r.gwd[...] = (
+        lax.dot_general(
+            r.hid[...].reshape(1024, 512),
+            r.gf[...].reshape(1024, 1024),
+            FIRST,
+            preferred_element_type=f32,
+        )
+        .astype(bf)
+        .reshape(2, 2, 128, 1024)
+    )
+    y_far.append(net.send(r.gwd.at[1 - zh, 1 - y], r.y_wd.at[1], ("y",)))
+    for copy in reduced[1]:
+        copy.wait_recv()
+    total = r.kept[4] + resid
+    for k in range(3):
+        total = total + r.red_land[1, k].astype(f32)
+    r.out[...] = total.astype(bf)
+    for copy in arrive:
+        copy.wait_recv()
+
+    @pl.loop(0, 16)
+    def _(i):
+        both = r.ag1[i // 8, i % 8]
+        low, high = both[:, :64].astype(f32), both[:, 64:].astype(f32)
+        r.lb[i] = jnp.where(c == 0, high, low).astype(bf)
+        r.gatt[i, c] = jnp.where(c == 0, low, high).astype(bf)
+
+    step = net.send(r.lb, r.gatt.at[:, c], ("c",))
+    y_near = [net.send(r.gwgu.at[k, zh, :, 1 - y], r.y_wgu.at[k, 0], ("y",)) for k in range(2)]
+    y_near.append(net.send(r.gwd.at[zh, 1 - y], r.y_wd.at[0], ("y",)))
+    r.feat[...] = jnp.zeros_like(r.feat)
+    r.bias_s[...] = jnp.zeros_like(r.bias_s)
+    r.gh[...] = jnp.zeros_like(r.gh)
+    step.wait_recv()
+
+    @pl.loop(0, 4)
+    def _(i):
+        row = pl.ds(pl.multiple_of(i * SPAN, SPAN), SPAN)
+        kept = r.kept_o[row, :]
+        grad = r.gatt[pl.ds(i * 4, 4)].reshape(SPAN, 64).astype(f32)
+        grad = jnp.concatenate([grad, jnp.zeros((SPAN, 64), f32)], axis=1)
+        delta = jnp.sum(jnp.where(lane_span < 64, grad * kept, 0.0), axis=1, keepdims=True)
+        query = r.qf[row, :].astype(f32)
+        for j, part in enumerate(pieces(kept[:, 64:65])):
+            query = jnp.where(lane_span == 64 + 40 + j, -part, query)
+        r.qf[row, :] = query.astype(bf)
+        for j, part in enumerate(pieces(delta)):
+            grad = jnp.where(lane_span == 64 + j, -part, grad)
+        r.gb[row, :] = grad.astype(bf)
+
+    grad_k, grad_v = r.feat, r.kept_o
+    grad_v[...] = jnp.zeros_like(grad_v)
+    tree_o = Reduce(
+        net,
+        ("x", "zl", "y"),
+        lambda mask, core: r.gwo.at[:, net.index(CHIPS, mask), core],
+        lambda slot: r.wo.at[0, pl.ds(2 * slot, 2)],
+        lambda slot: r.wo.at[1, pl.ds(2 * slot, 2)],
+        lambda slot: r.o_arr.at[slot],
+    )
+    for mask in tree_o.masks:
+        tree_o.begin(mask)
+
+    def attend_back(i):
+        row = pl.ds(i * SPAN, SPAN)
+        query, grad = r.qf[row, :], r.gb[row, :]
+
+        def one_chunk(k, total):
+            col = pl.ds(pl.multiple_of(k * SPAN, SPAN), SPAN)
+            key = r.kf[col, :]
+            scores = lax.dot_general(query, key, LAST, preferred_element_type=f32)
+            probs = jnp.exp(scores)
+            centred = lax.dot_general(grad, r.vf[col, :], LAST, preferred_element_type=f32)
+            back = (probs * centred).astype(bf)
+            grad_v[col, :] += lax.dot_general(
+                probs.astype(bf), grad, FIRST, preferred_element_type=f32
+            )
+            grad_k[col, :] += lax.dot_general(back, query, FIRST, preferred_element_type=f32)
+            return total + jnp.dot(back, key, preferred_element_type=f32)
+
+        total = lax.fori_loop(0, 2048 // SPAN, one_chunk, jnp.zeros((SPAN, 128), f32))
+        r.gq[row, :] = (total * 0.125).astype(bf)
+        marks = r.kf[row, :].astype(f32)
+        same = jnp.where((lane_span >= 80) & (lane_span < 88), total * marks, 0.0)
+        every = jnp.where(lane_span == 72, total, 0.0)
+        r.bias_s[0:1, :] += jnp.sum(same, axis=0, keepdims=True)
+        r.bias_s[1:2, :] += jnp.sum(every, axis=0, keepdims=True)
+
+    h_steps = []
+
+    def half_gate_up(k):
+        y_far[k].wait_recv()
+        r.h_wgu[k] = (r.gwgu[k, 1 - zh, :, y].astype(f32) + r.y_wgu[k, 1].astype(f32)).astype(bf)
+        h_steps.append(net.send(r.h_wgu.at[k], r.h_wgu_land.at[k], ("zh",)))
+
+    half_gate_up(0)
+    attend_back(0)
+    half_gate_up(1)
+    for mask in tree_o.masks[:4]:
+        tree_o.forward(mask)
+    attend_back(1)
+    y_far[2].wait_recv()
+    r.h_wd[...] = (r.gwd[1 - zh, y].astype(f32) + r.y_wd[1].astype(f32)).astype(bf)
+    h_steps.append(net.send(r.h_wd, r.h_wd_land, ("zh",)))
+    attend_back(2)
+    tree_o.forward(("zl", "y"))
+    tree_o.forward(("zl",))
+    attend_back(3)
+    tree_o.forward(("y",))
+
+    def token_tree(part, dims):
+        return Reduce(
+            net,
+            dims,
+            lambda mask, core: r.x.at[part * 16 + 2 * net.index(CHIPS, mask) + core],
+            lambda slot: r.landed.at[slot, part],
+            lambda slot: r.sent.at[slot, part],
+            lambda slot: r.n2.at[slot, part],
+        )
+
+    trees = [token_tree(0, ("x", "zl", "y")), token_tree(1, ("y", "zl", "x"))]
+
+    def project_back(part, flips):
+        start = (part * 4 + net.index(("zl", "x"), flips)) * ROW_BLOCK
+        row, blocks = pl.ds(pl.multiple_of(start, ROW_BLOCK), ROW_BLOCK), pl.ds(start // 64, 4)
+        raw = r.raw[row, :]
+        scale = lax.rsqrt(pair_mean(raw * raw) + EPS)
+        cosine, sine = angles_of(r.cs[row, :])
+        key_part = pltpu.roll(grad_k[row, :].astype(bf).astype(f32), 64, 1)
+        grad = jnp.where(lane < 64, r.gq[row, :].astype(f32), key_part)
+        turned = grad * cosine - swap_halves(grad) * sine
+        r.bias_s[2:3, :] += jnp.sum(turned * raw * scale, axis=0, keepdims=True)
+        weighted = turned * qk_gain
+        back = scale * weighted - raw * (scale * scale * scale) * pair_mean(weighted * raw)
+        grad_qkv = jnp.concatenate([back, grad_v[row, :][:, :64]], axis=1).astype(bf)
+        grad_normed = lax.dot_general(
+            grad_qkv, r.wh[...].reshape(1024, 192), LAST, preferred_element_type=f32
+        )
+        value = r.x[blocks].reshape(ROW_BLOCK, 1024).astype(f32)
+        shaped = value * row_scale(value)
+        r.sums[0:1, :] += jnp.sum(grad_normed * shaped, axis=0, keepdims=True)
+        normed = (shaped * gain_attn).astype(bf)
+        term = lax.dot_general(normed, grad_qkv, FIRST, preferred_element_type=f32)
+        r.gh[:, :, :192] += term.reshape(4, 256, 192)
+        r.x[blocks] = grad_normed.astype(bf).reshape(4, 64, 1024)
+        trees[part].begin(flips)
+        trees[part].begin(flips + ("y",))
+
+    project_back(0, ("zl", "x"))
+    project_back(1, ("zl", "x"))
+    project_back(0, ("x",))
+    trees[0].forward(("zl", "x", "y"))
+    trees[0].forward(("zl", "x"))
+    trees[1].forward(("zl", "x", "y"))
+    project_back(1, ("x",))
+    trees[0].forward(("x", "y"))
+    trees[0].forward(("x",))
+    trees[1].forward(("x", "y"))
+    project_back(1, ("zl",))
+    project_back(0, ("zl",))
+    trees[1].forward(("zl", "y"))
+    project_back(1, ())
+    trees[1].forward(("y",))
+    project_back(0, ())
+
+    one = lane_iota(8)
+    both = jnp.broadcast_to(r.bias_s[2:3, :], (8, 128))
+    turned = pltpu.roll(both, 64, 1)
+    wide = lane_iota(1, 1024)
+    query_gain = jnp.concatenate([jnp.where(one < 64, both, turned)[0:1]] * 8, axis=1)
+    key_gain = jnp.concatenate([jnp.where(one < 64, turned, both)[0:1]] * 8, axis=1)
+    r.sums[2:3, :] = jnp.where(wide // 64 == head, query_gain, 0.0)
+    r.sums[3:4, :] = jnp.where(wide // 64 == head, key_gain, 0.0)
+    same = jnp.sum(r.bias_s[0:1, :], axis=1, keepdims=True)
+    every = jnp.sum(r.bias_s[1:2, :], axis=1, keepdims=True)
+    row_bias = jnp.where(wide == 2 * head, same, 0.0)
+    r.sums[4:5, :] = jnp.where(wide == 2 * head + 1, every - same, row_bias)
+    for k in range(8):
+        r.s_acc[0, k] = r.sums[:, 128 * k : 128 * (k + 1)]
+    rounds = ("c", "x", "y", "zl", "zh")
+    s_step = net.send(r.s_acc.at[0], r.s_land.at[0], (rounds[0],))
+
+    def small_round(step, k):
+        step.wait_recv()
+        total = r.s_acc[k] + r.s_land[k]
+        if k == 4:
+            r.gsmall[...] = total
+            return None
+        r.s_acc[k + 1] = total
+        return net.send(r.s_acc.at[k + 1], r.s_land.at[k + 1], (rounds[k + 1],))
+
+    r.gw[...] = r.gh[:, :, :192].astype(bf).reshape(2, 8, 2, 32, 192)
+    w_zh = net.send(r.gw.at[1 - zh], r.w_land, ("zh",))
+    trees[0].forward(("zl", "y"))
+    trees[0].forward(("zl",))
+    trees[1].forward(("zl", "x"))
+    trees[1].forward(("zl",))
+    s_step = small_round(s_step, 0)
+    trees[0].forward(("y",))
+    trees[1].forward(("x",))
+    s_step = small_round(s_step, 1)
+    w_zh.wait_recv()
+    r.w_t[...] = (r.gw[zh].astype(f32) + r.w_land[...].astype(f32)).astype(bf)
+    w_c = net.send(r.w_t.at[:, 1 - c], r.wp.at[:, c], ("c",))
+    r.wp[:, c] = r.w_t[:, c]
+    r.kept[1, :64] = trees[0].result()
+    r.kept[2, :64] = trees[1].result()
+    r.n_half[...] = r.kept[2 - zh, :64].astype(bf)
+    n_step = net.send(r.n_half, r.n_half_land, ("zh",))
+    s_step = small_round(s_step, 2)
+    w_c.wait_recv()
+    w_steps = []
+    for flips in CHIP_FLIPS:
+        w_steps.append(net.send(r.wp.at[net.index(CHIPS, flips)], r.wl.at[my_chip], flips))
+    r.wl[my_chip] = r.wp[my_chip]
+    total = tree_o.result()
+    r.kept[3, :32] = total[0]
+    r.kept[4, :32] = total[1]
+    r.o_half[...] = r.kept[4 - zh, :32].astype(bf)
+    o_step = net.send(r.o_half, r.o_half_land, ("zh",))
+    s_step = small_round(s_step, 3)
+
+    f_steps = []
+    for k in range(2):
+        y_near[k].wait_recv()
+        h_steps[k].wait_recv()
+        for j in range(4):
+            rows = r.gwgu[k, zh, j, y].astype(f32) + r.y_wgu[k, 0, j].astype(f32)
+            rows = rows + r.h_wgu_land[k, j].astype(f32)
+            r.gp[j, k, 0] = rows[:32].astype(bf)
+            r.gp[j, k, 1] = rows[32:].astype(bf)
+        for flips in GROUP_FLIPS:
+            f_steps.append(
+                net.send(
+                    r.gp.at[net.index(("zl", "x"), flips), k], r.gl.at[my_pair, k], flips
+                )
+            )
+        r.gl[my_pair, k] = r.gp[my_pair, k]
+    y_near[2].wait_recv()
+    h_steps[2].wait_recv()
+    r.gwdown[...] = r.gwd[zh, y].astype(f32) + r.y_wd[0].astype(f32) + r.h_wd_land[...].astype(f32)
+    f_c = []
+    for k in range(2):
+        for j in range(3):
+            f_steps[3 * k + j].wait_recv()
+        f_c.append(net.send(r.gl.at[:, k, 1 - c], r.f2.at[k, :, c], ("c",)))
+        r.f2[k, :, c] = r.gl[:, k, c]
+
+    n_step.wait_recv()
+    r.kept[2 - zh, :64] = r.n_half_land[...].astype(f32)
+    for b in range(2):
+        value = r.tok[b].astype(f32)
+        scale = row_scale(value)
+        weighted = r.kept[1 + b, :64] * gain_attn
+        mean = jnp.mean(weighted * value, axis=1, keepdims=True)
+        back = scale * weighted - value * (scale * scale * scale) * mean
+        r.gtok[b] = (r.kept[7, 64 * b : 64 * (b + 1), :] + back).astype(bf)
+    for copy in w_steps:
+        copy.wait_recv()
+    for h in range(16):
+        r.gwqkv[:, 192 * h : 192 * (h + 1)] = r.wl[h // 2, h % 2].astype(f32)
+    o_step.wait_recv()
+    r.gwout[...] = r.kept[3 + zh, :32] + r.o_half_land[...].astype(f32)
+    for k, out in ((0, r.gwgate), (1, r.gwup)):
+        f_c[k].wait_recv()
+        for pair in range(4):
+            for cc in range(2):
+                for part in range(4):
+                    idx = (part // 2) * 16 + pair * 4 + (part % 2) * 2 + cc
+                    out[:, 128 * idx : 128 * (idx + 1)] = r.f2[
+                        k, pair, cc, :, 128 * part : 128 * (part + 1)
+                    ].astype(f32)
+    small_round(s_step, 4)
+    net.drain()
+
+
+def layer(*arrays):
+    sm = pl.BlockSpec(memory_space=pltpu.SMEM)
+    vm = pl.BlockSpec(memory_space=pltpu.VMEM)
+    outs = layer_outputs()
+    return pl.pallas_call(
+        layer_kernel,
+        out_shape=[jax.ShapeDtypeStruct(*spec) for spec in outs.values()],
+        in_specs=[sm, sm] + [vm] * (len(layer_inputs()) - 2),
+        out_specs=[vm] * len(outs),
+        scratch_shapes=[pltpu.VMEM(*spec) for spec in layer_scratch().values()]
+        + [
+            pltpu.SemaphoreType.DMA((N_COPIES,)),
+            pltpu.SemaphoreType.DMA((N_COPIES,)),
+            pltpu.SemaphoreType.DMA((2,)),
+        ],
+        compiler_params=pltpu.CompilerParams(
+            collective_id=1, has_side_effects=True, vmem_limit_bytes=VMEM_BYTES
+        ),
+        name="layer",
+    )(*arrays)
+
+
+def frequencies():
+    index = np.arange(32, dtype=np.float32)
+    return np.broadcast_to((THETA ** (-2.0 * index / 64.0)).astype(np.float32)[:, None], (32, 128))
+
+
+def on_device_cube(
+    tokens,
+    cotangent,
+    w_qkv,
+    w_out,
+    w_gate,
+    w_up,
+    w_down,
+    norm_attn,
+    norm_ffn,
+    q_gain,
+    k_gain,
+    var_bias,
+    doc_lengths,
+    variate,
+    times,
+):
+    rank = jnp.int32(0)
+    for name in AXES:
+        rank = rank * 2 + lax.axis_index(name)
+    gains = jnp.concatenate([norm_attn, norm_ffn, q_gain, k_gain]).astype(jnp.float32)
+    out, gtok, gwqkv, gwout, gwgate, gwup, gwdown, small = layer(
+        doc_lengths, var_bias, tokens, cotangent, w_qkv, w_out, w_gate, w_up, w_down,
+        gains.reshape(1, 128), variate, times, jnp.asarray(frequencies()),
+    )
+    tile = lax.dynamic_slice(small, (rank // 4, 0, (rank % 4) * 32), (1, 8, 32))[0]
+    return (
+        out.reshape(2, 64, 1024),
+        gtok,
+        gwqkv,
+        gwout,
+        gwgate,
+        gwup,
+        gwdown,
+        tile[0],
+        tile[1],
+        tile[2],
+        tile[3],
+        small[0, 4, :32].reshape(16, 2),
+    )
+
+
+def run_parts(mesh, body, split):
+    rows, cut = P(split, None), P(split)
+    part = P(None, split, None)
+    return jax.shard_map(
+        body,
+        mesh=mesh,
+        in_specs=(part, part) + (rows,) * 5 + (cut,) * 4 + (P(), P(), P(None, split), P(None, split)),
+        out_specs=(part, part) + (rows,) * 5 + (cut,) * 4 + (P(),),
+        check_vma=False,
+    )
+
+
 def solution(mesh):
-    return jax.shard_map(
-        on_device,
-        mesh=mesh,
-        in_specs=(
-            P(None, ("head", "blk"), None),
-            P(None, ("head", "blk"), None),
-            P(("head", "blk"), None),
-            P(("head", "blk"), None),
-            P(("head", "blk"), None),
-            P(("head", "blk"), None),
-            P(("head", "blk"), None),
-            P(("head", "blk")),
-            P(("head", "blk")),
-            P(("head", "blk")),
-            P(("head", "blk")),
-            P(),
-            P(),
-            P(None, ("head", "blk")),
-            P(None, ("head", "blk")),
-        ),
-        out_specs=(
-            P(None, ("head", "blk"), None),
-            P(None, ("head", "blk"), None),
-            P(("head", "blk"), None),
-            P(("head", "blk"), None),
-            P(("head", "blk"), None),
-            P(("head", "blk"), None),
-            P(("head", "blk"), None),
-            P(("head", "blk")),
-            P(("head", "blk")),
-            P(("head", "blk")),
-            P(("head", "blk")),
-            P(),
-        ),
-        check_vma=False,
-    )
+    sizes = (mesh.shape["head"], mesh.shape["blk"])
+    general = run_parts(mesh, on_device, ("head", "blk"))
+    if sizes != (8, 4):
+        return general
+    cube = jax.sharding.Mesh(mesh.devices.reshape(2, 2, 2, 2, 2), AXES)
+    special = run_parts(cube, on_device_cube, AXES)
+
+    def chosen(*arrays):
+        tokens, w_gate, var_bias, lengths = arrays[0], arrays[4], arrays[11], arrays[12]
+        shapes = (tokens.shape, w_gate.shape, var_bias.shape, lengths.shape)
+        if shapes == ((2, 2048, 1024), (1024, 4096), (16, 2), (2, 8)):
+            return special(*arrays)
+        return general(*arrays)
+
+    return chosen

time: 1740 us -> 254 us (0.15)
  waiting for transfers between devices: 1150 us -> 0 us
  Pallas kernels: 0 us -> 239 us
  matrix products: 196 us -> 0 us
  blocking collectives: 132 us -> 0 us
  local copies, waits for them, and re-layouts: 122 us -> 12.2 us
  other arithmetic: 55.2 us -> 0.59 us
  starting transfers between devices: 47.5 us -> 0 us
    unnamed x11 -> x0, waiting for transfers between devices: 918 us -> none
    pallas_call x0 -> x1, Pallas kernels: none -> 239 us  [layer(): pl.pallas_call(layer_kernel, out_shape=[jax.ShapeDtypeStruct(*spec) for s...]
    all_gather x7 -> x0, waiting for transfers between devices: 228 us -> none  [the longest x1 74.1 us: on_device(): lax.all_gather(w_down, ('head', 'blk'), axis=0, tiled=True)]
    dot_general x58 -> x0, matrix products: 196 us -> none  [the longest x10 64.5 us: row_contract(): lax.dot_general(left_mat, right_mat, (((0,), (0,)), ((), ())), preferred_...]
    unnamed x2 -> x0, blocking collectives: 85.1 us -> none
    unnamed x252 -> x33, local copies, waits for them, and re-layouts: 67.8 us -> 9.42 us
    all_to_all x8 -> x0, starting transfers between devices: 47.1 us -> none  [the longest x2 20.4 us: on_device(): lax.all_to_all(attn_heads.astype(jnp.bfloat16), 'head', split_axis=0, con...]
    all_to_all x2 -> x0, blocking collectives: 36.6 us -> none  [on_device(): lax.all_to_all(packed, 'head', split_axis=1, concat_axis=0, tiled=True)]
  transfers between devices with their start and end apart: 18 -> 0, of which waited for: 7 -> 0; matrix products, arithmetic and copies ran while one was open for 13% -> 0% of each run, Pallas kernels for 0% -> 0%
where the time goes in v2:
time: 254 us; the launch traced here: 253 us
  Pallas kernels  239 us (94%)
  local copies, waits for them, and re-layouts  12.2 us (5%)
    pallas_call x1, Pallas kernels, layer(): pl.pallas_call(layer_kernel, out_shape=[jax.ShapeDtypeStruct(*spec) for s...  239 us
    unnamed x33, local copies, waits for them, and re-layouts  9.42 us

profile of v2, /device:TPU:0, one launch (start us, length us, event | category | flops | bytes accessed | tf_op | source)
XLA Modules:
  0.0 252.8 jit_solution(319520530307752502)
XLA Ops:
  0.7 0.6 copy-done.10
  1.3 0.0 copy-done.7
  1.4 0.0 copy-done.8
  1.4 0.0 copy-done.9
  1.4 0.6 maximum_convert_fusion.refs_9_
  2.0 0.1 copy-done.6
  2.1 0.7 copy.30.refs_1_
  2.8 0.7 jit_solution_.3.refs_12_
  3.4 239.3 %layer.1 = (bf16[128,1024]{1,0:T(8,128)(2,1)}, bf16[2,64,1024]{2,1,0:T(8,128)(2,1)}, f32[32,3072]{1,0:T(8,128)}, f32[32,1024]{1,0:T(8,128)}, f32[32,4096]{1,0:T(...) custom-call(s32[2,8]{1,0:T(2,128)} %refs_0_.1, f32[16,2]{1,0:T(8,128)} %copy.30.refs_1_, ...), custom_call_target="tpu_custom_call" | custom-call | tf_op jit(solution)/shard_map/layer/pallas_call | solution.py:1359
  242.7 0.7 slice_reduce_fusion
  243.4 0.8 constant_dynamic-slice_fusion
  244.2 0.5 slice_bitcast_fusion
  244.7 0.1 reshape_squeeze.3
  244.8 0.6 copy.31
  245.4 1.7 copy.39
  247.2 0.7 copy.40
  247.9 0.7 copy.41
  248.6 0.2 copy-done.5
  248.9 0.7 copy.42
  249.5 0.8 copy.43
  250.3 0.4 copy-done.1
  250.8 0.8 copy.44
  251.6 0.4 copy-done
  252.0 0.8 copy.45
  (16 shorter events, 0.0 us)
Async XLA Ops:
  0.7 0.7 copy-start.10
  0.7 0.7 copy-start.7
  0.7 0.7 copy-start.8
  0.7 0.7 copy-start.9
  1.4 0.7 copy-start.6
  2.1 0.7 copy-start.11
  244.8 2.4 copy-start.4
  245.4 2.4 copy-start.3
  247.9 1.0 copy-start.5
  247.9 1.7 copy-start.2
  249.5 1.2 copy-start.1
  250.8 1.2 copy-start

commit v3 on v2

--- a/solution.py
+++ b/solution.py
@@ -446,6 +446,12 @@
         copy.start()
         return copy
 
+    def settle(self, copies):
+        for copy in copies:
+            copy.wait_send()
+        gone = [id(copy) for copy in copies]
+        self.open = [copy for copy in self.open if id(copy) not in gone]
+
     def drain(self):
         for copy in self.open:
             copy.wait_send()
@@ -561,7 +567,7 @@
 
 def layer_inputs():
     return ["lengths", "bias", "tok", "cot", "wqkv", "wout", "wgate", "wup", "wdown"] + [
-        "gains", "variate", "times", "freq",
+        "norm_attn", "norm_ffn", "q_gain", "k_gain", "variate", "times", "freq",
     ]
 
 
@@ -610,7 +616,8 @@
         "att_s": ((128, 1024), bf),
         "resid": ((128, 1024), f32),
         "n2": ((8, 2, 64, 1024), bf),
-        "gh": ((4, 256, 512), f32),
+        "gate": ((4, 256, 512), f32),
+        "up": ((4, 256, 512), f32),
         "hid": ((4, 256, 512), bf),
         "ggu": ((2, 4, 256, 512), bf),
         "kept": ((8, 128, 1024), f32),
@@ -618,6 +625,7 @@
         "landed": ((8, 2, 64, 1024), bf),
         "red_send": ((2, 3, 128, 1024), bf),
         "red_land": ((2, 3, 128, 1024), bf),
+        "branch": ((128, 1024), bf),
         "ga3": ((2, 8, 64, 128), bf),
         "ga2": ((2, 8, 64, 128), bf),
         "ag1": ((2, 8, 64, 128), bf),
@@ -644,8 +652,8 @@
         "f2": ((2, 4, 2, 32, 512), bf),
         "w_land": ((8, 2, 32, 192), bf),
         "w_t": ((8, 2, 32, 192), bf),
-        "s_acc": ((5, 8, 8, 128), f32),
-        "s_land": ((5, 8, 8, 128), f32),
+        "s_acc": ((3, 8, 8, 128), f32),
+        "s_land": ((9, 8, 8, 128), f32),
     }
 
 
@@ -672,23 +680,21 @@
 
     x_own = Gather(net, x_region(0), ("zl", "y", "x"))
     x_far = Gather(net, x_region(1), ("zl", "x", "y"))
-    wo_tree = Gather(net, lambda f: r.wo.at[:, net.index(AXES[1:], f)], ("y", "zl", "x"))
+    wo_tree = Gather(net, lambda f: r.wo.at[:, net.index(AXES[1:], f)], ("zl", "y", "x"))
     gf_tree = Gather(net, lambda f: r.gf.at[net.index(("zl", "x", "c"), f)], ("zl", "x"))
-    swap = net.send(r.tok.at[1 - zh], r.x.at[mine], ("zh",))
-    x_own.push((), r.tok.at[zh])
     r.tile[...] = jnp.zeros_like(r.tile)
     r.tile[0:2, 0:64] = r.variate[...].astype(f32)
     r.tile[2:4, 0:64] = r.times[...].astype(f32)
-    r.tile[4:5, :] = r.gains[...]
+    for k, gain in enumerate((r.norm_attn, r.norm_ffn, r.q_gain, r.k_gain)):
+        r.tile[4 + k : 5 + k, 0:32] = gain[...].astype(f32)
     sm_step = net.send(r.tile, r.sm.at[zh, zl, x, y, c], ("zh",))
+    swap = net.send(r.tok.at[1 - zh], r.x.at[mine], ("zh",))
     for h in range(16):
         r.wp[h // 2, h % 2] = r.wqkv[:, 192 * h : 192 * (h + 1)]
     w_arrive = []
     for flips in CHIP_FLIPS:
         w_arrive.append(net.send(r.wp.at[net.index(CHIPS, flips)], r.wl.at[my_chip], flips))
-    r.x[mine] = r.tok[zh]
-    r.sm[zh, zl, x, y, c] = r.tile[...]
-    r.wl[my_chip] = r.wp[my_chip]
+    x_own.push((), r.tok.at[zh])
     for pair in range(4):
         for cc in range(2):
             for part in range(4):
@@ -701,54 +707,58 @@
         g_arrive.append(
             net.send(r.gp.at[net.index(("zl", "x"), flips)], r.gl.at[my_pair], flips)
         )
+    r.sm[zh, zl, x, y, c] = r.tile[...]
+    r.wl[my_chip] = r.wp[my_chip]
+    r.x[mine] = r.tok[zh]
     r.gl[my_pair] = r.gp[my_pair]
     r.gf[net.index(("zl", "x", "c"))] = r.cot[...]
     r.wd[zh, y] = r.wdown[...]
     r.wo[zh, in_half] = r.wout[...]
-    wo_zh = net.send(r.wout, r.wo.at[zh, in_half], ("zh",))
 
     sm_step.wait_recv()
     sm_step = net.send(r.sm.at[:, zl, x, y, c], r.sm.at[:, zl, x, y, c], ("c",))
-    x_own.take("zl")
-    x_own.take("y")
-    sm_step.wait_recv()
-    sm_step = net.send(r.sm.at[:, zl, x, y], r.sm.at[:, zl, x, y], ("y",))
     for copy in w_arrive:
         copy.wait_recv()
     w_c = net.send(r.wl.at[:, 1 - c], r.wh.at[zh, :, c], ("c",))
     r.wh[zh, :, c] = r.wl[:, c]
+    sm_step.wait_recv()
+    sm_step = net.send(r.sm.at[:, zl, x, y], r.sm.at[:, zl, x, y], ("y",))
+    x_own.take("zl")
+    x_own.take("y")
+    w_c.wait_recv()
+    w_zh = net.send(r.wh.at[zh], r.wh.at[zh], ("zh",))
     swap.wait_recv()
     x_far.push(())
+    wo_zh = net.send(r.wout, r.wo.at[zh, in_half], ("zh",))
     sm_step.wait_recv()
     sm_step = net.send(r.sm.at[:, zl, x], r.sm.at[:, zl, x], ("zl",))
     x_own.take("zl", "y")
-    w_c.wait_recv()
-    w_zh = net.send(r.wh.at[zh], r.wh.at[zh], ("zh",))
+    x_own.take("x")
     x_far.take("zl")
     sm_step.wait_recv()
     sm_step = net.send(r.sm.at[:, :, x], r.sm.at[:, :, x], ("x",))
+    def g_piece(k, half):
+        return r.wgu.at[k // 2, half, pl.ds(2 * (k % 2), 2), y]
+
+    g_c, g_zh, g_y, g_fwd = [], [], [], []
+
     for copy in g_arrive:
         copy.wait_recv()
-    g_c = []
     for k in range(2):
         g_c.append(net.send(r.gl.at[:, k, 1 - c], r.wgu.at[k, zh, :, y, c], ("c",)))
         r.wgu[k, zh, :, y, c] = r.gl[:, k, c]
-    x_own.take("x")
+    x_far.take("x")
     x_own.take("zl", "x")
-    x_far.take("x")
-    x_far.take("zl", "x")
-
-    def g_piece(k, half):
-        return r.wgu.at[k // 2, half, pl.ds(2 * (k % 2), 2), y]
-
-    g_zh, g_y, g_fwd = [], [], []
+    x_own.take("y", "x")
+    wo_zh.wait_recv()
+    wo_tree.push(())
     for k in range(4):
         if k % 2 == 0:
             g_c[k // 2].wait_recv()
         g_zh.append(net.send(g_piece(k, zh), g_piece(k, zh), ("zh",)))
-    wd_zh = net.send(r.wdown, r.wd.at[zh, y], ("zh",))
-    x_own.take("y", "x")
-    x_far.take("y")
+    x_far.take("zl", "x")
+    for k in range(4):
+        g_y.append(net.send(g_piece(k, zh), g_piece(k, zh), ("y",)))
     sm_step.wait_recv()
 
     lane8 = lane_iota(8)
@@ -760,9 +770,9 @@
                 held = r.sm[
                     block // 16, (block // 8) % 2, (block // 4) % 2, (block // 2) % 2, block % 2
                 ]
-                moved = held if j == which else pltpu.roll(held, (32 * (j - which)) % 128, 1)
+                moved = held if j == 0 else pltpu.roll(held, 32 * j, 1)
                 row = jnp.where(lane8 // 32 == j, moved, row)
-            r.gain_s[which, group : group + 1] = row[4:5, :]
+            r.gain_s[which, group : group + 1] = row[4 + which : 5 + which, :]
     gain_attn = jnp.concatenate([r.gain_s[0, k : k + 1] for k in range(8)], axis=1)
     gain_ffn = jnp.concatenate([r.gain_s[1, k : k + 1] for k in range(8)], axis=1)
     held_q = r.gain_s[2, pl.ds(my_chip, 1)]
@@ -783,8 +793,8 @@
     for j in range(8):
         start_col = jnp.where(sub == j, starts[j], start_col)
         end_col = jnp.where(sub == j, ends[j], end_col)
-    same_bias = jnp.full((8, 128), r.bias[head, 0], f32)
-    other_bias = jnp.full((8, 128), r.bias[head, 1], f32)
+    same_bias = jnp.full((8, 128), r.bias[0, head], f32)
+    other_bias = jnp.full((8, 128), r.bias[1, head], f32)
     diff_parts = pieces(same_bias - other_bias)
     zero = jnp.zeros((8, 128), f32)
     const_q = jnp.where(sub == 0, -256.0, 0.0)
@@ -807,32 +817,23 @@
         rows = [doc * 256.0, const_q] + [var * part for part in diff_parts] + [zero, zero, zero]
         rows += [doc, const_k, var, var, var, ones_k, zero, zero]
         r.feat[col, :] = jnp.concatenate(rows, axis=0).T
-        angle = jnp.broadcast_to(time_row, (32, 128)) * r.freq[...]
+        angle = jnp.broadcast_to(time_row, (32, 128)) * jnp.broadcast_to(r.freq[...], (32, 128))
         cosine, sine = jnp.cos(angle), jnp.sin(angle)
         r.cs[col, :] = jnp.concatenate([cosine, cosine, -sine, sine], axis=0).T
 
-    x_own.take("zl", "y", "x")
-    x_far.take("zl", "y")
-    x_far.take("x", "y")
-    x_far.take("zl", "x", "y")
-    for k in range(4):
-        g_y.append(net.send(g_piece(k, zh), g_piece(k, zh), ("y",)))
-    gf_tree.push((), r.cot)
-    wd_y = net.send(r.wdown, r.wd.at[zh, y], ("y",))
-    w_zh.wait_recv()
-
     lane = lane_iota(ROW_BLOCK)
 
-    def rows_at(part, flips):
-        z_part = zh if part == 0 else 1 - zh
-        start = ((z_part * 2 + net.index(("zl",), flips)) * 2 + net.index(("x",), flips)) * ROW_BLOCK
-        return pl.ds(pl.multiple_of(start, ROW_BLOCK), ROW_BLOCK), pl.ds(start // 64, 4)
-
-    def project(part, flips):
+    def arrived(part, *flips):
         tree = x_own if part == 0 else x_far
         tree.ready(*flips)
         tree.ready(*(flips + ("y",)))
-        row, blocks = rows_at(part, flips)
+
+    def project(j):
+        part, far_x, far_zl = j // 4, (j // 2) % 2, j % 2
+        at = ((zh + part - 2 * zh * part) * 2 + zl + far_zl - 2 * zl * far_zl) * 2
+        at = (at + x + far_x - 2 * x * far_x) * ROW_BLOCK
+        row = pl.ds(pl.multiple_of(at, ROW_BLOCK), ROW_BLOCK)
+        blocks = pl.ds(at // 64, 4)
         value = r.x[blocks].reshape(ROW_BLOCK, 1024).astype(f32)
         normed = (value * row_scale(value) * gain_attn).astype(bf)
         qkv = jnp.dot(normed, r.wh[...].reshape(1024, 192), preferred_element_type=f32)
@@ -847,25 +848,28 @@
         third = jnp.concatenate([qkv[:, 128:192], jnp.zeros((ROW_BLOCK, 64), f32)], axis=1)
         r.vf[row, :] = jnp.where((lane >= 64) & (lane < 67), 1.0, third).astype(bf)
 
-    project(0, ())
-    project(0, ("zl",))
-    wo_zh.wait_recv()
-    wo_tree.push(())
-    project(1, ())
-    project(1, ("zl",))
-    gf_tree.take("zl")
-    project(0, ("x",))
-    project(0, ("zl", "x"))
-    wo_tree.take("y")
-    project(1, ("x",))
-    project(1, ("zl", "x"))
+    w_zh.wait_recv()
+    arrived(0)
+    arrived(0, "zl")
+    x_own.take("zl", "y", "x")
+    x_far.take("y")
+    x_far.take("zl", "y")
+    arrived(0, "x")
+    arrived(0, "zl", "x")
+    pl.loop(0, 4)(project)
+    x_far.take("x", "y")
+    x_far.take("zl", "x", "y")
+    arrived(1)
+    arrived(1, "zl")
+    arrived(1, "x")
+    arrived(1, "zl", "x")
+    pl.loop(4, 8)(project)
     wo_tree.take("zl")
-    wo_tree.take("zl", "y")
 
     lane_span = lane_iota(SPAN)
 
     def attend(i):
-        row = pl.ds(i * SPAN, SPAN)
+        row = pl.ds(pl.multiple_of(i * SPAN, SPAN), SPAN)
         query = r.qf[row, :]
 
         def one_chunk(k, total):
@@ -878,30 +882,19 @@
         weight = total[:, 64:65]
         result = total / weight
         r.kept_o[row, :] = jnp.where(lane_span < 64, result, jnp.log(weight))
-        r.att[4 * i : 4 * i + 4] = result[:, :64].astype(bf).reshape(4, 2, 64, 64)
+        r.att[pl.ds(4 * i, 4)] = result[:, :64].astype(bf).reshape(4, 2, 64, 64)
 
     def g_pass(k):
         g_zh[k].wait_recv()
         g_fwd.append(net.send(g_piece(k, 1 - zh), g_piece(k, 1 - zh), ("y",)))
 
-    attend(0)
-    gf_tree.take("x")
-    gf_tree.take("zl", "x")
+    pl.loop(0, 2)(attend)
+    wo_tree.take("y")
     g_pass(0)
-    attend(1)
-    wo_tree.take("x")
-    wo_tree.take("y", "x")
-    g_pass(1)
-    attend(2)
-    wo_tree.take("zl", "x")
-    wo_tree.take("zl", "y", "x")
-    g_pass(2)
-    attend(3)
+    pl.loop(2, 4)(attend)
 
     step = net.send(r.att.at[:, 1 - c], r.lb, ("c",))
-    g_pass(3)
-    wd_zh.wait_recv()
-    wd_fwd = net.send(r.wd.at[1 - zh, y], r.wd.at[1 - zh, y], ("y",))
+    wo_tree.take("zl", "y")
     step.wait_recv()
     lane64 = lane_iota(64)
 
@@ -917,6 +910,7 @@
             net.send(r.ap.at[:, net.index(CHIPS, flips)], r.at2.at[my_chip], flips)
         )
     r.at2[my_chip] = r.ap[:, my_chip]
+
     def w_down():
         return r.wd[...].reshape(512, 1024)
 
@@ -926,23 +920,21 @@
     def w_in(k):
         return r.wgu[k].reshape(1024, 512)
 
-    gf_tree.ready()
-    gf_tree.ready("zl")
-    gf_tree.ready("x")
-    gf_tree.ready("zl", "x")
-    wd_y.wait_recv()
-    wd_fwd.wait_recv()
-    for p in range(2):
-        rows = r.gf[2 * p : 2 * p + 2].reshape(256, 1024)
-        r.gh[p] = lax.dot_general(rows, w_down(), LAST, preferred_element_type=f32)
     for copy in arrive:
         copy.wait_recv()
     step = net.send(r.at2.at[:, 1 - zh], r.at3, ("zh",))
-    for p in range(2, 4):
-        rows = r.gf[2 * p : 2 * p + 2].reshape(256, 1024)
-        r.gh[p] = lax.dot_general(rows, w_down(), LAST, preferred_element_type=f32)
+    wd_zh = net.send(r.wdown, r.wd.at[zh, y], ("zh",))
     for k in range(8):
         r.att_s[pl.ds(pl.multiple_of(zh * 64, 64), 64), 128 * k : 128 * (k + 1)] = r.at2[k, zh]
+    gf_tree.push((), r.cot)
+    g_pass(1)
+    g_pass(2)
+    wd_y = net.send(r.wdown, r.wd.at[zh, y], ("y",))
+    wo_tree.take("x")
+    wo_tree.take("y", "x")
+    wo_tree.take("zl", "x")
+    wo_tree.take("zl", "y", "x")
+    g_pass(3)
     for flips in [(), ("y",), ("zl",), ("zl", "y"), ("x",), ("y", "x"), ("zl", "x"), ("zl", "y", "x")]:
         wo_tree.ready(*flips)
     step.wait_recv()
@@ -957,20 +949,20 @@
     r.n2[mine8] = (resid * scale * gain_ffn).astype(bf).reshape(2, 64, 1024)
     to_sibling = [net.send(r.n2.at[mine8], r.n2.at[mine8], ("c",))]
     from_chips = [net.send(r.n2.at[mine8], r.n2.at[mine8], flips) for flips in GROUP_FLIPS]
-    for copy in g_y + g_fwd:
-        copy.wait_recv()
-
     def pair_rows(ref, pair):
         return ref[pl.ds(2 * pair, 2)].reshape(256, 1024)
 
     def feed(pair):
         rows = pair_rows(r.n2, pair)
-        gate = jnp.dot(rows, w_in(0), preferred_element_type=f32)
-        up = jnp.dot(rows, w_in(1), preferred_element_type=f32)
+        r.gate[pair] = jnp.dot(rows, w_in(0), preferred_element_type=f32)
+        r.up[pair] = jnp.dot(rows, w_in(1), preferred_element_type=f32)
+
+    def feed_back(pair):
+        back = lax.dot_general(pair_rows(r.gf, pair), w_down(), LAST, preferred_element_type=f32)
+        gate, up = r.gate[pair], r.up[pair]
         sig = 1.0 / (1.0 + jnp.exp(-gate))
         silu = gate * sig
         r.hid[pair] = (silu * up).astype(bf)
-        back = r.gh[pair]
         r.ggu[0, pair] = (back * up * sig * (1.0 + gate * (1.0 - sig))).astype(bf)
         r.ggu[1, pair] = (back * silu).astype(bf)
 
@@ -983,10 +975,16 @@
 
     halves, reduced = {}, {0: [], 1: []}
 
-    def share(kind, slot, value):
-        at = 4 * kind + slot
+    def pair_at(slot):
+        far_zl, far_x = slot % 2, slot // 2
+        return (zl + far_zl - 2 * zl * far_zl) * 2 + x + far_x - 2 * x * far_x
+
+    def keep_half(at, value):
         r.kept[at] = jnp.where(c == 0, value[:128], value[128:])
         r.sent[at] = jnp.where(c == 0, value[128:], value[:128]).astype(bf).reshape(2, 64, 1024)
+
+    def share(kind, slot):
+        at = 4 * kind + slot
         halves[at] = net.send(r.sent.at[at], r.landed.at[at], ("c",))
 
     def finish_half(kind, slot):
@@ -1006,28 +1004,48 @@
             )
 
     pairs = [my_pair] + [net.index(("zl", "x"), flips) for flips in GROUP_FLIPS]
+    wd_zh.wait_recv()
+    wd_fwd = net.send(r.wd.at[1 - zh, y], r.wd.at[1 - zh, y], ("y",))
+    gf_tree.take("zl")
+    for copy in g_y + g_fwd:
+        copy.wait_recv()
     to_sibling[0].wait_recv()
-    feed(pairs[0])
     for k in range(3):
         from_chips[k].wait_recv()
-        to_sibling.append(
-            net.send(r.n2.at[2 * pairs[k + 1] + c], r.n2.at[2 * pairs[k + 1] + c], ("c",))
-        )
-    for k in range(3):
-        to_sibling[k + 1].wait_recv()
-        feed(pairs[k + 1])
-        share(0, k + 1, back_product(pairs[k + 1]))
-        if k > 0:
-            finish_half(0, k)
+        at = 2 * pairs[k + 1] + c
+        to_sibling.append(net.send(r.n2.at[at], r.n2.at[at], ("c",)))
+        if k == 0:
+            to_sibling[1].wait_recv()
+            pl.loop(0, 2)(lambda slot: feed(pair_at(slot)))
+    gf_tree.take("x")
+    gf_tree.take("zl", "x")
+    to_sibling[2].wait_recv()
+    to_sibling[3].wait_recv()
+    pl.loop(2, 4)(lambda slot: feed(pair_at(slot)))
+    gf_tree.ready()
+    gf_tree.ready("zl")
+    gf_tree.ready("x")
+    gf_tree.ready("zl", "x")
+    wd_y.wait_recv()
+    wd_fwd.wait_recv()
+    net.drain()
+
+    def feed_both(slot):
+        pair = pair_at(slot)
+        feed_back(pair)
+        keep_half(slot, back_product(pair))
+
+    pl.loop(2, 4)(feed_both)
+    share(0, 2)
+    share(0, 3)
+    pl.loop(0, 2)(feed_both)
     finish_half(0, 3)
-    share(0, 0, back_product(pairs[0]))
-    for k in (1, 2, 3):
-        share(1, k, out_product(pairs[k]))
-        if k > 1:
-            finish_half(1, k - 1)
-    finish_half(0, 0)
-    finish_half(1, 3)
-    for k in range(2):
+    finish_half(0, 2)
+    share(0, 1)
+    share(0, 0)
+
+    @pl.loop(0, 2)
+    def _(k):
         r.gwgu[k] = (
             lax.dot_general(
                 r.n2[...].reshape(1024, 1024),
@@ -1038,9 +1056,41 @@
             .astype(bf)
             .reshape(2, 4, 2, 64, 512)
         )
+    finish_half(0, 1)
     y_far = [net.send(r.gwgu.at[k, 1 - zh, :, 1 - y], r.y_wgu.at[k, 1], ("y",)) for k in range(2)]
-    share(1, 0, out_product(pairs[0]))
-    net.drain()
+    finish_half(0, 0)
+
+    @pl.loop(0, 4)
+    def _(slot):
+        keep_half(4 + slot, out_product(pair_at(slot)))
+
+    for k in range(4):
+        share(1, k)
+    for half in range(2):
+        cols = slice(512 * half, 512 * (half + 1))
+        r.gwd[:, :, :, cols] = (
+            lax.dot_general(
+                r.hid[...].reshape(1024, 512),
+                r.gf[:, :, :, cols].reshape(1024, 512),
+                FIRST,
+                preferred_element_type=f32,
+            )
+            .astype(bf)
+            .reshape(2, 2, 128, 512)
+        )
+    net.settle(list(halves.values()))
+
+    h_steps = []
+
+    def half_gate_up(k):
+        y_far[k].wait_recv()
+        r.h_wgu[k] = (r.gwgu[k, 1 - zh, :, y].astype(f32) + r.y_wgu[k, 1].astype(f32)).astype(bf)
+        h_steps.append(net.send(r.h_wgu.at[k], r.h_wgu_land.at[k], ("zh",)))
+
+    def half_down():
+        y_far[2].wait_recv()
+        r.h_wd[...] = (r.gwd[1 - zh, y].astype(f32) + r.y_wd[1].astype(f32)).astype(bf)
+        h_steps.append(net.send(r.h_wd, r.h_wd_land, ("zh",)))
 
     for copy in reduced[0]:
         copy.wait_recv()
@@ -1055,20 +1105,14 @@
     mean = jnp.mean(weighted * resid, axis=1, keepdims=True)
     grad_resid = r.cot[...].reshape(128, 1024).astype(f32) + scale * weighted
     grad_resid = grad_resid - resid * (scale * scale * scale) * mean
-    r.kept[7] = grad_resid
-    branch = grad_resid.astype(bf)
-    grad_att = lax.dot_general(branch, w_o(), LAST, preferred_element_type=f32).astype(bf)
+    r.kept[0] = grad_resid
+    r.branch[...] = grad_resid.astype(bf)
+    grad_att = lax.dot_general(r.branch[...], w_o(), LAST, preferred_element_type=f32).astype(bf)
     for k in range(8):
         for b in range(2):
             r.ga3[b, k] = grad_att[64 * b : 64 * (b + 1), 128 * k : 128 * (k + 1)]
     step = net.send(r.ga3.at[1 - zh], r.ga2.at[zh], ("zh",))
     r.ga2[zh] = r.ga3[zh]
-    finish_half(1, 0)
-    r.gwo[...] = (
-        lax.dot_general(r.att_s[...], branch, FIRST, preferred_element_type=f32)
-        .astype(bf)
-        .reshape(2, 8, 2, 32, 1024)
-    )
     step.wait_recv()
     arrive = []
     for flips in CHIP_FLIPS:
@@ -1076,23 +1120,13 @@
             net.send(r.ga2.at[:, net.index(CHIPS, flips)], r.ag1.at[:, my_chip], flips)
         )
     r.ag1[:, my_chip] = r.ga2[:, my_chip]
-    r.gwd[...] = (
-        lax.dot_general(
-            r.hid[...].reshape(1024, 512),
-            r.gf[...].reshape(1024, 1024),
-            FIRST,
-            preferred_element_type=f32,
-        )
-        .astype(bf)
-        .reshape(2, 2, 128, 1024)
-    )
-    y_far.append(net.send(r.gwd.at[1 - zh, 1 - y], r.y_wd.at[1], ("y",)))
-    for copy in reduced[1]:
-        copy.wait_recv()
-    total = r.kept[4] + resid
-    for k in range(3):
-        total = total + r.red_land[1, k].astype(f32)
-    r.out[...] = total.astype(bf)
+    for j in range(8):
+        cols = slice(128 * j, 128 * (j + 1))
+        r.gwo[j // 4, 2 * (j % 4) : 2 * (j % 4) + 2] = (
+            lax.dot_general(r.att_s[:, cols], r.branch[...], FIRST, preferred_element_type=f32)
+            .astype(bf)
+            .reshape(2, 2, 32, 1024)
+        )
     for copy in arrive:
         copy.wait_recv()
 
@@ -1103,12 +1137,17 @@
         r.lb[i] = jnp.where(c == 0, high, low).astype(bf)
         r.gatt[i, c] = jnp.where(c == 0, low, high).astype(bf)
 
+    for k in (3, 2, 1, 0):
+        finish_half(1, k)
     step = net.send(r.lb, r.gatt.at[:, c], ("c",))
+    half_gate_up(0)
+    half_gate_up(1)
+    y_far.append(net.send(r.gwd.at[1 - zh, 1 - y], r.y_wd.at[1], ("y",)))
     y_near = [net.send(r.gwgu.at[k, zh, :, 1 - y], r.y_wgu.at[k, 0], ("y",)) for k in range(2)]
     y_near.append(net.send(r.gwd.at[zh, 1 - y], r.y_wd.at[0], ("y",)))
     r.feat[...] = jnp.zeros_like(r.feat)
     r.bias_s[...] = jnp.zeros_like(r.bias_s)
-    r.gh[...] = jnp.zeros_like(r.gh)
+    r.gate[...] = jnp.zeros_like(r.gate)
     step.wait_recv()
 
     @pl.loop(0, 4)
@@ -1140,7 +1179,7 @@
         tree_o.begin(mask)
 
     def attend_back(i):
-        row = pl.ds(i * SPAN, SPAN)
+        row = pl.ds(pl.multiple_of(i * SPAN, SPAN), SPAN)
         query, grad = r.qf[row, :], r.gb[row, :]
 
         def one_chunk(k, total):
@@ -1164,27 +1203,13 @@
         r.bias_s[0:1, :] += jnp.sum(same, axis=0, keepdims=True)
         r.bias_s[1:2, :] += jnp.sum(every, axis=0, keepdims=True)
 
-    h_steps = []
-
-    def half_gate_up(k):
-        y_far[k].wait_recv()
-        r.h_wgu[k] = (r.gwgu[k, 1 - zh, :, y].astype(f32) + r.y_wgu[k, 1].astype(f32)).astype(bf)
-        h_steps.append(net.send(r.h_wgu.at[k], r.h_wgu_land.at[k], ("zh",)))
-
-    half_gate_up(0)
-    attend_back(0)
-    half_gate_up(1)
+    half_down()
+    pl.loop(0, 2)(attend_back)
     for mask in tree_o.masks[:4]:
         tree_o.forward(mask)
-    attend_back(1)
-    y_far[2].wait_recv()
-    r.h_wd[...] = (r.gwd[1 - zh, y].astype(f32) + r.y_wd[1].astype(f32)).astype(bf)
-    h_steps.append(net.send(r.h_wd, r.h_wd_land, ("zh",)))
-    attend_back(2)
+    pl.loop(2, 4)(attend_back)
     tree_o.forward(("zl", "y"))
     tree_o.forward(("zl",))
-    attend_back(3)
-    tree_o.forward(("y",))
 
     def token_tree(part, dims):
         return Reduce(
@@ -1196,10 +1221,10 @@
             lambda slot: r.n2.at[slot, part],
         )
 
-    trees = [token_tree(0, ("x", "zl", "y")), token_tree(1, ("y", "zl", "x"))]
-
-    def project_back(part, flips):
-        start = (part * 4 + net.index(("zl", "x"), flips)) * ROW_BLOCK
+    trees = [token_tree(0, ("x", "y", "zl")), token_tree(1, ("y", "x", "zl"))]
+
+    def project_back(part, where):
+        start = (part * 4 + where) * ROW_BLOCK
         row, blocks = pl.ds(pl.multiple_of(start, ROW_BLOCK), ROW_BLOCK), pl.ds(start // 64, 4)
         raw = r.raw[row, :]
         scale = lax.rsqrt(pair_mean(raw * raw) + EPS)
@@ -1219,27 +1244,53 @@
         r.sums[0:1, :] += jnp.sum(grad_normed * shaped, axis=0, keepdims=True)
         normed = (shaped * gain_attn).astype(bf)
         term = lax.dot_general(normed, grad_qkv, FIRST, preferred_element_type=f32)
-        r.gh[:, :, :192] += term.reshape(4, 256, 192)
+        r.gate[:, :, :192] += term.reshape(4, 256, 192)
         r.x[blocks] = grad_normed.astype(bf).reshape(4, 64, 1024)
-        trees[part].begin(flips)
-        trees[part].begin(flips + ("y",))
-
-    project_back(0, ("zl", "x"))
-    project_back(1, ("zl", "x"))
-    project_back(0, ("x",))
+
+    f_steps, f_c = [], []
+
+    def feed_sum(k):
+        y_near[k].wait_recv()
+        h_steps[k].wait_recv()
+        for j in range(4):
+            rows = r.gwgu[k, zh, j, y].astype(f32) + r.y_wgu[k, 0, j].astype(f32)
+            rows = rows + r.h_wgu_land[k, j].astype(f32)
+            r.gp[j, k, 0] = rows[:32].astype(bf)
+            r.gp[j, k, 1] = rows[32:].astype(bf)
+        for flips in GROUP_FLIPS:
+            f_steps.append(
+                net.send(r.gp.at[net.index(("zl", "x"), flips), k], r.gl.at[my_pair, k], flips)
+            )
+        r.gl[my_pair, k] = r.gp[my_pair, k]
+
+    def feed_sibling(k):
+        for j in range(3):
+            f_steps[3 * k + j].wait_recv()
+        f_c.append(net.send(r.gl.at[:, k, 1 - c], r.f2.at[k, :, c], ("c",)))
+        r.f2[k, :, c] = r.gl[:, k, c]
+
+    def two_back(*flips):
+        where = net.index(("zl", "x"), flips)
+        pl.loop(0, 2)(lambda part: project_back(part, where))
+        for tree in trees:
+            tree.begin(flips)
+            tree.begin(flips + ("y",))
+
+    two_back("zl", "x")
+    tree_o.forward(("y",))
+    two_back("x")
     trees[0].forward(("zl", "x", "y"))
     trees[0].forward(("zl", "x"))
     trees[1].forward(("zl", "x", "y"))
-    project_back(1, ("x",))
+    two_back("zl")
     trees[0].forward(("x", "y"))
     trees[0].forward(("x",))
     trees[1].forward(("x", "y"))
-    project_back(1, ("zl",))
-    project_back(0, ("zl",))
+    two_back()
     trees[1].forward(("zl", "y"))
-    project_back(1, ())
     trees[1].forward(("y",))
-    project_back(0, ())
+    trees[0].forward(("zl", "y"))
+    trees[1].forward(("zl", "x"))
 
     one = lane_iota(8)
     both = jnp.broadcast_to(r.bias_s[2:3, :], (8, 128))
@@ -1251,32 +1302,37 @@
     r.sums[3:4, :] = jnp.where(wide // 64 == head, key_gain, 0.0)
     same = jnp.sum(r.bias_s[0:1, :], axis=1, keepdims=True)
     every = jnp.sum(r.bias_s[1:2, :], axis=1, keepdims=True)
-    row_bias = jnp.where(wide == 2 * head, same, 0.0)
-    r.sums[4:5, :] = jnp.where(wide == 2 * head + 1, every - same, row_bias)
+    row_bias = jnp.where(wide == head, same, 0.0)
+    r.sums[4:5, :] = jnp.where(wide == 16 + head, every - same, row_bias)
     for k in range(8):
         r.s_acc[0, k] = r.sums[:, 128 * k : 128 * (k + 1)]
-    rounds = ("c", "x", "y", "zl", "zh")
-    s_step = net.send(r.s_acc.at[0], r.s_land.at[0], (rounds[0],))
-
-    def small_round(step, k):
-        step.wait_recv()
-        total = r.s_acc[k] + r.s_land[k]
-        if k == 4:
-            r.gsmall[...] = total
-            return None
-        r.s_acc[k + 1] = total
-        return net.send(r.s_acc.at[k + 1], r.s_land.at[k + 1], (rounds[k + 1],))
-
-    r.gw[...] = r.gh[:, :, :192].astype(bf).reshape(2, 8, 2, 32, 192)
+    s_steps = [net.send(r.s_acc.at[0], r.s_land.at[k], f) for k, f in enumerate(CHIP_FLIPS)]
+
+    r.gw[...] = r.gate[:, :, :192].astype(bf).reshape(2, 8, 2, 32, 192)
     w_zh = net.send(r.gw.at[1 - zh], r.w_land, ("zh",))
-    trees[0].forward(("zl", "y"))
-    trees[0].forward(("zl",))
-    trees[1].forward(("zl", "x"))
-    trees[1].forward(("zl",))
-    s_step = small_round(s_step, 0)
     trees[0].forward(("y",))
     trees[1].forward(("x",))
-    s_step = small_round(s_step, 1)
+    for copy in reduced[1]:
+        copy.wait_recv()
+    total = r.kept[4] + r.resid[...]
+    for k in range(3):
+        total = total + r.red_land[1, k].astype(f32)
+    r.out[...] = total.astype(bf)
+    total = tree_o.result()
+    r.kept[3, :32] = total[0]
+    r.kept[4, :32] = total[1]
+    r.o_half[...] = r.kept[4 - zh, :32].astype(bf)
+    o_step = net.send(r.o_half, r.o_half_land, ("zh",))
+    trees[0].forward(("zl",))
+    trees[1].forward(("zl",))
+    feed_sum(0)
+    feed_sum(1)
+    total = r.s_acc[0]
+    for k, copy in enumerate(s_steps):
+        copy.wait_recv()
+        total = total + r.s_land[k]
+    r.s_acc[1] = total
+    s_step = net.send(r.s_acc.at[1], r.s_land.at[7], ("zh",))
     w_zh.wait_recv()
     r.w_t[...] = (r.gw[zh].astype(f32) + r.w_land[...].astype(f32)).astype(bf)
     w_c = net.send(r.w_t.at[:, 1 - c], r.wp.at[:, c], ("c",))
@@ -1285,45 +1341,20 @@
     r.kept[2, :64] = trees[1].result()
     r.n_half[...] = r.kept[2 - zh, :64].astype(bf)
     n_step = net.send(r.n_half, r.n_half_land, ("zh",))
-    s_step = small_round(s_step, 2)
     w_c.wait_recv()
     w_steps = []
     for flips in CHIP_FLIPS:
         w_steps.append(net.send(r.wp.at[net.index(CHIPS, flips)], r.wl.at[my_chip], flips))
     r.wl[my_chip] = r.wp[my_chip]
-    total = tree_o.result()
-    r.kept[3, :32] = total[0]
-    r.kept[4, :32] = total[1]
-    r.o_half[...] = r.kept[4 - zh, :32].astype(bf)
-    o_step = net.send(r.o_half, r.o_half_land, ("zh",))
-    s_step = small_round(s_step, 3)
-
-    f_steps = []
-    for k in range(2):
-        y_near[k].wait_recv()
-        h_steps[k].wait_recv()
-        for j in range(4):
-            rows = r.gwgu[k, zh, j, y].astype(f32) + r.y_wgu[k, 0, j].astype(f32)
-            rows = rows + r.h_wgu_land[k, j].astype(f32)
-            r.gp[j, k, 0] = rows[:32].astype(bf)
-            r.gp[j, k, 1] = rows[32:].astype(bf)
-        for flips in GROUP_FLIPS:
-            f_steps.append(
-                net.send(
-                    r.gp.at[net.index(("zl", "x"), flips), k], r.gl.at[my_pair, k], flips
-                )
-            )
-        r.gl[my_pair, k] = r.gp[my_pair, k]
+    s_step.wait_recv()
+    r.s_acc[2] = r.s_acc[1] + r.s_land[7]
+    s_step = net.send(r.s_acc.at[2], r.s_land.at[8], ("c",))
+
     y_near[2].wait_recv()
     h_steps[2].wait_recv()
     r.gwdown[...] = r.gwd[zh, y].astype(f32) + r.y_wd[0].astype(f32) + r.h_wd_land[...].astype(f32)
-    f_c = []
-    for k in range(2):
-        for j in range(3):
-            f_steps[3 * k + j].wait_recv()
-        f_c.append(net.send(r.gl.at[:, k, 1 - c], r.f2.at[k, :, c], ("c",)))
-        r.f2[k, :, c] = r.gl[:, k, c]
-
+    feed_sibling(0)
+    feed_sibling(1)
     n_step.wait_recv()
     r.kept[2 - zh, :64] = r.n_half_land[...].astype(f32)
     for b in range(2):
@@ -1332,7 +1363,7 @@
         weighted = r.kept[1 + b, :64] * gain_attn
         mean = jnp.mean(weighted * value, axis=1, keepdims=True)
         back = scale * weighted - value * (scale * scale * scale) * mean
-        r.gtok[b] = (r.kept[7, 64 * b : 64 * (b + 1), :] + back).astype(bf)
+        r.gtok[b] = (r.kept[0, 64 * b : 64 * (b + 1), :] + back).astype(bf)
     for copy in w_steps:
         copy.wait_recv()
     for h in range(16):
@@ -1348,7 +1379,8 @@
                     out[:, 128 * idx : 128 * (idx + 1)] = r.f2[
                         k, pair, cc, :, 128 * part : 128 * (part + 1)
                     ].astype(f32)
-    small_round(s_step, 4)
+    s_step.wait_recv()
+    r.gsmall[...] = r.s_acc[2] + r.s_land[8]
     net.drain()
 
 
@@ -1374,9 +1406,43 @@
     )(*arrays)
 
 
+def give_out_kernel(small, *refs):
+    n = (len(refs) - 5) // 2
+    gains, bias = refs[2 * n : 2 * n + 4], refs[-1]
+    for source, dest in zip(refs[:n], refs[n : 2 * n]):
+        dest[...] = source[...]
+    rank = jnp.int32(0)
+    for name in AXES:
+        rank = rank * 2 + lax.axis_index(name)
+    held = small[rank // 4]
+    mine = held
+    for k in range(1, 4):
+        mine = jnp.where(rank % 4 == k, pltpu.roll(held, 128 - 32 * k, 1), mine)
+    for k, gain in enumerate(gains):
+        gain[...] = mine[k : k + 1, :32]
+    first = small[0]
+    bias[0:1, :] = first[4:5, :16]
+    bias[1:2, :] = pltpu.roll(first, 112, 1)[4:5, :16]
+
+
+def give_out(small, *large):
+    f32 = jnp.float32
+    vm = pl.BlockSpec(memory_space=pltpu.VMEM)
+    n = len(large)
+    return pl.pallas_call(
+        give_out_kernel,
+        out_shape=[jax.ShapeDtypeStruct(a.shape, a.dtype) for a in large]
+        + [jax.ShapeDtypeStruct((1, 32), f32)] * 4
+        + [jax.ShapeDtypeStruct((2, 16), f32)],
+        in_specs=[vm] * (n + 1),
+        out_specs=[vm] * (n + 5),
+        name="give_out",
+    )(small, *large)
+
+
 def frequencies():
     index = np.arange(32, dtype=np.float32)
-    return np.broadcast_to((THETA ** (-2.0 * index / 64.0)).astype(np.float32)[:, None], (32, 128))
+    return (THETA ** (-2.0 * index / 64.0)).astype(np.float32)[:, None]
 
 
 def on_device_cube(
@@ -1396,15 +1462,13 @@
     variate,
     times,
 ):
-    rank = jnp.int32(0)
-    for name in AXES:
-        rank = rank * 2 + lax.axis_index(name)
-    gains = jnp.concatenate([norm_attn, norm_ffn, q_gain, k_gain]).astype(jnp.float32)
-    out, gtok, gwqkv, gwout, gwgate, gwup, gwdown, small = layer(
-        doc_lengths, var_bias, tokens, cotangent, w_qkv, w_out, w_gate, w_up, w_down,
-        gains.reshape(1, 128), variate, times, jnp.asarray(frequencies()),
+    results = layer(
+        doc_lengths, var_bias.T, tokens, cotangent, w_qkv, w_out, w_gate, w_up, w_down,
+        *(gain.reshape(1, 32) for gain in (norm_attn, norm_ffn, q_gain, k_gain)),
+        variate, times, jnp.asarray(frequencies()),
     )
-    tile = lax.dynamic_slice(small, (rank // 4, 0, (rank % 4) * 32), (1, 8, 32))[0]
+    *large, small = results
+    out, gtok, gwqkv, gwout, gwgate, gwup, gwdown, *gains, bias = give_out(small, *large)
     return (
         out.reshape(2, 64, 1024),
         gtok,
@@ -1413,11 +1477,8 @@
         gwgate,
         gwup,
         gwdown,
-        tile[0],
-        tile[1],
-        tile[2],
-        tile[3],
-        small[0, 4, :32].reshape(16, 2),
+        *(gain.reshape(32) for gain in gains),
+        bias.T,
     )
 
 

time: 254 us -> 216 us (0.85)
  Pallas kernels: 239 us -> 215 us
  local copies, waits for them, and re-layouts: 12.2 us -> 0 us
    pallas_call x1, Pallas kernels: 239 us -> 212 us  [layer(): pl.pallas_call(layer_kernel, out_shape=[jax.ShapeDtypeStruct(*spec) for s...]
    unnamed x33 -> x0, local copies, waits for them, and re-layouts: 9.42 us -> none
    pallas_call x0 -> x1, Pallas kernels: none -> 3.24 us  [give_out(): pl.pallas_call(give_out_kernel, out_shape=[jax.ShapeDtypeStruct(a.shape,...]
where the time goes in v3:
time: 216 us
  Pallas kernels  215 us (100%)
    pallas_call x1, Pallas kernels, layer(): pl.pallas_call(layer_kernel, out_shape=[jax.ShapeDtypeStruct(*spec) for s...  212 us

profile of v3, /device:TPU:0, one launch (start us, length us, event | category | flops | bytes accessed | tf_op | source)
XLA Modules:
  0.0 216.3 jit_solution(17356673982438657686)
XLA Ops:
  0.7 212.2 %layer.1 = (bf16[128,1024]{1,0:T(8,128)(2,1)}, bf16[2,64,1024]{2,1,0:T(8,128)(2,1)}, f32[32,3072]{1,0:T(8,128)}, f32[32,1024]{1,0:T(8,128)}, f32[32,4096]{1,0:T(...) custom-call(s32[2,8]{1,0:T(2,128)} %refs_0_.1, f32[2,16]{1,0:T(2,128)} %bitcast.11, ...), custom_call_target="tpu_custom_call" | custom-call | tf_op jit(solution)/shard_map/layer/pallas_call | solution.py:1391
  212.9 3.2 %give_out.1 = (bf16[128,1024]{1,0:T(8,128)(2,1)}, bf16[2,64,1024]{2,1,0:T(8,128)(2,1)}, f32[32,3072]{1,0:T(8,128)}, f32[32,1024]{1,0:T(8,128)}, f32[32,4096]{1,0...) custom-call(f32[8,8,128]{2,1,0:T(8,128)} %get-tuple-element.32.small, ...), custom_call_target="tpu_custom_call" | custom-call | tf_op jit(solution)/shard_map/give_out/pallas_call | solution.py:1432

commit v4 on v3

--- a/solution.py
+++ b/solution.py
@@ -611,8 +611,7 @@
         "att": ((16, 2, 64, 64), bf),
         "lb": ((16, 64, 64), bf),
         "ap": ((2, 8, 64, 128), bf),
-        "at2": ((8, 2, 64, 128), bf),
-        "at3": ((8, 64, 128), bf),
+        "at2": ((2, 8, 64, 128), bf),
         "att_s": ((128, 1024), bf),
         "resid": ((128, 1024), f32),
         "n2": ((8, 2, 64, 1024), bf),
@@ -627,7 +626,6 @@
         "red_land": ((2, 3, 128, 1024), bf),
         "branch": ((128, 1024), bf),
         "ga3": ((2, 8, 64, 128), bf),
-        "ga2": ((2, 8, 64, 128), bf),
         "ag1": ((2, 8, 64, 128), bf),
         "gatt": ((16, 2, 64, 64), bf),
         "gwgu": ((2, 2, 4, 2, 64, 512), bf),
@@ -670,7 +668,8 @@
     mine, in_half = net.index(AXES), net.index(AXES[1:])
     my_chip, my_pair = net.index(CHIPS), net.index(("zl", "x"))
     head = in_half
-    net.barrier(CHIP_FLIPS + [("c",), ("zh",)])
+    far_flips = [("zh",) + flips for flips in [()] + CHIP_FLIPS]
+    net.barrier(CHIP_FLIPS + [("c",)] + far_flips)
 
     def x_region(part):
         def region(flips):
@@ -702,11 +701,12 @@
                 col, lane = 128 * idx, 128 * part
                 r.gp[pair, 0, cc, :, lane : lane + 128] = r.wgate[:, col : col + 128]
                 r.gp[pair, 1, cc, :, lane : lane + 128] = r.wup[:, col : col + 128]
-    g_arrive = []
-    for flips in GROUP_FLIPS:
-        g_arrive.append(
-            net.send(r.gp.at[net.index(("zl", "x"), flips)], r.gl.at[my_pair], flips)
-        )
+
+    def g_send(flips):
+        return net.send(r.gp.at[net.index(("zl", "x"), flips)], r.gl.at[my_pair], flips)
+
+    g_arrive = [g_send(("x",))]
+    wd_y = net.send(r.wdown, r.wd.at[zh, y], ("y",))
     r.sm[zh, zl, x, y, c] = r.tile[...]
     r.wl[my_chip] = r.wp[my_chip]
     r.x[mine] = r.tok[zh]
@@ -716,49 +716,37 @@
     r.wo[zh, in_half] = r.wout[...]
 
     sm_step.wait_recv()
-    sm_step = net.send(r.sm.at[:, zl, x, y, c], r.sm.at[:, zl, x, y, c], ("c",))
+    sm_step = net.send(r.sm.at[:, zl, x, y, c], r.sm.at[:, zl, x, y, c], ("x",))
     for copy in w_arrive:
         copy.wait_recv()
     w_c = net.send(r.wl.at[:, 1 - c], r.wh.at[zh, :, c], ("c",))
     r.wh[zh, :, c] = r.wl[:, c]
     sm_step.wait_recv()
-    sm_step = net.send(r.sm.at[:, zl, x, y], r.sm.at[:, zl, x, y], ("y",))
+    sm_step = net.send(r.sm.at[:, zl, :, y, c], r.sm.at[:, zl, :, y, c], ("y",))
     x_own.take("zl")
     x_own.take("y")
     w_c.wait_recv()
-    w_zh = net.send(r.wh.at[zh], r.wh.at[zh], ("zh",))
     swap.wait_recv()
     x_far.push(())
+    w_zh = net.send(r.wh.at[zh], r.wh.at[zh], ("zh",))
+    sm_step.wait_recv()
+    sm_step = net.send(r.sm.at[:, zl, :, :, c], r.sm.at[:, zl, :, :, c], ("zl",))
+    g_arrive += [g_send(("zl",)), g_send(("zl", "x"))]
     wo_zh = net.send(r.wout, r.wo.at[zh, in_half], ("zh",))
-    sm_step.wait_recv()
-    sm_step = net.send(r.sm.at[:, zl, x], r.sm.at[:, zl, x], ("zl",))
     x_own.take("zl", "y")
     x_own.take("x")
     x_far.take("zl")
     sm_step.wait_recv()
-    sm_step = net.send(r.sm.at[:, :, x], r.sm.at[:, :, x], ("x",))
+    sm_step = net.send(r.sm.at[:, :, :, :, c], r.sm.at[:, :, :, :, c], ("c",))
+
     def g_piece(k, half):
         return r.wgu.at[k // 2, half, pl.ds(2 * (k % 2), 2), y]
 
     g_c, g_zh, g_y, g_fwd = [], [], [], []
 
-    for copy in g_arrive:
-        copy.wait_recv()
-    for k in range(2):
-        g_c.append(net.send(r.gl.at[:, k, 1 - c], r.wgu.at[k, zh, :, y, c], ("c",)))
-        r.wgu[k, zh, :, y, c] = r.gl[:, k, c]
     x_far.take("x")
     x_own.take("zl", "x")
     x_own.take("y", "x")
-    wo_zh.wait_recv()
-    wo_tree.push(())
-    for k in range(4):
-        if k % 2 == 0:
-            g_c[k // 2].wait_recv()
-        g_zh.append(net.send(g_piece(k, zh), g_piece(k, zh), ("zh",)))
-    x_far.take("zl", "x")
-    for k in range(4):
-        g_y.append(net.send(g_piece(k, zh), g_piece(k, zh), ("y",)))
     sm_step.wait_recv()
 
     lane8 = lane_iota(8)
@@ -821,6 +809,22 @@
         cosine, sine = jnp.cos(angle), jnp.sin(angle)
         r.cs[col, :] = jnp.concatenate([cosine, cosine, -sine, sine], axis=0).T
 
+    x_far.take("zl", "x")
+    for copy in g_arrive:
+        copy.wait_recv()
+    for k in range(2):
+        g_c.append(net.send(r.gl.at[:, k, 1 - c], r.wgu.at[k, zh, :, y, c], ("c",)))
+        r.wgu[k, zh, :, y, c] = r.gl[:, k, c]
+    wo_zh.wait_recv()
+    wo_tree.push(())
+    for k in range(4):
+        if k % 2 == 0:
+            g_c[k // 2].wait_recv()
+        g_zh.append(net.send(g_piece(k, zh), g_piece(k, zh), ("zh",)))
+    for k in range(4):
+        g_y.append(net.send(g_piece(k, zh), g_piece(k, zh), ("y",)))
+    gf_tree.push((), r.cot)
+
     lane = lane_iota(ROW_BLOCK)
 
     def arrived(part, *flips):
@@ -895,6 +899,7 @@
 
     step = net.send(r.att.at[:, 1 - c], r.lb, ("c",))
     wo_tree.take("zl", "y")
+    g_pass(1)
     step.wait_recv()
     lane64 = lane_iota(64)
 
@@ -905,11 +910,12 @@
         r.ap[i // 8, i % 8] = jnp.where((lane64 < 64) == (c == 0), own, other)
 
     arrive = []
-    for flips in CHIP_FLIPS:
+    for flips in far_flips + CHIP_FLIPS:
+        z_part = 1 - zh if "zh" in flips else zh
         arrive.append(
-            net.send(r.ap.at[:, net.index(CHIPS, flips)], r.at2.at[my_chip], flips)
-        )
-    r.at2[my_chip] = r.ap[:, my_chip]
+            net.send(r.ap.at[z_part, net.index(CHIPS, flips)], r.at2.at[zh, my_chip], flips)
+        )
+    r.at2[zh, my_chip] = r.ap[zh, my_chip]
 
     def w_down():
         return r.wd[...].reshape(512, 1024)
@@ -922,24 +928,19 @@
 
     for copy in arrive:
         copy.wait_recv()
-    step = net.send(r.at2.at[:, 1 - zh], r.at3, ("zh",))
     wd_zh = net.send(r.wdown, r.wd.at[zh, y], ("zh",))
-    for k in range(8):
-        r.att_s[pl.ds(pl.multiple_of(zh * 64, 64), 64), 128 * k : 128 * (k + 1)] = r.at2[k, zh]
-    gf_tree.push((), r.cot)
-    g_pass(1)
     g_pass(2)
-    wd_y = net.send(r.wdown, r.wd.at[zh, y], ("y",))
+    gf_tree.take("zl")
+    for b in range(2):
+        for k in range(8):
+            r.att_s[64 * b : 64 * (b + 1), 128 * k : 128 * (k + 1)] = r.at2[b, k]
+    g_pass(3)
     wo_tree.take("x")
     wo_tree.take("y", "x")
     wo_tree.take("zl", "x")
     wo_tree.take("zl", "y", "x")
-    g_pass(3)
     for flips in [(), ("y",), ("zl",), ("zl", "y"), ("x",), ("y", "x"), ("zl", "x"), ("zl", "y", "x")]:
         wo_tree.ready(*flips)
-    step.wait_recv()
-    for k in range(8):
-        r.att_s[pl.ds(pl.multiple_of(64 - zh * 64, 64), 64), 128 * k : 128 * (k + 1)] = r.at3[k]
 
     resid = r.tok[...].reshape(128, 1024).astype(f32)
     resid = resid + jnp.dot(r.att_s[...], w_o(), preferred_element_type=f32)
@@ -1004,12 +1005,11 @@
             )
 
     pairs = [my_pair] + [net.index(("zl", "x"), flips) for flips in GROUP_FLIPS]
-    wd_zh.wait_recv()
-    wd_fwd = net.send(r.wd.at[1 - zh, y], r.wd.at[1 - zh, y], ("y",))
-    gf_tree.take("zl")
     for copy in g_y + g_fwd:
         copy.wait_recv()
     to_sibling[0].wait_recv()
+    wd_zh.wait_recv()
+    wd_fwd = net.send(r.wd.at[1 - zh, y], r.wd.at[1 - zh, y], ("y",))
     for k in range(3):
         from_chips[k].wait_recv()
         at = 2 * pairs[k + 1] + c
@@ -1078,7 +1078,6 @@
             .astype(bf)
             .reshape(2, 2, 128, 512)
         )
-    net.settle(list(halves.values()))
 
     h_steps = []
 
@@ -1111,15 +1110,13 @@
     for k in range(8):
         for b in range(2):
             r.ga3[b, k] = grad_att[64 * b : 64 * (b + 1), 128 * k : 128 * (k + 1)]
-    step = net.send(r.ga3.at[1 - zh], r.ga2.at[zh], ("zh",))
-    r.ga2[zh] = r.ga3[zh]
-    step.wait_recv()
     arrive = []
-    for flips in CHIP_FLIPS:
+    for flips in far_flips + CHIP_FLIPS:
+        z_part = 1 - zh if "zh" in flips else zh
         arrive.append(
-            net.send(r.ga2.at[:, net.index(CHIPS, flips)], r.ag1.at[:, my_chip], flips)
-        )
-    r.ag1[:, my_chip] = r.ga2[:, my_chip]
+            net.send(r.ga3.at[z_part, net.index(CHIPS, flips)], r.ag1.at[zh, my_chip], flips)
+        )
+    r.ag1[zh, my_chip] = r.ga3[zh, my_chip]
     for j in range(8):
         cols = slice(128 * j, 128 * (j + 1))
         r.gwo[j // 4, 2 * (j % 4) : 2 * (j % 4) + 2] = (
@@ -1141,10 +1138,7 @@
         finish_half(1, k)
     step = net.send(r.lb, r.gatt.at[:, c], ("c",))
     half_gate_up(0)
-    half_gate_up(1)
     y_far.append(net.send(r.gwd.at[1 - zh, 1 - y], r.y_wd.at[1], ("y",)))
-    y_near = [net.send(r.gwgu.at[k, zh, :, 1 - y], r.y_wgu.at[k, 0], ("y",)) for k in range(2)]
-    y_near.append(net.send(r.gwd.at[zh, 1 - y], r.y_wd.at[0], ("y",)))
     r.feat[...] = jnp.zeros_like(r.feat)
     r.bias_s[...] = jnp.zeros_like(r.bias_s)
     r.gate[...] = jnp.zeros_like(r.gate)
@@ -1203,13 +1197,15 @@
         r.bias_s[0:1, :] += jnp.sum(same, axis=0, keepdims=True)
         r.bias_s[1:2, :] += jnp.sum(every, axis=0, keepdims=True)
 
-    half_down()
-    pl.loop(0, 2)(attend_back)
+    half_gate_up(1)
+    pl.loop(0, 1)(attend_back)
+    y_near = [net.send(r.gwgu.at[k, zh, :, 1 - y], r.y_wgu.at[k, 0], ("y",)) for k in range(2)]
+    y_near.append(net.send(r.gwd.at[zh, 1 - y], r.y_wd.at[0], ("y",)))
     for mask in tree_o.masks[:4]:
         tree_o.forward(mask)
+    half_down()
+    pl.loop(1, 2)(attend_back)
     pl.loop(2, 4)(attend_back)
-    tree_o.forward(("zl", "y"))
-    tree_o.forward(("zl",))
 
     def token_tree(part, dims):
         return Reduce(
@@ -1276,12 +1272,15 @@
             tree.begin(flips)
             tree.begin(flips + ("y",))
 
+    net.settle(list(halves.values()))
+    feed_sum(0)
     two_back("zl", "x")
-    tree_o.forward(("y",))
     two_back("x")
     trees[0].forward(("zl", "x", "y"))
     trees[0].forward(("zl", "x"))
     trees[1].forward(("zl", "x", "y"))
+    tree_o.forward(("zl", "y"))
+    tree_o.forward(("zl",))
     two_back("zl")
     trees[0].forward(("x", "y"))
     trees[0].forward(("x",))
@@ -1312,21 +1311,24 @@
     w_zh = net.send(r.gw.at[1 - zh], r.w_land, ("zh",))
     trees[0].forward(("y",))
     trees[1].forward(("x",))
+    tree_o.forward(("y",))
     for copy in reduced[1]:
         copy.wait_recv()
     total = r.kept[4] + r.resid[...]
     for k in range(3):
         total = total + r.red_land[1, k].astype(f32)
     r.out[...] = total.astype(bf)
+    trees[0].forward(("zl",))
+    trees[1].forward(("zl",))
+    r.kept[1, :64] = trees[0].result()
+    r.kept[2, :64] = trees[1].result()
+    r.n_half[...] = r.kept[2 - zh, :64].astype(bf)
+    n_step = net.send(r.n_half, r.n_half_land, ("zh",))
     total = tree_o.result()
     r.kept[3, :32] = total[0]
     r.kept[4, :32] = total[1]
     r.o_half[...] = r.kept[4 - zh, :32].astype(bf)
     o_step = net.send(r.o_half, r.o_half_land, ("zh",))
-    trees[0].forward(("zl",))
-    trees[1].forward(("zl",))
-    feed_sum(0)
-    feed_sum(1)
     total = r.s_acc[0]
     for k, copy in enumerate(s_steps):
         copy.wait_recv()
@@ -1337,10 +1339,7 @@
     r.w_t[...] = (r.gw[zh].astype(f32) + r.w_land[...].astype(f32)).astype(bf)
     w_c = net.send(r.w_t.at[:, 1 - c], r.wp.at[:, c], ("c",))
     r.wp[:, c] = r.w_t[:, c]
-    r.kept[1, :64] = trees[0].result()
-    r.kept[2, :64] = trees[1].result()
-    r.n_half[...] = r.kept[2 - zh, :64].astype(bf)
-    n_step = net.send(r.n_half, r.n_half_land, ("zh",))
+    feed_sum(1)
     w_c.wait_recv()
     w_steps = []
     for flips in CHIP_FLIPS:
@@ -1349,7 +1348,6 @@
     s_step.wait_recv()
     r.s_acc[2] = r.s_acc[1] + r.s_land[7]
     s_step = net.send(r.s_acc.at[2], r.s_land.at[8], ("c",))
-
     y_near[2].wait_recv()
     h_steps[2].wait_recv()
     r.gwdown[...] = r.gwd[zh, y].astype(f32) + r.y_wd[0].astype(f32) + r.h_wd_land[...].astype(f32)

time: 216 us -> 196 us (0.907)
  Pallas kernels: 215 us -> 195 us
    pallas_call x1, Pallas kernels: 212 us -> 192 us  [layer(): pl.pallas_call(layer_kernel, out_shape=[jax.ShapeDtypeStruct(*spec) for s...]
where the time goes in v4:
time: 196 us
  Pallas kernels  195 us (99%)
    pallas_call x1, Pallas kernels, layer(): pl.pallas_call(layer_kernel, out_shape=[jax.ShapeDtypeStruct(*spec) for s...  192 us

profile of v4, /device:TPU:0, one launch (start us, length us, event | category | flops | bytes accessed | tf_op | source)
XLA Modules:
  0.0 196.1 jit_solution(5400321985396689774)
XLA Ops:
  0.7 192.1 %layer.1 = (bf16[128,1024]{1,0:T(8,128)(2,1)}, bf16[2,64,1024]{2,1,0:T(8,128)(2,1)}, f32[32,3072]{1,0:T(8,128)}, f32[32,1024]{1,0:T(8,128)}, f32[32,4096]{1,0:T(...) custom-call(s32[2,8]{1,0:T(2,128)} %refs_0_.1, f32[2,16]{1,0:T(2,128)} %bitcast.11, ...), custom_call_target="tpu_custom_call" | custom-call | tf_op jit(solution)/shard_map/layer/pallas_call | solution.py:1389
  192.7 3.2 %give_out.1 = (bf16[128,1024]{1,0:T(8,128)(2,1)}, bf16[2,64,1024]{2,1,0:T(8,128)(2,1)}, f32[32,3072]{1,0:T(8,128)}, f32[32,1024]{1,0:T(8,128)}, f32[32,4096]{1,0...) custom-call(f32[8,8,128]{2,1,0:T(8,128)} %get-tuple-element.32.small, ...), custom_call_target="tpu_custom_call" | custom-call | tf_op jit(solution)/shard_map/give_out/pallas_call | solution.py:1430

commit v5 on v4

--- a/solution.py
+++ b/solution.py
@@ -389,7 +389,7 @@
 
 AXES = ("zh", "zl", "x", "y", "c")
 CHIPS = ("zl", "x", "y")
-VMEM_BYTES = 62 * 2**20
+VMEM_BYTES = 63 * 2**20
 ROW_BLOCK = 256
 SPAN = 512
 LAST = (((1,), (1,)), ((), ()))
@@ -747,6 +747,7 @@
     x_far.take("x")
     x_own.take("zl", "x")
     x_own.take("y", "x")
+    x_far.take("y")
     sm_step.wait_recv()
 
     lane8 = lane_iota(8)
@@ -809,6 +810,8 @@
         cosine, sine = jnp.cos(angle), jnp.sin(angle)
         r.cs[col, :] = jnp.concatenate([cosine, cosine, -sine, sine], axis=0).T
 
+    x_own.take("zl", "y", "x")
+    x_far.take("zl", "y")
     x_far.take("zl", "x")
     for copy in g_arrive:
         copy.wait_recv()
@@ -855,9 +858,6 @@
     w_zh.wait_recv()
     arrived(0)
     arrived(0, "zl")
-    x_own.take("zl", "y", "x")
-    x_far.take("y")
-    x_far.take("zl", "y")
     arrived(0, "x")
     arrived(0, "zl", "x")
     pl.loop(0, 4)(project)
@@ -894,11 +894,11 @@
 
     pl.loop(0, 2)(attend)
     wo_tree.take("y")
-    g_pass(0)
     pl.loop(2, 4)(attend)
 
     step = net.send(r.att.at[:, 1 - c], r.lb, ("c",))
     wo_tree.take("zl", "y")
+    g_pass(0)
     g_pass(1)
     step.wait_recv()
     lane64 = lane_iota(64)
@@ -1008,14 +1008,14 @@
     for copy in g_y + g_fwd:
         copy.wait_recv()
     to_sibling[0].wait_recv()
-    wd_zh.wait_recv()
-    wd_fwd = net.send(r.wd.at[1 - zh, y], r.wd.at[1 - zh, y], ("y",))
     for k in range(3):
         from_chips[k].wait_recv()
         at = 2 * pairs[k + 1] + c
         to_sibling.append(net.send(r.n2.at[at], r.n2.at[at], ("c",)))
         if k == 0:
             to_sibling[1].wait_recv()
+            wd_zh.wait_recv()
+            wd_fwd = net.send(r.wd.at[1 - zh, y], r.wd.at[1 - zh, y], ("y",))
             pl.loop(0, 2)(lambda slot: feed(pair_at(slot)))
     gf_tree.take("x")
     gf_tree.take("zl", "x")
@@ -1035,14 +1035,17 @@
         feed_back(pair)
         keep_half(slot, back_product(pair))
 
-    pl.loop(2, 4)(feed_both)
+    pl.loop(3, 4)(feed_both)
+    share(0, 3)
+    pl.loop(2, 3)(feed_both)
     share(0, 2)
-    share(0, 3)
-    pl.loop(0, 2)(feed_both)
     finish_half(0, 3)
+    pl.loop(1, 2)(feed_both)
+    share(0, 1)
     finish_half(0, 2)
-    share(0, 1)
+    pl.loop(0, 1)(feed_both)
     share(0, 0)
+    finish_half(0, 1)
 
     @pl.loop(0, 2)
     def _(k):
@@ -1056,7 +1059,6 @@
             .astype(bf)
             .reshape(2, 4, 2, 64, 512)
         )
-    finish_half(0, 1)
     y_far = [net.send(r.gwgu.at[k, 1 - zh, :, 1 - y], r.y_wgu.at[k, 1], ("y",)) for k in range(2)]
     finish_half(0, 0)
 
@@ -1179,15 +1181,13 @@
         def one_chunk(k, total):
             col = pl.ds(pl.multiple_of(k * SPAN, SPAN), SPAN)
             key = r.kf[col, :]
-            scores = lax.dot_general(query, key, LAST, preferred_element_type=f32)
+            scores = lax.dot_general(key, query, LAST, preferred_element_type=f32)
             probs = jnp.exp(scores)
-            centred = lax.dot_general(grad, r.vf[col, :], LAST, preferred_element_type=f32)
+            centred = lax.dot_general(r.vf[col, :], grad, LAST, preferred_element_type=f32)
             back = (probs * centred).astype(bf)
-            grad_v[col, :] += lax.dot_general(
-                probs.astype(bf), grad, FIRST, preferred_element_type=f32
-            )
-            grad_k[col, :] += lax.dot_general(back, query, FIRST, preferred_element_type=f32)
-            return total + jnp.dot(back, key, preferred_element_type=f32)
+            grad_v[col, :] += jnp.dot(probs.astype(bf), grad, preferred_element_type=f32)
+            grad_k[col, :] += jnp.dot(back, query, preferred_element_type=f32)
+            return total + lax.dot_general(back, key, FIRST, preferred_element_type=f32)
 
         total = lax.fori_loop(0, 2048 // SPAN, one_chunk, jnp.zeros((SPAN, 128), f32))
         r.gq[row, :] = (total * 0.125).astype(bf)
@@ -1207,17 +1207,17 @@
     pl.loop(1, 2)(attend_back)
     pl.loop(2, 4)(attend_back)
 
-    def token_tree(part, dims):
+    def token_tree(part, half, dims):
         return Reduce(
             net,
             dims,
-            lambda mask, core: r.x.at[part * 16 + 2 * net.index(CHIPS, mask) + core],
+            lambda mask, core: r.x.at[half * 16 + 2 * net.index(CHIPS, mask) + core],
             lambda slot: r.landed.at[slot, part],
             lambda slot: r.sent.at[slot, part],
             lambda slot: r.n2.at[slot, part],
         )
 
-    trees = [token_tree(0, ("x", "y", "zl")), token_tree(1, ("y", "x", "zl"))]
+    trees = [token_tree(0, 1 - zh, ("x", "y", "zl")), token_tree(1, zh, ("y", "x", "zl"))]
 
     def project_back(part, where):
         start = (part * 4 + where) * ROW_BLOCK
@@ -1273,8 +1273,8 @@
             tree.begin(flips + ("y",))
 
     net.settle(list(halves.values()))
+    two_back("zl", "x")
     feed_sum(0)
-    two_back("zl", "x")
     two_back("x")
     trees[0].forward(("zl", "x", "y"))
     trees[0].forward(("zl", "x"))
@@ -1286,9 +1286,9 @@
     trees[0].forward(("x",))
     trees[1].forward(("x", "y"))
     two_back()
+    trees[0].forward(("zl", "y"))
     trees[1].forward(("zl", "y"))
     trees[1].forward(("y",))
-    trees[0].forward(("zl", "y"))
     trees[1].forward(("zl", "x"))
 
     one = lane_iota(8)
@@ -1310,6 +1310,7 @@
     r.gw[...] = r.gate[:, :, :192].astype(bf).reshape(2, 8, 2, 32, 192)
     w_zh = net.send(r.gw.at[1 - zh], r.w_land, ("zh",))
     trees[0].forward(("y",))
+    trees[0].forward(("zl",))
     trees[1].forward(("x",))
     tree_o.forward(("y",))
     for copy in reduced[1]:
@@ -1318,33 +1319,31 @@
     for k in range(3):
         total = total + r.red_land[1, k].astype(f32)
     r.out[...] = total.astype(bf)
-    trees[0].forward(("zl",))
     trees[1].forward(("zl",))
-    r.kept[1, :64] = trees[0].result()
-    r.kept[2, :64] = trees[1].result()
-    r.n_half[...] = r.kept[2 - zh, :64].astype(bf)
+    w_zh.wait_recv()
+    r.w_t[...] = (r.gw[zh].astype(f32) + r.w_land[...].astype(f32)).astype(bf)
+    w_c = net.send(r.w_t.at[:, 1 - c], r.wp.at[:, c], ("c",))
+    r.wp[:, c] = r.w_t[:, c]
+    r.n_half[...] = trees[0].result().astype(bf)
     n_step = net.send(r.n_half, r.n_half_land, ("zh",))
-    total = tree_o.result()
-    r.kept[3, :32] = total[0]
-    r.kept[4, :32] = total[1]
-    r.o_half[...] = r.kept[4 - zh, :32].astype(bf)
-    o_step = net.send(r.o_half, r.o_half_land, ("zh",))
+    feed_sum(1)
     total = r.s_acc[0]
     for k, copy in enumerate(s_steps):
         copy.wait_recv()
         total = total + r.s_land[k]
     r.s_acc[1] = total
     s_step = net.send(r.s_acc.at[1], r.s_land.at[7], ("zh",))
-    w_zh.wait_recv()
-    r.w_t[...] = (r.gw[zh].astype(f32) + r.w_land[...].astype(f32)).astype(bf)
-    w_c = net.send(r.w_t.at[:, 1 - c], r.wp.at[:, c], ("c",))
-    r.wp[:, c] = r.w_t[:, c]
-    feed_sum(1)
     w_c.wait_recv()
     w_steps = []
     for flips in CHIP_FLIPS:
         w_steps.append(net.send(r.wp.at[net.index(CHIPS, flips)], r.wl.at[my_chip], flips))
     r.wl[my_chip] = r.wp[my_chip]
+    total = tree_o.result()
+    r.kept[3, :32] = total[0]
+    r.kept[4, :32] = total[1]
+    r.o_half[...] = r.kept[4 - zh, :32].astype(bf)
+    o_step = net.send(r.o_half, r.o_half_land, ("zh",))
+    r.kept[1 + zh, :64] = trees[1].result()
     s_step.wait_recv()
     r.s_acc[2] = r.s_acc[1] + r.s_land[7]
     s_step = net.send(r.s_acc.at[2], r.s_land.at[8], ("c",))

time: 196 us -> 192 us (0.980)
  Pallas kernels: 195 us -> 191 us
    pallas_call x1, Pallas kernels: 192 us -> 188 us  [layer(): pl.pallas_call(layer_kernel, out_shape=[jax.ShapeDtypeStruct(*spec) for s...]
where the time goes in v5:
time: 192 us
  Pallas kernels  191 us (99%)
    pallas_call x1, Pallas kernels, layer(): pl.pallas_call(layer_kernel, out_shape=[jax.ShapeDtypeStruct(*spec) for s...  188 us

profile of v5, /device:TPU:0, one launch (start us, length us, event | category | flops | bytes accessed | tf_op | source)
XLA Modules:
  0.0 192.1 jit_solution(16080489570894344694)
XLA Ops:
  0.7 188.0 %layer.1 = (bf16[128,1024]{1,0:T(8,128)(2,1)}, bf16[2,64,1024]{2,1,0:T(8,128)(2,1)}, f32[32,3072]{1,0:T(8,128)}, f32[32,1024]{1,0:T(8,128)}, f32[32,4096]{1,0:T(...) custom-call(s32[2,8]{1,0:T(2,128)} %refs_0_.1, f32[2,16]{1,0:T(2,128)} %bitcast.11, ...), custom_call_target="tpu_custom_call" | custom-call | tf_op jit(solution)/shard_map/layer/pallas_call | solution.py:1388
  188.7 3.2 %give_out.1 = (bf16[128,1024]{1,0:T(8,128)(2,1)}, bf16[2,64,1024]{2,1,0:T(8,128)(2,1)}, f32[32,3072]{1,0:T(8,128)}, f32[32,1024]{1,0:T(8,128)}, f32[32,4096]{1,0...) custom-call(f32[8,8,128]{2,1,0:T(8,128)} %get-tuple-element.32.small, ...), custom_call_target="tpu_custom_call" | custom-call | tf_op jit(solution)/shard_map/give_out/pallas_call | solution.py:1429

commit v6 on v5

--- a/solution.py
+++ b/solution.py
@@ -882,7 +882,7 @@
             weights = jnp.exp(scores).astype(bf)
             return total + jnp.dot(weights, r.vf[col, :], preferred_element_type=f32)
 
-        total = lax.fori_loop(0, 2048 // SPAN, one_chunk, jnp.zeros((SPAN, 128), f32))
+        total = lax.fori_loop(0, 2048 // SPAN, one_chunk, jnp.zeros((SPAN, 128), f32), unroll=2)
         weight = total[:, 64:65]
         result = total / weight
         r.kept_o[row, :] = jnp.where(lane_span < 64, result, jnp.log(weight))
@@ -903,7 +903,7 @@
     step.wait_recv()
     lane64 = lane_iota(64)
 
-    @pl.loop(0, 16)
+    @pl.loop(0, 16, unroll=4)
     def _(i):
         own = jnp.concatenate([r.att[i, c]] * 2, axis=1)
         other = jnp.concatenate([r.lb[i]] * 2, axis=1)
@@ -1189,7 +1189,7 @@
             grad_k[col, :] += jnp.dot(back, query, preferred_element_type=f32)
             return total + lax.dot_general(back, key, FIRST, preferred_element_type=f32)
 
-        total = lax.fori_loop(0, 2048 // SPAN, one_chunk, jnp.zeros((SPAN, 128), f32))
+        total = lax.fori_loop(0, 2048 // SPAN, one_chunk, jnp.zeros((SPAN, 128), f32), unroll=2)
         r.gq[row, :] = (total * 0.125).astype(bf)
         marks = r.kf[row, :].astype(f32)
         same = jnp.where((lane_span >= 80) & (lane_span < 88), total * marks, 0.0)
@@ -1274,11 +1274,11 @@
 
     net.settle(list(halves.values()))
     two_back("zl", "x")
-    feed_sum(0)
     two_back("x")
     trees[0].forward(("zl", "x", "y"))
     trees[0].forward(("zl", "x"))
     trees[1].forward(("zl", "x", "y"))
+    feed_sum(0)
     tree_o.forward(("zl", "y"))
     tree_o.forward(("zl",))
     two_back("zl")

time: 192 us -> 192 us (level)
  no operation moved by 1% of the time
where the time goes in v6:
time: 192 us
  Pallas kernels  191 us (99%)
    pallas_call x1, Pallas kernels, layer(): pl.pallas_call(layer_kernel, out_shape=[jax.ShapeDtypeStruct(*spec) for s...  188 us

profile of v6, /device:TPU:0, one launch (start us, length us, event | category | flops | bytes accessed | tf_op | source)
XLA Modules:
  0.0 192.2 jit_solution(6685014801556857764)
XLA Ops:
  0.7 188.1 %layer.1 = (bf16[128,1024]{1,0:T(8,128)(2,1)}, bf16[2,64,1024]{2,1,0:T(8,128)(2,1)}, f32[32,3072]{1,0:T(8,128)}, f32[32,1024]{1,0:T(8,128)}, f32[32,4096]{1,0:T(...) custom-call(s32[2,8]{1,0:T(2,128)} %refs_0_.1, f32[2,16]{1,0:T(2,128)} %bitcast.11, ...), custom_call_target="tpu_custom_call" | custom-call | tf_op jit(solution)/shard_map/layer/pallas_call | solution.py:1388
  188.7 3.2 %give_out.1 = (bf16[128,1024]{1,0:T(8,128)(2,1)}, bf16[2,64,1024]{2,1,0:T(8,128)(2,1)}, f32[32,3072]{1,0:T(8,128)}, f32[32,1024]{1,0:T(8,128)}, f32[32,4096]{1,0...) custom-call(f32[8,8,128]{2,1,0:T(8,128)} %get-tuple-element.32.small, ...), custom_call_target="tpu_custom_call" | custom-call | tf_op jit(solution)/shard_map/give_out/pallas_call | solution.py:1429
